TPU v7x, 32 devices: a whole 2x2x4 slice. The times are simulated.
32 devices in a mesh: dp: 8 (over z, y), ctx: 4 (over x, core).
Axes of the slice: x: 2, y: 2, z: 4, core: 2. Of those that a mesh axis runs over, the one named last changes fastest.
Arguments:
- hidden_in: bfloat16 [8, 512, 5376], P('dp', 'ctx'), may hold values from -30 to 30
- w_qkv: bfloat16 [5376, 512], P('ctx'), may hold values from -1 to 1
- d_attn: bfloat16 [8, 512, 256], P('dp', 'ctx'), may hold values from -6 to 6
- range_len: int32 [8, 4], P('dp', 'ctx'), may hold values from 96 to 128, as said below
- doc_ids: int32 [8, 512], P('dp', 'ctx'), may hold values from 0 to 1, never falling along the last dimension, each value on 1 to 384 neighbouring positions
Outputs:
- d_x: bfloat16 [8, 512, 5376], P('dp', 'ctx')
- d_w: float32 [5376, 512], P('ctx')
Inputs may be any that keep to these rules, and one draw needn't show every extreme that they name: `range_len`: every range holds between 96 and 128 live tokens; in every sequence one range holds exactly 128 and another exactly 96.
All inputs are finite; a program needn't handle non-finite values.
Results may differ from a plain program's by a relative error of at most 0.015.
Values may be sent and summed in bfloat16 or wider, within the bound.
No kernel may reach another device: no remote copies, remote signals or barrier semaphores. Data moves between devices by JAX's collectives and lax.ppermute only.
A program may use at most 64 MiB of HBM per device.

v0:
```python
import jax
import jax.numpy as jnp
from jax import lax
from jax.sharding import PartitionSpec as P

HD = 128
WINDOW = 1024
QHEADS = 2
REACH = 11


score_scale = 168.0 ** (-0.5)
neg_fill = -1e30


def carried_in(value, axis, join, neutral):
    count, mine = (lax.axis_size(axis), lax.axis_index(axis))
    pieces = lax.all_gather(value, axis)
    subtotal = jnp.full_like(value, 0) + jnp.asarray(neutral, value.dtype)

    def hop(position, subtotal):
        longer = join(subtotal, pieces[position])
        return jnp.where(position < mine, longer, subtotal)

    return lax.fori_loop(0, count - 1, hop, subtotal)


def passed_along(value, axis, steps):
    count = lax.axis_size(axis)
    first, last = (max(0, -steps), min(count, count - steps))
    return lax.ppermute(value, axis, [(source, source + steps) for source in range(first, last)])


def rotary_tables(positions, head_size):
    half = head_size // 2
    freqs = 10000.0 ** (-(jnp.arange(half, dtype=jnp.float32) * 2.0) / head_size)
    angles = positions.astype(jnp.float32)[:, None] * freqs[None, :]
    return (jnp.cos(angles), jnp.sin(angles))


def rotate(values, cosine, sine, sign):
    half = values.shape[-1] // 2
    first = values[..., :half]
    second = values[..., half:]
    return jnp.concatenate(
        [first * cosine - sign * second * sine, second * cosine + sign * first * sine], axis=-1
    )


def allowed_pairs(query_meta, key_meta):
    qpos = query_meta[:, 0][:, None]
    kpos = key_meta[:, 0][None, :]
    same_doc = query_meta[:, 1][:, None] == key_meta[:, 1][None, :]
    both_live = (query_meta[:, 2][:, None] == 1) & (key_meta[:, 2][None, :] == 1)
    return both_live & same_doc & (kpos <= qpos) & (qpos - kpos < WINDOW)


def add_ints(earlier, later):
    return earlier + later


def body(hidden_in, w_qkv, d_attn, range_len, doc_ids):
    tokens = hidden_in[0]
    cap = tokens.shape[0]
    groups = lax.axis_size("ctx")
    own_len = range_len[0, 0]
    start = carried_in(own_len, "ctx", add_ints, jnp.int32(0))
    slot = jnp.arange(cap, dtype=jnp.int32)
    live = slot < own_len
    meta = jnp.stack([start + slot, doc_ids[0], live.astype(jnp.int32)], axis=1)
    cosine, sine = rotary_tables(meta[:, 0], HD)
    nq = QHEADS * HD
    x_cols = lax.all_to_all(tokens, "ctx", split_axis=1, concat_axis=0, tiled=True)
    proj = jnp.dot(
        tokens, lax.all_gather(w_qkv, "ctx", axis=0, tiled=True), preferred_element_type=jnp.float32
    )
    queries = rotate(
        proj[:, :nq].reshape(cap, QHEADS, HD), cosine[:, None, :], sine[:, None, :], 1.0
    ).astype(jnp.bfloat16)
    keys = rotate(proj[:, nq : nq + HD], cosine, sine, 1.0).astype(jnp.bfloat16)
    values = proj[:, nq + HD :].astype(jnp.bfloat16)
    key_pack = jnp.concatenate([keys, values], axis=1)
    grad_out = d_attn[0].reshape(cap, QHEADS, HD)
    top = jnp.full((QHEADS, cap), neg_fill, jnp.float32)
    pack = lax.all_gather(key_pack, "ctx", axis=0, tiled=True)
    key_meta = lax.all_gather(meta, "ctx", axis=0, tiled=True)
    scores = score_scale * jnp.einsum(
        "qhd,kd->hqk", queries, pack[:, :HD], preferred_element_type=jnp.float32
    )
    dots = jnp.einsum("qhd,kd->hqk", grad_out, pack[:, HD:], preferred_element_type=jnp.float32)
    allowed = allowed_pairs(meta, key_meta)[None]
    new_top = jnp.maximum(top, jnp.max(jnp.where(allowed, scores, neg_fill), axis=2))
    expo = jnp.where(allowed, jnp.exp(scores - new_top[:, :, None]), 0.0)
    carry = (new_top, jnp.sum(expo, axis=2), jnp.sum(expo * dots, axis=2))
    top, total, weighted = carry
    live_rows = live[None, :]
    safe_total = jnp.where(live_rows, total, 1.0)
    lse = jnp.where(live_rows, top + jnp.log(safe_total), 0.0)
    delta = jnp.where(live_rows, weighted / safe_total, 0.0)
    pack = lax.all_gather(key_pack, "ctx", axis=0, tiled=True)
    key_meta = lax.all_gather(meta, "ctx", axis=0, tiled=True)
    scores = score_scale * jnp.einsum(
        "qhd,kd->hqk", queries, pack[:, :HD], preferred_element_type=jnp.float32
    )
    dots = jnp.einsum("qhd,kd->hqk", grad_out, pack[:, HD:], preferred_element_type=jnp.float32)
    allowed = allowed_pairs(meta, key_meta)[None]
    probs = jnp.where(allowed, jnp.exp(scores - lse[:, :, None]), 0.0)
    mixed = (probs * (dots - delta[:, :, None])).astype(jnp.bfloat16)
    dq_sum = jnp.einsum("hqk,kd->qhd", mixed, pack[:, :HD], preferred_element_type=jnp.float32)
    dq = score_scale * dq_sum

    def key_step(carry, piece):
        dkey, dval = carry
        query_pack, stats, query_meta = piece
        rows = query_pack.shape[0]
        query_b = query_pack[:, :nq].reshape(rows, QHEADS, HD)
        grad_b = query_pack[:, nq:].reshape(rows, QHEADS, HD)
        scores = score_scale * jnp.einsum(
            "qhd,kd->hqk", query_b, keys, preferred_element_type=jnp.float32
        )
        dots = jnp.einsum("qhd,kd->hqk", grad_b, values, preferred_element_type=jnp.float32)
        allowed = allowed_pairs(query_meta, meta)[None]
        lse_b = stats[:, :QHEADS].T
        delta_b = stats[:, QHEADS:].T
        probs = jnp.where(allowed, jnp.exp(scores - lse_b[:, :, None]), 0.0)
        mixed = (probs * (dots - delta_b[:, :, None])).astype(jnp.bfloat16)
        dval = dval + jnp.einsum(
            "hqk,qhd->kd", probs.astype(jnp.bfloat16), grad_b, preferred_element_type=jnp.float32
        )
        dkey = dkey + jnp.einsum("hqk,qhd->kd", mixed, query_b, preferred_element_type=jnp.float32)
        return (dkey, dval)

    query_pack = jnp.concatenate([queries.reshape(cap, nq), d_attn[0]], axis=1)
    stats = jnp.concatenate([lse.T, delta.T], axis=1)
    init_keys = (jnp.zeros((cap, HD), jnp.float32), jnp.zeros((cap, HD), jnp.float32))
    carry = key_step(init_keys, (query_pack, stats, meta))
    for hop in range(1, min(REACH, groups - 1) + 1):
        later = (
            passed_along(query_pack.astype(jnp.float32), "ctx", -hop).astype(query_pack.dtype),
            passed_along(stats, "ctx", -hop),
            passed_along(meta, "ctx", -hop),
        )
        carry = key_step(carry, later)
    dkey, dval = carry
    dq_pre = rotate(dq, cosine[:, None, :], sine[:, None, :], -1.0).reshape(cap, nq)
    dk_pre = rotate(score_scale * dkey, cosine, sine, -1.0)
    d_proj = jnp.concatenate([dq_pre, dk_pre, dval], axis=1).astype(jnp.bfloat16)
    every = lax.all_gather(d_proj, "ctx", axis=0, tiled=True)
    partial_w = lax.dot_general(
        x_cols, every, (((0,), (0,)), ((), ())), preferred_element_type=jnp.float32
    )
    d_w = lax.psum(partial_w, "dp")
    rows_back = lax.dot_general(
        every, w_qkv, (((1,), (1,)), ((), ())), preferred_element_type=jnp.float32
    ).astype(jnp.bfloat16)
    d_x = lax.all_to_all(rows_back, "ctx", split_axis=0, concat_axis=1, tiled=True)
    return (d_x[None], d_w)


def solution(mesh):
    return jax.shard_map(
        body,
        mesh=mesh,
        in_specs=(
            P("dp", "ctx", None),
            P("ctx", None),
            P("dp", "ctx", None),
            P("dp", "ctx"),
            P("dp", "ctx"),
        ),
        out_specs=(P("dp", "ctx", None), P("ctx", None)),
        check_vma=False,
    )
```

profile of v0, /device:TPU:0, one launch (start us, length us, event | category | flops | bytes accessed | tf_op | source)
XLA Modules:
  0.0 247.6 jit_solution(8831942214447779360)
XLA Ops:
  7.2 0.7 all-gather.3.cloned.1.call-update
  8.6 0.6 dynamic-slice
  9.2 0.7 bitcast_dynamic-update-slice_fusion
  9.9 6.4 %all-reduce = s32[4]{0:T(128)S(1)} all-reduce(s32[4]{0:T(128)S(1)} %bitcast_dynamic-update-slice_fusion), channel_id=2, replica_groups=mesh['dp'=8,'ctx'=4] {'ctx'}, use_global_device_ids=true, to_apply=%add | all-reduce | flops 4 | bytes 32 | tf_op jit(solution)/shard_map/all_gather | solution.py:18
  16.2 4.1 %while.13 = (s32[]{:T(128)}, s32[]{:T(128)}, s32[]{:T(128)}, s32[4]{0:T(128)S(1)}, s32[]{:T(128)}) while((s32[]{:T(128)}, s32[]{:T(128)}, s32[]{:T(128)}, s32[4]{0:T(128)S(1)}, s32[]{:T(128)}) %tuple.63), condition=%wide.region_1.2_spmd, body=%wide.region_0.1_spmd.sunk | while | flops 5 | bytes 107 | solution.py:25
  16.2 0.7 dynamic_slice.8
  17.6 0.7 dynamic_slice.8
  19.0 0.7 dynamic_slice.8
  20.4 1.3 collective-permute-start
  21.7 1.3 collective-permute-start.3
  23.0 1.3 collective-permute-start.6
  24.4 1.5 copy.146
  25.9 4.5 %all-to-all-start.1 = ((bf16[128,4,1344]{0,2,1:T(8,128)(2,1)}), bf16[128,4,1344]{0,2,1:T(8,128)(2,1)S(1)}, u32[]{:S(2)}, u32[]{:S(2)}) async-start(bf16[128,4,1344]{0,2,1:T(8,128)(2,1)} %bitcast.240), calls=%async_computation.1 | async-start | bytes 2752512 | tf_op jit(solution)/shard_map/all_to_all | solution.py:73
  30.4 34.2 %all_gather.20 = s32[512,3]{0,1:T(4,128)S(1)} all-gather(s32[128,3]{0,1:T(4,128)S(1)} %pad_add_fusion), channel_id=1, replica_groups=mesh['dp'=8,'ctx'=4] {'ctx'}, dimensions={0}, use_global_device_ids=true | all-gather | bytes 7680 | tf_op jit(solution)/shard_map/all_gather | solution.py:101
  64.5 0.6 fusion.85
  66.0 0.5 multiply_power_fusion
  66.7 0.8 fusion.56
  67.5 1.1 copy-done.1
  68.6 1.8 copy.147
  70.4 3.4 %fusion.1 = f32[128,512]{1,0:T(8,128)S(1)} fusion(bf16[5376,512]{1,0:T(8,128)(2,1)} %all-gather.3.cloned.1.call-done, bf16[1,128,5376]{2,1,0:T(8,128)(2,1)S(1)} %copy-done), kind=kOutput, calls=%fused_computation.4 | convolution fusion | flops 704643072 | bytes 7143424 | tf_op jit(solution)/shard_map/dot_general | solution.py:74
  74.1 0.9 fusion.61
  75.9 5.8 %all_gather.19 = bf16[512,256]{1,0:T(8,128)(2,1)S(1)} all-gather(bf16[128,256]{1,0:T(8,128)(2,1)S(1)} %pad_maximum_fusion.1), channel_id=1, replica_groups=mesh['dp'=8,'ctx'=4] {'ctx'}, dimensions={0}, use_global_device_ids=true | all-gather | bytes 327680 | tf_op jit(solution)/shard_map/all_gather | solution.py:100
  82.6 0.6 pad_maximum_fusion.3
  83.2 1.3 collective-permute-start.5
  84.5 1.3 collective-permute-start.8
  85.8 0.7 maximum_convert_fusion.1
  86.4 1.3 collective-permute-start.4
  87.7 1.3 collective-permute-start.7
  89.0 1.3 collective-permute-start.2
  90.3 0.9 fusion.28
  91.3 1.6 convolution_bitcast_fusion.13
  92.9 0.8 convolution_bitcast_fusion.9
  93.7 1.0 fusion.4
  95.2 1.3 collective-permute-start.1
  96.5 0.7 slice_bitcast_fusion.7
  97.2 0.8 slice_bitcast_fusion.5
  98.0 0.7 slice_bitcast_fusion.9
  98.7 0.9 fusion.88
  99.6 0.9 fusion.20
  101.1 0.9 fusion.89
  103.7 10.8 %all_gather.21 = bf16[512,512]{0,1:T(8,128)(2,1)S(1)} all-gather(bf16[128,512]{0,1:T(8,128)(2,1)S(1)} %pad_maximum_fusion), channel_id=1, replica_groups=mesh['dp'=8,'ctx'=4] {'ctx'}, dimensions={0}, use_global_device_ids=true | all-gather | bytes 655360 | tf_op jit(solution)/shard_map/all_gather | solution.py:148
  114.5 2.5 convolution_bitcast_fusion
  117.0 1.3 copy-done.2
  118.3 0.9 fusion
  119.4 20.8 %all_to_all.35 = bf16[4,128,1344]{1,2,0:T(8,128)(2,1)S(1)} all-to-all(bf16[4,128,1344]{1,2,0:T(8,128)(2,1)S(1)} %bitcast.241), channel_id=1, replica_groups=mesh['dp'=8,'ctx'=4] {'ctx'}, dimensions={0} | all-to-all | bytes 2752512 | tf_op jit(solution)/shard_map/all_to_all | solution.py:156
  140.2 1.5 copy.148
  141.7 95.5 %all-reduce.3.cloned.1.call-done = f32[1344,512]{1,0:T(8,128)} async-done(((f32[1344,512]{1,0:T(8,128)}), f32[1344,512]{1,0:T(8,128)}) %all-reduce.3.cloned.1.call-update) | async-done | bytes 2752528 | tf_op jit(solution)/shard_map/psum | solution.py:152
  237.2 3.6 %copy.199 = f32[1344,512]{1,0:T(8,128)} copy(f32[1344,512]{1,0:T(8,128)} %all-reduce.3.cloned.1.call-done) | data formatting | bytes 5505024
  (91 shorter events, 5.7 us)
Async XLA Ops:
  7.2 1.4 copy-start.13
  7.2 13.2 %copy-start.9 = (s32[1,128]{1,0:T(1,128)S(1)}, s32[1,128]{1,0:T(1,128)}, u32[]{:S(2)}) copy-start(s32[1,128]{1,0:T(1,128)} %param.11) | copy-start | bytes 1540
  7.2 17.2 %copy-start = (bf16[1,128,5376]{2,1,0:T(8,128)(2,1)S(1)}, bf16[1,128,5376]{2,1,0:T(8,128)(2,1)}, u32[]{:S(2)}) copy-start(bf16[1,128,5376]{2,1,0:T(8,128)(2,1)} %param.7) | copy-start | bytes 4128772
  7.2 63.2 %all-gather.3.cloned.1.call-start = ((), (), s32[]{:S(2)}) async-start(), calls=%async_computation.2 | async-start | bytes 6881280 | tf_op jit(solution)/shard_map/all_gather | solution.py:75
  20.4 46.2 %collective-permute-start = (s32[128,3]{0,1:T(4,128)S(1)}, s32[128,3]{0,1:T(4,128)S(1)}, u32[]{:S(2)}, u32[]{:S(2)}) collective-permute-start(s32[128,3]{0,1:T(4,128)S(1)} %pad_add_fusion), channel_id=1, source_target_pairs={{1,0},{2,1},{3,2},{5,4},{6,5},{7,6},{9,8},{10,9},{11,10},{13,12},{... | collective-permute-start | bytes 4616 | tf_op jit(solution)/shard_map/ppermute | solution.py:31
  21.7 44.9 %collective-permute-start.3 = (s32[128,3]{0,1:T(4,128)S(1)}, s32[128,3]{0,1:T(4,128)S(1)}, u32[]{:S(2)}, u32[]{:S(2)}) collective-permute-start(s32[128,3]{0,1:T(4,128)S(1)} %pad_add_fusion), channel_id=1, source_target_pairs={{2,0},{3,1},{6,4},{7,5},{10,8},{11,9},{14,12},{15,13},{18,16},{19,... | collective-permute-start | bytes 4616 | tf_op jit(solution)/shard_map/ppermute | solution.py:31
  23.0 43.6 %collective-permute-start.6 = (s32[128,3]{0,1:T(4,128)S(1)}, s32[128,3]{0,1:T(4,128)S(1)}, u32[]{:S(2)}, u32[]{:S(2)}) collective-permute-start(s32[128,3]{0,1:T(4,128)S(1)} %pad_add_fusion), channel_id=1, source_target_pairs={{3,0},{7,4},{11,8},{15,12},{19,16},{23,20},{27,24},{31,28}} | collective-permute-start | bytes 4616 | tf_op jit(solution)/shard_map/ppermute | solution.py:31
  25.9 40.6 %copy-start.5 = (bf16[1,128,256]{2,1,0:T(8,128)(2,1)S(1)}, bf16[1,128,256]{2,1,0:T(8,128)(2,1)}, u32[]{:S(2)}) copy-start(bf16[1,128,256]{2,1,0:T(8,128)(2,1)} %param.9) | copy-start | bytes 196612
  25.9 41.6 %all-to-all-start.1 = ((bf16[128,4,1344]{0,2,1:T(8,128)(2,1)}), bf16[128,4,1344]{0,2,1:T(8,128)(2,1)S(1)}, u32[]{:S(2)}, u32[]{:S(2)}) async-start(bf16[128,4,1344]{0,2,1:T(8,128)(2,1)} %bitcast.240), calls=%async_computation.1 | async-start | bytes 2752512 | tf_op jit(solution)/shard_map/all_to_all | solution.py:73
  30.4 206.8 %all-reduce.3.cloned.1.call-start = ((), (), s32[]{:S(2)}) async-start(), calls=%async_computation.3 | async-start | bytes 5505024 | tf_op jit(solution)/shard_map/psum | solution.py:152
  67.5 1.1 copy-start.1
  81.8 0.8 copy-start.12
  82.6 7.8 %copy-start.7 = (f32[2,128]{1,0:T(2,128)}, f32[2,128]{1,0:T(2,128)S(1)}, u32[]{:S(2)}) copy-start(f32[2,128]{1,0:T(2,128)S(1)} %get-tuple-element.135) | copy-start | bytes 3076
  82.6 7.8 %copy-start.8 = (f32[2,128]{1,0:T(2,128)}, f32[2,128]{1,0:T(2,128)S(1)}, u32[]{:S(2)}) copy-start(f32[2,128]{1,0:T(2,128)S(1)} %get-tuple-element.134) | copy-start | bytes 3076
  83.2 12.0 %collective-permute-start.5 = (f32[128,4]{0,1:T(4,128)}, f32[128,4]{0,1:T(4,128)}, u32[]{:S(2)}, u32[]{:S(2)}) collective-permute-start(f32[128,4]{0,1:T(4,128)} %pad_maximum_fusion.3), channel_id=1, source_target_pairs={{2,0},{3,1},{6,4},{7,5},{10,8},{11,9},{14,12},{15,13},{18,16},{19,... | collective-permute-start | bytes 6152 | tf_op jit(solution)/shard_map/ppermute | solution.py:31
  84.5 12.8 %collective-permute-start.8 = (f32[128,4]{0,1:T(4,128)}, f32[128,4]{0,1:T(4,128)}, u32[]{:S(2)}, u32[]{:S(2)}) collective-permute-start(f32[128,4]{0,1:T(4,128)} %pad_maximum_fusion.3), channel_id=1, source_target_pairs={{3,0},{7,4},{11,8},{15,12},{19,16},{23,20},{27,24},{31,28}} | collective-permute-start | bytes 6152 | tf_op jit(solution)/shard_map/ppermute | solution.py:31
  86.4 12.3 %collective-permute-start.4 = (bf16[128,512]{0,1:T(8,128)(2,1)}, bf16[128,512]{0,1:T(8,128)(2,1)}, u32[]{:S(2)}, u32[]{:S(2)}) collective-permute-start(bf16[128,512]{0,1:T(8,128)(2,1)} %maximum_convert_fusion.1), channel_id=1, source_target_pairs={{2,0},{3,1},{6,4},{7,5},{10,8},{11,9},{14,12},{15,13},{18,16},{19,... | collective-permute-start | bytes 393224 | tf_op jit(solution)/shard_map/ppermute | solution.py:31
  87.7 13.3 %collective-permute-start.7 = (bf16[128,512]{0,1:T(8,128)(2,1)}, bf16[128,512]{0,1:T(8,128)(2,1)}, u32[]{:S(2)}, u32[]{:S(2)}) collective-permute-start(bf16[128,512]{0,1:T(8,128)(2,1)} %maximum_convert_fusion.1), channel_id=1, source_target_pairs={{3,0},{7,4},{11,8},{15,12},{19,16},{23,20},{27,24},{31,28}} | collective-permute-start | bytes 393224 | tf_op jit(solution)/shard_map/ppermute | solution.py:31
  89.0 9.0 %collective-permute-start.2 = (f32[128,4]{0,1:T(4,128)}, f32[128,4]{0,1:T(4,128)}, u32[]{:S(2)}, u32[]{:S(2)}) collective-permute-start(f32[128,4]{0,1:T(4,128)} %pad_maximum_fusion.3), channel_id=1, source_target_pairs={{1,0},{2,1},{3,2},{5,4},{6,5},{7,6},{9,8},{10,9},{11,10},{13,12},{... | collective-permute-start | bytes 6152 | tf_op jit(solution)/shard_map/ppermute | solution.py:31
  94.7 7.2 %copy-start.6 = (pred[128,128]{0,1:T(8,128)(4,1)S(1)}, pred[128,128]{0,1:T(8,128)(4,1)}, u32[]{:S(2)}) copy-start(pred[128,128]{0,1:T(8,128)(4,1)} %get-tuple-element.132) | copy-start | bytes 49156
  95.2 7.5 %collective-permute-start.1 = (bf16[128,512]{0,1:T(8,128)(2,1)}, bf16[128,512]{0,1:T(8,128)(2,1)S(1)}, u32[]{:S(2)}, u32[]{:S(2)}) collective-permute-start(bf16[128,512]{0,1:T(8,128)(2,1)} %maximum_convert_fusion.1), channel_id=1, source_target_pairs={{1,0},{2,1},{3,2},{5,4},{6,5},{7,6},{9,8},{10,9},{11,10},{13,12},{... | collective-permute-start | bytes 393224 | tf_op jit(solution)/shard_map/ppermute | solution.py:31
  98.7 4.2 %copy-start.3 = (f32[128,128]{0,1:T(8,128)S(1)}, f32[128,128]{0,1:T(8,128)}, u32[]{:S(2)}) copy-start(f32[128,128]{0,1:T(8,128)} %convolution_bitcast_fusion.13) | copy-start | bytes 196612
  100.7 2.5 %copy-start.10 = (f32[128]{0:T(128)S(1)}, f32[128]{0:T(128)}, u32[]{:S(2)}) copy-start(f32[128]{0:T(128)} %fusion.85) | copy-start | bytes 1540
  100.7 2.5 %copy-start.11 = (f32[64]{0:T(128)S(1)}, f32[64]{0:T(128)}, u32[]{:S(2)}) copy-start(f32[64]{0:T(128)} %multiply_power_fusion) | copy-start | bytes 772
  100.7 2.7 %copy-start.4 = (f32[128,128]{0,1:T(8,128)S(1)}, f32[128,128]{0,1:T(8,128)}, u32[]{:S(2)}) copy-start(f32[128,128]{0,1:T(8,128)} %convolution_bitcast_fusion.9) | copy-start | bytes 196612
  117.0 1.3 copy-start.2
Sparse Core Ops, SparseCore 0:
  9.6 59.4 all-gather.2
  117.1 120.0 all-reduce.2
where the time goes:
time: 249 us; the launch traced here: 248 us
  waiting for transfers between devices  96.2 us (39%)
  blocking collectives  78 us (31%)
  local copies, waits for them, and re-layouts  19.8 us (8%)
  starting transfers between devices  16.1 us (6%)
  between operations  15.3 us (6%)
  matrix products  14.4 us (6%)
  other arithmetic  5.61 us (2%)
    psum x1, waiting for transfers between devices, body(): d_w = lax.psum(partial_w, 'dp')  95.5 us
    all_gather x1, blocking collectives, body(): key_meta = lax.all_gather(meta, 'ctx', axis=0, tiled=True)  34.2 us
    all_to_all x1, blocking collectives, body(): lax.all_to_all(rows_back, 'ctx', split_axis=0, concat_axis=1, tiled=True)  20.8 us
    ppermute x9, starting transfers between devices, passed_along(): lax.ppermute(value, axis, [(source, source + steps) for source in range(f...  11.6 us
    all_gather x1, blocking collectives, body(): every = lax.all_gather(d_proj, 'ctx', axis=0, tiled=True)  10.8 us
    unnamed x36, local copies, waits for them, and re-layouts  10.5 us
    all_gather x1, blocking collectives, carried_in(): pieces = lax.all_gather(value, axis)  6.39 us
    all_gather x1, blocking collectives, body(): pack = lax.all_gather(key_pack, 'ctx', axis=0, tiled=True)  5.82 us
  transfers between devices with their start and end apart: 12, of which 1 were waited for; matrix products, arithmetic and copies ran while one was open for 10% of the time, Pallas kernels for 0%

commit v1 on v0

v1 whole, which is shorter than its diff:
```python
import functools

import jax
import jax.numpy as jnp
from jax import lax
from jax.experimental import pallas as pl
from jax.experimental.pallas import tpu as pltpu
from jax.sharding import PartitionSpec as P

HD = 128
WINDOW = 1024
QHEADS = 2
NQ = QHEADS * HD
LANES = 128
QUAD = 4
SPLITS = 2
EXTRA = 16
SUM_COST = 8_000_000_000
DOC_STEP = 1 << 20
VMEM_BYTES = 48 * 1024 * 1024

score_scale = 168.0 ** (-0.5)
neg_fill = -1e30
f32 = jnp.float32
bf16 = jnp.bfloat16


def swap(value, axis, mask):
    count = lax.axis_size(axis)
    return lax.ppermute(value, axis, [(i, i ^ mask) for i in range(count)])


def after(value, *others):
    return lax.optimization_barrier((value, others))[0]


def rotate(values, cosine, sine):
    return values * cosine + pltpu.roll(values, HD // 2, 1) * sine


def call(kernel, out_shape, scratch=(), flops=0, moved=0, **more):
    return pl.pallas_call(
        kernel,
        out_shape=out_shape,
        scratch_shapes=list(scratch),
        compiler_params=pltpu.CompilerParams(vmem_limit_bytes=VMEM_BYTES),
        cost_estimate=pl.CostEstimate(flops=flops, bytes_accessed=moved, transcendentals=0),
        **more,
    )


def shape(dims, dtype):
    return jax.ShapeDtypeStruct(dims, dtype)


class Sizes:
    def __init__(self, tokens, w_qkv):
        self.n = lax.axis_size("ctx")
        self.cap, self.width = tokens.shape
        self.rows, self.qkv = w_qkv.shape
        self.slots = self.n * self.cap
        tiles = self.width // LANES
        need = 1
        for c in range(self.n):
            low, high = (c * self.rows, (c + 1) * self.rows)
            need = max(need, -(-high // LANES) - low // LANES)
        self.win = need * LANES
        self.last = tiles - need
        self.chunk = -(-self.rows // (QUAD * 16)) * 16

    def first(self, c):
        return pl.multiple_of(jnp.minimum(c * self.rows // LANES, self.last) * LANES, LANES)

    def inset(self, c):
        return pl.multiple_of(c * self.rows - self.first(c), 16)

    def block(self, k):
        return pl.ds(pl.multiple_of((lax.axis_index("ctx") ^ k) * self.cap, self.cap), self.cap)

    def own_window(self, x_ref):
        return x_ref[:, pl.ds(self.first(lax.axis_index("ctx")), self.win)]


def windows_kernel(z, x_ref, *refs):
    outs, sems = (refs[: z.n - 1], refs[z.n - 1])
    me = lax.axis_index("ctx")
    copies = [
        pltpu.make_async_copy(x_ref.at[:, pl.ds(z.first(me ^ k), z.win)], outs[k - 1], sems.at[k - 1])
        for k in range(1, z.n)
    ]
    for copy in copies:
        copy.start()
    for copy in copies:
        copy.wait()


def pad_kernel(z, w_ref, pad):
    pad[...] = jnp.zeros_like(pad)
    pad[pl.ds(z.inset(lax.axis_index("ctx")), z.rows), :] = w_ref[...]


def spread_kernel(z, order, packs, grads, qrow, kcol, poscol):
    me = lax.axis_index("ctx")
    rows = lax.broadcasted_iota(jnp.int32, (z.n, z.cap), 0)
    docs = jnp.zeros((z.n, z.cap), f32)
    lens = jnp.zeros((z.n, z.cap), f32)
    tall = z.cap + EXTRA
    for place, k in enumerate(order):
        at = place * tall
        grads[z.block(k), :] = packs[at : at + z.cap, :]
        extra = packs[at + z.cap : at + tall, :].astype(f32)[:1]
        docs = jnp.where(rows == (me ^ k), extra[:, : z.cap], docs)
        lens = jnp.where(rows == (me ^ k), extra[:, z.cap : 2 * z.cap], lens)
    docs = docs.astype(jnp.int32)
    lens = lens.astype(jnp.int32)
    offset = lax.broadcasted_iota(jnp.int32, (z.n, z.cap), 1)
    start = jnp.zeros((1, z.cap), jnp.int32)
    for c in range(z.n):
        pos = start + offset[c : c + 1]
        live = offset[c : c + 1] < lens[c : c + 1]
        mark = docs[c : c + 1] * DOC_STEP + pos
        qrow[c : c + 1, :] = jnp.where(live, mark, -DOC_STEP)
        at = slice(c * z.cap, (c + 1) * z.cap)
        key = jnp.where(live, mark, 4 * DOC_STEP).astype(f32)
        kcol[at, :] = jnp.broadcast_to(key, (LANES, z.cap)).T.astype(jnp.int32)
        poscol[at, :] = jnp.broadcast_to(pos.astype(f32), (LANES, z.cap)).T
        start = start + lens[c : c + 1]


def near_kernel(z, x_ref, x1_ref, w_ref, keep, send):
    keep[...] = jnp.dot(z.own_window(x_ref), w_ref[...], preferred_element_type=f32)
    send[...] = jnp.dot(x1_ref[...], w_ref[...], preferred_element_type=f32).astype(bf16)


def far_kernel(z, *refs):
    xs, (w_ref, _, keep, send) = (refs[: z.n - 2], refs[z.n - 2 :])
    for k in range(0, z.n - 2, 2):
        at = slice(k // 2 * z.cap, (k // 2 + 1) * z.cap)
        send[at, :] = jnp.dot(xs[k + 1][...], w_ref[...], preferred_element_type=f32).astype(bf16)
        keep[at, :] = jnp.dot(xs[k][...], w_ref[...], preferred_element_type=f32)


def transpose_kernel(z, x_ref, *refs):
    xs, out = (refs[: z.n - 1], refs[z.n - 1])
    out[:, z.block(0)] = z.own_window(x_ref).T
    for k in range(1, z.n):
        out[:, z.block(k)] = xs[k - 1][...].T


def rotary_kernel(z, *refs):
    count = z.n // 2
    kept, came, (cos_ref, sin_ref, out) = (refs[:count], refs[count : 2 * count], refs[2 * count :])
    for i in range(count):
        proj = kept[i][...].astype(f32) + came[i][...].astype(f32)
        rows = z.block(2 * i)
        at = slice(i * z.cap, (i + 1) * z.cap)
        cosine, sine = (cos_ref[rows, :], sin_ref[rows, :])
        for h in range(QHEADS + 1):
            cols = slice(h * HD, (h + 1) * HD)
            out[at, cols] = rotate(proj[:, cols], cosine, sine).astype(bf16)
        out[at, NQ + HD :] = proj[:, NQ + HD :].astype(bf16)


def attention_kernel(z, own, other, g_ref, qrow, kcol, cos_ref, sin_ref, out, qkv, dk, dv):
    block = z.cap
    for k in range(z.n):
        source = other if k & 1 else own
        qkv[z.block(k), :] = source[k // 2 * block : (k // 2 + 1) * block, :]
    kt = qkv[:, NQ : NQ + HD].astype(f32).T.astype(bf16)
    for i in range(z.n):
        rows = slice(i * block, (i + 1) * block)
        extent = (i + 1) * block
        q2 = jnp.concatenate([qkv[rows, h * HD : (h + 1) * HD] for h in range(QHEADS)], axis=0)
        g2 = jnp.concatenate([g_ref[rows, h * HD : (h + 1) * HD] for h in range(QHEADS)], axis=0)
        keys = qkv[:extent, NQ : NQ + HD]
        values = qkv[:extent, NQ + HD :]
        nt = (((1,), (1,)), ((), ()))
        scores = lax.dot_general(keys, q2, nt, preferred_element_type=f32)
        dots = lax.dot_general(values, g2, nt, preferred_element_type=f32)
        query = qrow[i : i + 1, :]
        behind = query - kcol[:extent, :]
        allowed = (behind >= 0) & (behind < WINDOW)
        allowed = jnp.concatenate([allowed] * QHEADS, axis=1)
        query = jnp.concatenate([query] * QHEADS, axis=1)
        scores = jnp.where(allowed, scores, neg_fill)
        top = jnp.max(scores, axis=0, keepdims=True)
        expo = jnp.exp((scores - top) * score_scale)
        total = jnp.sum(expo, axis=0, keepdims=True)
        weighted = jnp.sum(expo * dots, axis=0, keepdims=True)
        inverse = jnp.where(query >= 0, 1.0 / total, 0.0)
        delta = weighted * inverse
        probs = expo * inverse
        mixed = (probs * (dots - delta)).astype(bf16)
        probs = probs.astype(bf16)
        dkey = jnp.dot(mixed, q2, preferred_element_type=f32)
        dval = jnp.dot(probs, g2, preferred_element_type=f32)
        before = i * block
        if before:
            dk[:before, :] += dkey[:before]
            dv[:before, :] += dval[:before]
        dk[before:extent, :] = dkey[before:]
        dv[before:extent, :] = dval[before:]
        dq = score_scale * jnp.dot(kt[:, :extent], mixed, preferred_element_type=f32)
        for h in range(QHEADS):
            dq_h = dq[:, h * block : (h + 1) * block].T
            out[rows, h * HD : (h + 1) * HD] = rotate(dq_h, cos_ref[rows, :], -sin_ref[rows, :]).astype(bf16)
    out[:, NQ : NQ + HD] = rotate(score_scale * dk[...], cos_ref[...], -sin_ref[...]).astype(bf16)
    out[:, NQ + HD :] = dv[...].astype(bf16)


def weight_kernel(z, xt, g_ref, *refs):
    pieces, whole = (refs[:-1], refs[-1])
    if whole.shape[0] > z.win:
        whole[z.win :, :] = jnp.zeros_like(whole[z.win :, :])
    inset = z.inset(lax.axis_index("ctx"))
    mine = lax.axis_index("dp") & (QUAD - 1)
    wide = z.qkv // SPLITS
    for s in range(SPLITS):
        cols = slice(s * wide, (s + 1) * wide)
        whole[: z.win, :] = jnp.dot(xt[...], g_ref[:, cols], preferred_element_type=f32)
        for k in range(QUAD):
            at = pl.multiple_of(inset + (mine ^ k) * z.chunk, 16)
            pieces[s * QUAD + k][...] = whole[pl.ds(at, z.chunk), :].astype(bf16)


def sum_kernel(*refs):
    refs[-1][...] = functools.reduce(lambda a, b: a + b, [r[...].astype(f32) for r in refs[:-1]]).astype(bf16)


def total_of(*pieces):
    return call(sum_kernel, shape(pieces[0].shape, bf16), flops=SUM_COST)(*pieces)


def inputs_kernel(z, g_ref, w_ref, near, far):
    for k in range(z.n):
        target = near if k < z.n // 2 else far
        at = k % (z.n // 2) * z.cap
        target[at : at + z.cap, :] = lax.dot_general(
            g_ref[z.block(k), :], w_ref[...], (((1,), (1,)), ((), ())), preferred_element_type=f32
        ).astype(bf16)


def place_weight_kernel(z, exact, first, *refs):
    pieces, out, whole = (refs[:QUAD], refs[-2], refs[-1])
    mine = lax.axis_index("dp") & (QUAD - 1)
    target = out if exact else whole
    for k in range(QUAD):
        at = pl.multiple_of((mine ^ k) * z.chunk, 16)
        target[pl.ds(at, z.chunk), :] = pieces[k][...].astype(f32)
    if not exact:
        out[...] = whole[: z.rows, :]


def place_weights(z, split, pieces, before):
    wide = z.qkv // SPLITS
    exact = QUAD * z.chunk == z.rows
    whole = lambda: pl.BlockSpec(memory_space=pltpu.VMEM)
    specs = [whole() for _ in pieces]
    more = {}
    if before is not None:
        specs.append(pl.BlockSpec(memory_space=pl.ANY))
        more["input_output_aliases"] = {QUAD: 0}
        pieces = [*pieces, before]
    return call(
        functools.partial(place_weight_kernel, z, exact, before is None),
        shape((z.rows, z.qkv), f32),
        [pltpu.VMEM((16, LANES) if exact else (QUAD * z.chunk, wide), f32)],
        flops=SUM_COST,
        grid=(1,),
        in_specs=specs,
        out_specs=pl.BlockSpec((z.rows, wide), lambda i: (0, split)),
        **more,
    )(*pieces)


def place_inputs_kernel(z, items, *refs):
    arrays, out = (refs[:-1], refs[-1])
    me = lax.axis_index("ctx")
    out[...] = jnp.zeros_like(out)
    for which, at, source in items:
        cols = pl.ds(z.first(me ^ source), z.win)
        out[:, cols] = out[:, cols] + arrays[which][at : at + z.cap, :]


def gather_packs(pack, n, first):
    order, mask = ([0], n // 2)
    came = first
    while mask:
        pack = jnp.concatenate([pack, came], axis=0)
        order = order + [k ^ mask for k in order]
        mask //= 2
        if mask:
            came = swap(pack, "ctx", mask)
    return pack, order


def exchange_inputs(z, near, far):
    arrays = [near]
    held = {(k, 0): (0, k * z.cap) for k in range(z.n // 2)}
    mask, sent = (z.n // 2, [(k, 0) for k in range(z.n // 2, z.n)])
    parcel = far
    while True:
        arrays.append(swap(parcel, "ctx", mask))
        for i, (k, j) in enumerate(sent):
            held[k ^ mask, j ^ mask] = (len(arrays) - 1, i * z.cap)
        mask //= 2
        if not mask:
            break
        sent = sorted(item for item in held if item[0] & mask)
        spots = [held.pop(item) for item in sent]
        parcel = jnp.concatenate([arrays[which][at : at + z.cap] for which, at in spots], axis=0)
    return arrays, [(which, at, j) for (k, j), (which, at) in sorted(held.items())]


def body(hidden_in, w_qkv, d_attn, range_len, doc_ids):
    tokens = hidden_in[0]
    z = Sizes(tokens, w_qkv)
    n, cap, slots, qkv, win = (z.n, z.cap, z.slots, z.qkv, z.win)
    any_spec = pl.BlockSpec(memory_space=pl.ANY)
    vmem_spec = pl.BlockSpec(memory_space=pltpu.VMEM)
    hbm_spec = pl.BlockSpec(memory_space=pltpu.HBM)

    extra = jnp.concatenate([doc_ids[0], jnp.broadcast_to(range_len[0, 0], (cap,))]).astype(bf16)
    pack = jnp.concatenate([d_attn[0], jnp.broadcast_to(extra[None], (EXTRA, NQ))], axis=0)
    cut = call(
        functools.partial(windows_kernel, z),
        [shape((cap, win), bf16)] * (n - 1),
        [pltpu.SemaphoreType.DMA((n - 1,))],
        moved=6 * cap * win,
        in_specs=[hbm_spec],
        out_specs=[any_spec] * (n - 1),
    )(tokens)
    xs = [swap(cut[k - 1], "ctx", k) for k in range(1, n)]
    pack_came = swap(pack, "ctx", n // 2)
    w_pad = call(functools.partial(pad_kernel, z), shape((win, qkv), bf16), moved=4 * win * qkv)(w_qkv)
    keep0, send0 = call(
        functools.partial(near_kernel, z),
        [shape((cap, qkv), f32), shape((cap, qkv), bf16)],
        flops=4 * cap * win * qkv,
        moved=4 * win * (cap + qkv),
    )(tokens, xs[0], w_pad)
    sum0 = keep0 + swap(send0, "ctx", 1).astype(f32)
    far_rows = (n // 2 - 1) * cap
    half0 = sum0.astype(bf16)
    cross0 = swap(half0, "ctx", 2)
    packs, order = gather_packs(pack, n, after(pack_came, sum0))
    grads, qrow, kcol, poscol = call(
        functools.partial(spread_kernel, z, order),
        [
            shape((slots, NQ), bf16),
            shape((n, cap), jnp.int32),
            shape((slots, LANES), jnp.int32),
            shape((slots, HD), f32),
        ],
        moved=8 * slots * NQ,
    )(packs)
    lane = jnp.arange(HD, dtype=jnp.int32)
    freqs = 10000.0 ** (-((lane % (HD // 2)).astype(f32) * 2.0) / HD)
    angles = poscol * freqs[None, :]
    cosine = jnp.cos(angles)
    sine = jnp.where(lane < HD // 2, -1.0, 1.0)[None, :] * jnp.sin(angles)

    keep1, send1 = call(
        functools.partial(far_kernel, z),
        [shape((far_rows, qkv), f32), shape((far_rows, qkv), bf16)],
        flops=4 * far_rows * win * qkv,
        moved=4 * win * (2 * far_rows + qkv),
        in_specs=[vmem_spec] * (n - 1) + [any_spec],
    )(*xs[1:], w_pad, half0)
    sum1 = keep1 + swap(send1, "ctx", 1).astype(f32)
    cross1 = swap(sum1.astype(bf16), "ctx", 2)
    kept = [sum0] + [sum1[i * cap : (i + 1) * cap] for i in range(n // 2 - 1)]
    came = [cross0] + [cross1[i * cap : (i + 1) * cap] for i in range(n // 2 - 1)]
    came = [came[i ^ 1] for i in range(n // 2)]
    mask = 4
    while mask < n:
        both = jnp.concatenate([a + b.astype(f32) for a, b in zip(kept, came)], axis=0)
        crossed = swap(both.astype(bf16), "ctx", mask)
        kept = [both[i * cap : (i + 1) * cap] for i in range(n // 2)]
        came = [crossed[i * cap : (i + 1) * cap] for i in range(n // 2)]
        came = [came[i ^ (mask // 2)] for i in range(n // 2)]
        mask *= 2
    xt = call(functools.partial(transpose_kernel, z), shape((win, slots), bf16), moved=4 * win * slots)(tokens, *xs)
    mine = call(functools.partial(rotary_kernel, z), shape((slots // 2, qkv), bf16), moved=4 * slots * qkv)(
        *kept, *came, cosine, sine
    )
    theirs = swap(mine, "ctx", 1)
    d_proj = call(
        functools.partial(attention_kernel, z),
        shape((slots, qkv), bf16),
        [pltpu.VMEM((slots, qkv), bf16), pltpu.VMEM((slots, HD), f32), pltpu.VMEM((slots, HD), f32)],
        flops=20 * slots * slots * HD,
        moved=8 * slots * qkv,
    )(mine, theirs, grads, qrow, kcol, cosine, sine)

    wide = qkv // SPLITS
    deep = max(win, win - z.rows + QUAD * z.chunk)
    parts = call(
        functools.partial(weight_kernel, z),
        [shape((z.chunk, wide), bf16)] * (QUAD * SPLITS),
        [pltpu.VMEM((deep, wide), f32)],
        flops=2 * win * slots * qkv,
        moved=4 * win * slots,
    )(xt, d_proj)
    sums = []
    for s in range(SPLITS):
        own = parts[s * QUAD : (s + 1) * QUAD]
        pieces = [own[0]] + [swap(own[k], "dp", k) for k in range(1, QUAD)]
        sums.append(total_of(*pieces))
    near, far = call(
        functools.partial(inputs_kernel, z),
        [shape((slots // 2, win), bf16)] * 2,
        flops=2 * win * slots * qkv,
        moved=4 * win * slots,
    )(d_proj, w_pad)
    totals = []
    for s in range(SPLITS):
        part, mask = (sums[s], QUAD)
        while mask < lax.axis_size("dp"):
            part = total_of(part, swap(part, "dp", mask))
            mask *= 2
        totals.append(part)
    arrays, items = exchange_inputs(z, near, far)
    d_w = None
    for s in range(SPLITS):
        d_w = place_weights(z, s, [totals[s]] + [swap(totals[s], "dp", k) for k in range(1, QUAD)], d_w)
    d_x = call(
        functools.partial(place_inputs_kernel, z, items), shape((cap, z.width), bf16), moved=4 * cap * z.width
    )(*arrays)
    return (d_x[None], d_w)


def solution(mesh):
    return jax.shard_map(
        body,
        mesh=mesh,
        in_specs=(
            P("dp", "ctx", None),
            P("ctx", None),
            P("dp", "ctx", None),
            P("dp", "ctx"),
            P("dp", "ctx"),
        ),
        out_specs=(P("dp", "ctx", None), P("ctx", None)),
        check_vma=False,
    )
```

time: 249 us -> 83.6 us (0.34)
  blocking collectives: 78 us -> 0 us
  waiting for transfers between devices: 96.2 us -> 37.8 us
  local copies, waits for them, and re-layouts: 19.8 us -> 1.42 us
  matrix products: 14.4 us -> 0 us
  starting transfers between devices: 16.1 us -> 30 us
  between operations: 15.3 us -> 1.54 us
  Pallas kernels: 0 us -> 11.5 us
  other arithmetic: 5.61 us -> 1.12 us
    psum x1 -> x0, waiting for transfers between devices: 95.5 us -> none  [body(): d_w = lax.psum(partial_w, 'dp')]
    all_gather x4 -> x0, blocking collectives: 57.2 us -> none  [the longest x1 34.2 us: body(): key_meta = lax.all_gather(meta, 'ctx', axis=0, tiled=True)]
    ppermute x9 -> x26, waiting for transfers between devices: 0.02 us -> 37.8 us  [swap(): return lax.ppermute(value, axis, [(i, i ^ mask) for i in range(count)])]
    all_to_all x1 -> x0, blocking collectives: 20.8 us -> none  [body(): lax.all_to_all(rows_back, 'ctx', split_axis=0, concat_axis=1, tiled=True)]
    ppermute x9 -> x26, starting transfers between devices: 11.6 us -> 30 us  [swap(): return lax.ppermute(value, axis, [(i, i ^ mask) for i in range(count)])]
    dot_general x18 -> x0, matrix products: 14.4 us -> none  [the longest x1 3.44 us: body(): jnp.dot(tokens, lax.all_gather(w_qkv, 'ctx', axis=0, tiled=True), preferr...]
    pallas_call x0 -> x17, Pallas kernels: none -> 11.5 us  [the longest x2 2.35 us: place_weights(): call(functools.partial(place_weight_kernel, z, exact, before is None), sh...]
    unnamed x36 -> x10, local copies, waits for them, and re-layouts: 10.5 us -> 1.36 us
  transfers between devices with their start and end apart: 12 -> 26, of which waited for: 1 -> 15; matrix products, arithmetic and copies ran while one was open for 10% -> 1% of each run, Pallas kernels for 0% -> 8%
where the time goes in v1:
time: 83.6 us; the launch traced here: 83.5 us
  waiting for transfers between devices  37.8 us (45%)
  starting transfers between devices  30 us (36%)
  Pallas kernels  11.5 us (14%)
  between operations  1.54 us (2%)
  local copies, waits for them, and re-layouts  1.42 us (2%)
  other arithmetic  1.12 us (1%)
    ppermute x26, waiting for transfers between devices, swap(): return lax.ppermute(value, axis, [(i, i ^ mask) for i in range(count)])  37.8 us
    ppermute x26, starting transfers between devices, swap(): return lax.ppermute(value, axis, [(i, i ^ mask) for i in range(count)])  30 us
    pallas_call x2, Pallas kernels, place_weights(): call(functools.partial(place_weight_kernel, z, exact, before is None), sh...  2.35 us
    pallas_call x1, Pallas kernels, body(): call(functools.partial(attention_kernel, z), shape((slots, qkv), bf16), [...  2.21 us
    pallas_call x1, Pallas kernels, body(): call(functools.partial(inputs_kernel, z), [shape((slots // 2, win), bf16)...  1.93 us
  transfers between devices with their start and end apart: 26, of which 15 were waited for; matrix products, arithmetic and copies ran while one was open for 1% of the time, Pallas kernels for 8%

profile of v1, /device:TPU:0, one launch (start us, length us, event | category | flops | bytes accessed | tf_op | source)
XLA Modules:
  0.0 83.5 jit_solution(17599570122389691077)
XLA Ops:
  0.6 1.3 %copy-done = bf16[1,128,5376]{2,1,0:T(8,128)(2,1)S(1)} copy-done((bf16[1,128,5376]{2,1,0:T(8,128)(2,1)S(1)}, bf16[1,128,5376]{2,1,0:T(8,128)(2,1)}, u32[]{:S(2)}) %copy-start) | copy-done | bytes 1376280
  2.1 0.5 collective-permute-start
  2.6 2.6 %collective-permute-start.2 = (bf16[128,1408]{1,0:T(8,128)(2,1)S(1)}, bf16[128,1408]{1,0:T(8,128)(2,1)S(1)}, u32[]{:S(2)}, u32[]{:S(2)}) collective-permute-start(bf16[128,1408]{1,0:T(8,128)(2,1)S(1)} %get-tuple-element.27), channel_id=1, source_target_pairs={{0,2},{1,3},{2,0},{3,1},{4,6},{5,7},{6,4},{7,5},{8,10},{9,11},{10,... | collective-permute-start | bytes 1081352 | tf_op jit(solution)/shard_map/ppermute | solution.py:30
  5.3 0.2 shard_map.69.w_ref.refs_2_
  5.5 0.6 shard_map.70
  6.1 0.2 collective-permute-start.1
  7.0 2.0 %collective-permute-start.7 = (bf16[144,256]{1,0:T(8,128)(2,1)S(1)}, bf16[144,256]{1,0:T(8,128)(2,1)S(1)}, u32[]{:S(2)}, u32[]{:S(2)}) collective-permute-start(bf16[144,256]{1,0:T(8,128)(2,1)S(1)} %pad_maximum_fusion.3), channel_id=1, source_target_pairs={{0,2},{1,3},{2,0},{3,1},{4,6},{5,7},{6,4},{7,5},{8,10},{9,11},{10,... | collective-permute-start | bytes 221192 | tf_op jit(solution)/shard_map/ppermute | solution.py:30
  9.1 5.4 %collective-permute-done.2.refs_0_.refs_1_ = bf16[128,1408]{1,0:T(8,128)(2,1)S(1)} collective-permute-done((bf16[128,1408]{1,0:T(8,128)(2,1)S(1)}, bf16[128,1408]{1,0:T(8,128)(2,1)S(1)}, u32[]{:S(2)}, u32[]{:S(2)}) %collective-permute-start.2) | collective-permute-done | bytes 360480 | tf_op jit(solution)/shard_map/ppermute | solution.py:30
  14.5 7.2 %collective-permute-done.3.refs_1_.refs_2_ = bf16[128,1408]{1,0:T(8,128)(2,1)S(1)} collective-permute-done((bf16[128,1408]{1,0:T(8,128)(2,1)S(1)}, bf16[128,1408]{1,0:T(8,128)(2,1)S(1)}, u32[]{:S(2)}, u32[]{:S(2)}) %collective-permute-start.3) | collective-permute-done | bytes 360480 | tf_op jit(solution)/shard_map/ppermute | solution.py:30
  21.7 0.6 shard_map.71
  22.2 0.4 collective-permute-start.4
  22.7 1.9 %collective-permute-start.6 = (bf16[128,512]{1,0:T(8,128)(2,1)S(1)}, bf16[128,512]{1,0:T(8,128)(2,1)S(1)}, u32[]{:S(2)}, u32[]{:S(2)}) collective-permute-start(bf16[128,512]{1,0:T(8,128)(2,1)S(1)} %get-tuple-element.48.refs_3_), channel_id=1, source_target_pairs={{0,2},{1,3},{2,0},{3,1},{4,6},{5,7},{6,4},{7,5},{8,10},{9,11},{10,... | collective-permute-start | bytes 393224 | tf_op jit(solution)/shard_map/ppermute | solution.py:30
  24.8 0.9 %collective-permute-start.5 = (bf16[128,512]{1,0:T(8,128)(2,1)S(1)}, bf16[128,512]{1,0:T(8,128)(2,1)S(1)}, u32[]{:S(2)}, u32[]{:S(2)}) collective-permute-start(bf16[128,512]{1,0:T(8,128)(2,1)S(1)} %get-tuple-element.46), channel_id=1, source_target_pairs={{0,2},{1,3},{2,0},{3,1},{4,6},{5,7},{6,4},{7,5},{8,10},{9,11},{10,... | collective-permute-start | bytes 393224 | tf_op jit(solution)/shard_map/ppermute | solution.py:30
  25.7 0.4 collective-permute-done.8
  26.1 0.2 shard_map.72
  26.3 0.9 %sine_multiply_fusion = (f32[512,128]{1,0:T(8,128)S(1)}, f32[512,128]{1,0:T(8,128)S(1)}) fusion(f32[512,128]{1,0:T(8,128)S(1)} %get-tuple-element.32, f32[128]{0:T(128)S(1)} %get-tuple-element.52, f32[128]{0:T(128)S(1)} %get-tuple-element.53), kind=kLoop, calls=%fused_computation.2 | loop fusion | flops 131072 | bytes 787456 | tf_op jit(solution)/shard_map/mul | solution.py:361
  27.2 1.5 %collective-permute-done.6.refs_3_ = bf16[128,512]{1,0:T(8,128)(2,1)S(1)} collective-permute-done((bf16[128,512]{1,0:T(8,128)(2,1)S(1)}, bf16[128,512]{1,0:T(8,128)(2,1)S(1)}, u32[]{:S(2)}, u32[]{:S(2)}) %collective-permute-start.6) | collective-permute-done | bytes 131104 | tf_op jit(solution)/shard_map/ppermute | solution.py:30
  28.7 2.4 %collective-permute-done.5.refs_2_ = bf16[128,512]{1,0:T(8,128)(2,1)S(1)} collective-permute-done((bf16[128,512]{1,0:T(8,128)(2,1)S(1)}, bf16[128,512]{1,0:T(8,128)(2,1)S(1)}, u32[]{:S(2)}, u32[]{:S(2)}) %collective-permute-start.5) | collective-permute-done | bytes 131104 | tf_op jit(solution)/shard_map/ppermute | solution.py:30
  31.2 0.2 shard_map.73.own
  31.4 0.4 shard_map.77.xt
  31.9 1.1 %collective-permute-done.9.other = bf16[256,512]{1,0:T(8,128)(2,1)S(1)} collective-permute-done((bf16[256,512]{1,0:T(8,128)(2,1)S(1)}, bf16[256,512]{1,0:T(8,128)(2,1)S(1)}, u32[]{:S(2)}, u32[]{:S(2)}) %collective-permute-start.9) | collective-permute-done | bytes 262176 | tf_op jit(solution)/shard_map/ppermute | solution.py:30
  32.9 2.2 %shard_map.74.g_ref = bf16[512,512]{1,0:T(8,128)(2,1)S(1)} custom-call(bf16[256,512]{1,0:T(8,128)(2,1)S(1)} %shard_map.73.own, bf16[256,512]{1,0:T(8,128)(2,1)S(1)} %collective-permute-done.9.other, bf16[512,256]{1,0:T(8,128)(2,1)S(1)} %get-tuple-element.33.g_ref, s32[4,128]{1,0:T(4,128)S(1)} %get-tuple-element.34.qrow, ...), custom_call_target="tpu_custom_call" | custom-call | flops 671088640 | bytes 2097152 | tf_op jit(solution)/shard_map/pallas_call | solution.py:388
  35.2 1.1 %shard_map.78 = (bf16[336,256]{1,0:T(8,128)(2,1)S(1)}, bf16[336,256]{1,0:T(8,128)(2,1)S(1)}, bf16[336,256]{1,0:T(8,128)(2,1)S(1)}, bf16[336,256]{1,0:T(8,128)(2,...) custom-call(bf16[1408,512]{1,0:T(8,128)(2,1)S(1)} %shard_map.77.xt, ...), custom_call_target="tpu_custom_call" | custom-call | flops 738197504 | bytes 2883584 | tf_op jit(solution)/shard_map/pallas_call | solution.py:398
  36.3 1.8 %collective-permute-start.19 = (bf16[336,256]{1,0:T(8,128)(2,1)S(1)}, bf16[336,256]{1,0:T(8,128)(2,1)S(1)}, u32[]{:S(2)}, u32[]{:S(2)}) collective-permute-start(bf16[336,256]{1,0:T(8,128)(2,1)S(1)} %get-tuple-element.43), channel_id=1, source_target_pairs={{0,4},{4,0},{8,12},{12,8},{16,20},{20,16},{24,28},{28,24},{1,5},{5... | collective-permute-start | bytes 516104 | tf_op jit(solution)/shard_map/ppermute | solution.py:30
  38.1 1.6 %collective-permute-start.20 = (bf16[336,256]{1,0:T(8,128)(2,1)S(1)}, bf16[336,256]{1,0:T(8,128)(2,1)S(1)}, u32[]{:S(2)}, u32[]{:S(2)}) collective-permute-start(bf16[336,256]{1,0:T(8,128)(2,1)S(1)} %get-tuple-element.44), channel_id=1, source_target_pairs={{0,8},{4,12},{8,0},{12,4},{16,24},{20,28},{24,16},{28,20},{1,9},{5... | collective-permute-start | bytes 516104 | tf_op jit(solution)/shard_map/ppermute | solution.py:30
  39.9 1.8 %collective-permute-start.12 = (bf16[336,256]{1,0:T(8,128)(2,1)S(1)}, bf16[336,256]{1,0:T(8,128)(2,1)S(1)}, u32[]{:S(2)}, u32[]{:S(2)}) collective-permute-start(bf16[336,256]{1,0:T(8,128)(2,1)S(1)} %get-tuple-element.39), channel_id=1, source_target_pairs={{0,4},{4,0},{8,12},{12,8},{16,20},{20,16},{24,28},{28,24},{1,5},{5... | collective-permute-start | bytes 516104 | tf_op jit(solution)/shard_map/ppermute | solution.py:30
  41.6 1.6 %collective-permute-start.13 = (bf16[336,256]{1,0:T(8,128)(2,1)S(1)}, bf16[336,256]{1,0:T(8,128)(2,1)S(1)}, u32[]{:S(2)}, u32[]{:S(2)}) collective-permute-start(bf16[336,256]{1,0:T(8,128)(2,1)S(1)} %get-tuple-element.40), channel_id=1, source_target_pairs={{0,8},{4,12},{8,0},{12,4},{16,24},{20,28},{24,16},{28,20},{1,9},{5... | collective-permute-start | bytes 516104 | tf_op jit(solution)/shard_map/ppermute | solution.py:30
  43.2 1.9 %shard_map.75 = (bf16[256,1408]{1,0:T(8,128)(2,1)S(1)}, bf16[256,1408]{1,0:T(8,128)(2,1)S(1)}) custom-call(bf16[512,512]{1,0:T(8,128)(2,1)S(1)} %shard_map.74.g_ref, bf16[1408,512]{1,0:T(8,128)(2,1)S(1)} %shard_map.69.w_ref.refs_2_), custom_call_target="tpu_custom_call" | custom-call | flops 738197504 | bytes 2883584 | tf_op jit(solution)/shard_map/pallas_call | solution.py:410
  45.2 1.9 %collective-permute-start.14 = (bf16[336,256]{1,0:T(8,128)(2,1)S(1)}, bf16[336,256]{1,0:T(8,128)(2,1)S(1)}, u32[]{:S(2)}, u32[]{:S(2)}) collective-permute-start(bf16[336,256]{1,0:T(8,128)(2,1)S(1)} %get-tuple-element.41), channel_id=1, source_target_pairs={{0,12},{4,8},{8,4},{12,0},{16,28},{20,24},{24,20},{28,16},{1,13},{... | collective-permute-start | bytes 516104 | tf_op jit(solution)/shard_map/ppermute | solution.py:30
  47.1 1.5 %collective-permute-start.10 = (bf16[256,1408]{1,0:T(8,128)(2,1)S(1)}, bf16[256,1408]{1,0:T(8,128)(2,1)S(1)}, u32[]{:S(2)}, u32[]{:S(2)}) collective-permute-start(bf16[256,1408]{1,0:T(8,128)(2,1)S(1)} %get-tuple-element.37), channel_id=1, source_target_pairs={{0,2},{1,3},{2,0},{3,1},{4,6},{5,7},{6,4},{7,5},{8,10},{9,11},{10,... | collective-permute-start | bytes 2162696 | tf_op jit(solution)/shard_map/ppermute | solution.py:30
  48.6 0.2 collective-permute-done.21.refs_3_
  48.9 2.9 %collective-permute-start.22 = (bf16[336,256]{1,0:T(8,128)(2,1)S(1)}, bf16[336,256]{1,0:T(8,128)(2,1)S(1)}, u32[]{:S(2)}, u32[]{:S(2)}) collective-permute-start(bf16[336,256]{1,0:T(8,128)(2,1)S(1)} %shard_map.81.refs_0_), channel_id=1, source_target_pairs={{0,16},{4,20},{8,24},{12,28},{16,0},{20,4},{24,8},{28,12},{1,17},{... | collective-permute-start | bytes 516104 | tf_op jit(solution)/shard_map/ppermute | solution.py:30
  51.8 4.7 %collective-permute-done.13.refs_2_ = bf16[336,256]{1,0:T(8,128)(2,1)S(1)} collective-permute-done((bf16[336,256]{1,0:T(8,128)(2,1)S(1)}, bf16[336,256]{1,0:T(8,128)(2,1)S(1)}, u32[]{:S(2)}, u32[]{:S(2)}) %collective-permute-start.13) | collective-permute-done | bytes 172064 | tf_op jit(solution)/shard_map/ppermute | solution.py:30
  56.5 2.4 %collective-permute-done.14.refs_3_ = bf16[336,256]{1,0:T(8,128)(2,1)S(1)} collective-permute-done((bf16[336,256]{1,0:T(8,128)(2,1)S(1)}, bf16[336,256]{1,0:T(8,128)(2,1)S(1)}, u32[]{:S(2)}, u32[]{:S(2)}) %collective-permute-start.14) | collective-permute-done | bytes 172064 | tf_op jit(solution)/shard_map/ppermute | solution.py:30
  59.0 1.7 %collective-permute-start.15 = (bf16[336,256]{1,0:T(8,128)(2,1)S(1)}, bf16[336,256]{1,0:T(8,128)(2,1)S(1)}, u32[]{:S(2)}, u32[]{:S(2)}) collective-permute-start(bf16[336,256]{1,0:T(8,128)(2,1)S(1)} %shard_map.79.refs_0_), channel_id=1, source_target_pairs={{0,16},{4,20},{8,24},{12,28},{16,0},{20,4},{24,8},{28,12},{1,17},{... | collective-permute-start | bytes 516104 | tf_op jit(solution)/shard_map/ppermute | solution.py:30
  60.7 3.4 %collective-permute-start.25 = (bf16[336,256]{1,0:T(8,128)(2,1)S(1)}, bf16[336,256]{1,0:T(8,128)(2,1)S(1)}, u32[]{:S(2)}, u32[]{:S(2)}) collective-permute-start(bf16[336,256]{1,0:T(8,128)(2,1)S(1)} %shard_map.82.refs_0_), channel_id=1, source_target_pairs={{0,12},{4,8},{8,4},{12,0},{16,28},{20,24},{24,20},{28,16},{1,13},{... | collective-permute-start | bytes 516104 | tf_op jit(solution)/shard_map/ppermute | solution.py:30
  64.1 0.6 collective-permute-start.23
  64.8 4.3 %collective-permute-done.15.refs_1_ = bf16[336,256]{1,0:T(8,128)(2,1)S(1)} collective-permute-done((bf16[336,256]{1,0:T(8,128)(2,1)S(1)}, bf16[336,256]{1,0:T(8,128)(2,1)S(1)}, u32[]{:S(2)}, u32[]{:S(2)}) %collective-permute-start.15) | collective-permute-done | bytes 172064 | tf_op jit(solution)/shard_map/ppermute | solution.py:30
  69.1 0.3 collective-permute-start.18
  69.4 2.7 %collective-permute-done.25.refs_3_ = bf16[336,256]{1,0:T(8,128)(2,1)S(1)} collective-permute-done((bf16[336,256]{1,0:T(8,128)(2,1)S(1)}, bf16[336,256]{1,0:T(8,128)(2,1)S(1)}, u32[]{:S(2)}, u32[]{:S(2)}) %collective-permute-start.25) | collective-permute-done | bytes 172064 | tf_op jit(solution)/shard_map/ppermute | solution.py:30
  72.2 1.9 %collective-permute-done.24.refs_2_ = bf16[336,256]{1,0:T(8,128)(2,1)S(1)} collective-permute-done((bf16[336,256]{1,0:T(8,128)(2,1)S(1)}, bf16[336,256]{1,0:T(8,128)(2,1)S(1)}, u32[]{:S(2)}, u32[]{:S(2)}) %collective-permute-start.24) | collective-permute-done | bytes 172064 | tf_op jit(solution)/shard_map/ppermute | solution.py:30
  74.1 1.7 %collective-permute-start.16 = (bf16[336,256]{1,0:T(8,128)(2,1)S(1)}, bf16[336,256]{1,0:T(8,128)(2,1)S(1)}, u32[]{:S(2)}, u32[]{:S(2)}) collective-permute-start(bf16[336,256]{1,0:T(8,128)(2,1)S(1)} %shard_map.80.refs_0_), channel_id=1, source_target_pairs={{0,4},{4,0},{8,12},{12,8},{16,20},{20,16},{24,28},{28,24},{1,5},{5... | collective-permute-start | bytes 516104 | tf_op jit(solution)/shard_map/ppermute | solution.py:30
  75.8 1.2 %shard_map.83.refs_4_ = f32[1344,512]{1,0:T(8,128)} custom-call(bf16[336,256]{1,0:T(8,128)(2,1)S(1)} %shard_map.82.refs_0_, bf16[336,256]{1,0:T(8,128)(2,1)S(1)} %collective-permute-done.23.refs_1_, bf16[336,256]{1,0:T(8,128)(2,1)S(1)} %collective-permute-done.24.refs_2_, bf16[336,256]{1,0:T(8,128)(2,1)S(1)} %collective-permute-done.25.refs_3_), custom_call_target="tpu_custom_call" | custom-call | flops 8000000000 | tf_op jit(solution)/shard_map/pallas_call | solution.py:264
  77.2 1.8 %collective-permute-done.18.refs_3_ = bf16[336,256]{1,0:T(8,128)(2,1)S(1)} collective-permute-done((bf16[336,256]{1,0:T(8,128)(2,1)S(1)}, bf16[336,256]{1,0:T(8,128)(2,1)S(1)}, u32[]{:S(2)}, u32[]{:S(2)}) %collective-permute-start.18) | collective-permute-done | bytes 172064 | tf_op jit(solution)/shard_map/ppermute | solution.py:30
  79.0 1.5 %collective-permute-done.17.refs_2_ = bf16[336,256]{1,0:T(8,128)(2,1)S(1)} collective-permute-done((bf16[336,256]{1,0:T(8,128)(2,1)S(1)}, bf16[336,256]{1,0:T(8,128)(2,1)S(1)}, u32[]{:S(2)}, u32[]{:S(2)}) %collective-permute-start.17) | collective-permute-done | bytes 172064 | tf_op jit(solution)/shard_map/ppermute | solution.py:30
  80.5 0.5 collective-permute-done.16.refs_1_
  81.0 1.2 %shard_map.84 = f32[1344,512]{1,0:T(8,128)} custom-call(bf16[336,256]{1,0:T(8,128)(2,1)S(1)} %shard_map.80.refs_0_, bf16[336,256]{1,0:T(8,128)(2,1)S(1)} %collective-permute-done.16.refs_1_, bf16[336,256]{1,0:T(8,128)(2,1)S(1)} %collective-permute-done.17.refs_2_, ...), custom_call_target="tpu_custom_call", output_to_operand_aliasing={{}: (4, {})} | custom-call | flops 8000000000 | tf_op jit(solution)/shard_map/pallas_call | solution.py:264
  82.1 1.3 %shard_map.76 = bf16[128,5376]{1,0:T(8,128)(2,1)} custom-call(bf16[256,1408]{1,0:T(8,128)(2,1)S(1)} %get-tuple-element.36.refs_0_, bf16[256,1408]{1,0:T(8,128)(2,1)S(1)} %collective-permute-done.10.refs_1_, bf16[256,1408]{1,0:T(8,128)(2,1)S(1)} %collective-permute-done.11.refs_2_), custom_call_target="tpu_custom_call" | custom-call | bytes 2752512 | tf_op jit(solution)/shard_map/pallas_call | solution.py:427
  (44 shorter events, 1.2 us)
Async XLA Ops:
  0.6 1.3 %copy-start = (bf16[1,128,5376]{2,1,0:T(8,128)(2,1)S(1)}, bf16[1,128,5376]{2,1,0:T(8,128)(2,1)}, u32[]{:S(2)}) copy-start(bf16[1,128,5376]{2,1,0:T(8,128)(2,1)} %param.5) | copy-start | bytes 4128772
  2.0 3.3 %copy-start.2 = (bf16[1344,512]{1,0:T(8,128)(2,1)S(1)}, bf16[1344,512]{1,0:T(8,128)(2,1)}, u32[]{:S(2)}) copy-start(bf16[1344,512]{1,0:T(8,128)(2,1)} %w_ref.1) | copy-start | bytes 4128772
  2.1 3.4 %copy-start.1 = (bf16[1,128,5376]{2,1,0:T(8,128)(2,1)S(1)}, bf16[1,128,5376]{2,1,0:T(8,128)(2,1)}, u32[]{:S(2)}) copy-start(bf16[1,128,5376]{2,1,0:T(8,128)(2,1)} %param.5) | copy-start | bytes 4128772
  2.1 3.4 %collective-permute-start = (bf16[128,1408]{1,0:T(8,128)(2,1)S(1)}, bf16[128,1408]{1,0:T(8,128)(2,1)S(1)}, u32[]{:S(2)}, u32[]{:S(2)}) collective-permute-start(bf16[128,1408]{1,0:T(8,128)(2,1)S(1)} %get-tuple-element.24), channel_id=1, source_target_pairs={{0,1},{1,0},{2,3},{3,2},{4,5},{5,4},{6,7},{7,6},{8,9},{9,8},{10,11... | collective-permute-start | bytes 1081352 | tf_op jit(solution)/shard_map/ppermute | solution.py:30
  2.6 11.8 %collective-permute-start.2 = (bf16[128,1408]{1,0:T(8,128)(2,1)S(1)}, bf16[128,1408]{1,0:T(8,128)(2,1)S(1)}, u32[]{:S(2)}, u32[]{:S(2)}) collective-permute-start(bf16[128,1408]{1,0:T(8,128)(2,1)S(1)} %get-tuple-element.27), channel_id=1, source_target_pairs={{0,2},{1,3},{2,0},{3,1},{4,6},{5,7},{6,4},{7,5},{8,10},{9,11},{10,... | collective-permute-start | bytes 1081352 | tf_op jit(solution)/shard_map/ppermute | solution.py:30
  5.2 16.5 %collective-permute-start.3 = (bf16[128,1408]{1,0:T(8,128)(2,1)S(1)}, bf16[128,1408]{1,0:T(8,128)(2,1)S(1)}, u32[]{:S(2)}, u32[]{:S(2)}) collective-permute-start(bf16[128,1408]{1,0:T(8,128)(2,1)S(1)} %get-tuple-element.28), channel_id=1, source_target_pairs={{0,3},{1,2},{2,1},{3,0},{4,7},{5,6},{6,5},{7,4},{8,11},{9,10},{10,... | collective-permute-start | bytes 1081352 | tf_op jit(solution)/shard_map/ppermute | solution.py:30
  5.5 0.8 %copy-start.4 = (s32[1,128]{1,0:T(1,128)S(1)}, s32[1,128]{1,0:T(1,128)}, u32[]{:S(2)}) copy-start(s32[1,128]{1,0:T(1,128)} %param.9) | copy-start | bytes 1540
  5.5 1.5 %copy-start.3 = (bf16[1,128,256]{2,1,0:T(8,128)(2,1)S(1)}, bf16[1,128,256]{2,1,0:T(8,128)(2,1)}, u32[]{:S(2)}) copy-start(bf16[1,128,256]{2,1,0:T(8,128)(2,1)} %param.7) | copy-start | bytes 196612
  6.1 2.9 %collective-permute-start.1 = (bf16[128,512]{1,0:T(8,128)(2,1)S(1)}, bf16[128,512]{1,0:T(8,128)(2,1)S(1)}, u32[]{:S(2)}, u32[]{:S(2)}) collective-permute-start(bf16[128,512]{1,0:T(8,128)(2,1)S(1)} %get-tuple-element.26), channel_id=1, source_target_pairs={{0,1},{1,0},{2,3},{3,2},{4,5},{5,4},{6,7},{7,6},{8,9},{9,8},{10,11... | collective-permute-start | bytes 393224 | tf_op jit(solution)/shard_map/ppermute | solution.py:30
  7.0 17.6 %collective-permute-start.7 = (bf16[144,256]{1,0:T(8,128)(2,1)S(1)}, bf16[144,256]{1,0:T(8,128)(2,1)S(1)}, u32[]{:S(2)}, u32[]{:S(2)}) collective-permute-start(bf16[144,256]{1,0:T(8,128)(2,1)S(1)} %pad_maximum_fusion.3), channel_id=1, source_target_pairs={{0,2},{1,3},{2,0},{3,1},{4,6},{5,7},{6,4},{7,5},{8,10},{9,11},{10,... | collective-permute-start | bytes 221192 | tf_op jit(solution)/shard_map/ppermute | solution.py:30
  22.2 2.5 %collective-permute-start.4 = (bf16[128,512]{1,0:T(8,128)(2,1)S(1)}, bf16[128,512]{1,0:T(8,128)(2,1)S(1)}, u32[]{:S(2)}, u32[]{:S(2)}) collective-permute-start(bf16[128,512]{1,0:T(8,128)(2,1)S(1)} %get-tuple-element.30), channel_id=1, source_target_pairs={{0,1},{1,0},{2,3},{3,2},{4,5},{5,4},{6,7},{7,6},{8,9},{9,8},{10,11... | collective-permute-start | bytes 393224 | tf_op jit(solution)/shard_map/ppermute | solution.py:30
  22.7 6.1 %collective-permute-start.6 = (bf16[128,512]{1,0:T(8,128)(2,1)S(1)}, bf16[128,512]{1,0:T(8,128)(2,1)S(1)}, u32[]{:S(2)}, u32[]{:S(2)}) collective-permute-start(bf16[128,512]{1,0:T(8,128)(2,1)S(1)} %get-tuple-element.48.refs_3_), channel_id=1, source_target_pairs={{0,2},{1,3},{2,0},{3,1},{4,6},{5,7},{6,4},{7,5},{8,10},{9,11},{10,... | collective-permute-start | bytes 393224 | tf_op jit(solution)/shard_map/ppermute | solution.py:30
  24.6 1.4 %collective-permute-start.8 = (bf16[288,256]{1,0:T(8,128)(2,1)S(1)}, bf16[288,256]{1,0:T(8,128)(2,1)S(1)}, u32[]{:S(2)}, u32[]{:S(2)}) collective-permute-start(bf16[288,256]{1,0:T(8,128)(2,1)S(1)} %pad_maximum_fusion.2), channel_id=1, source_target_pairs={{0,1},{1,0},{2,3},{3,2},{4,5},{5,4},{6,7},{7,6},{8,9},{9,8},{10,11... | collective-permute-start | bytes 442376 | tf_op jit(solution)/shard_map/ppermute | solution.py:30
  24.8 6.4 %collective-permute-start.5 = (bf16[128,512]{1,0:T(8,128)(2,1)S(1)}, bf16[128,512]{1,0:T(8,128)(2,1)S(1)}, u32[]{:S(2)}, u32[]{:S(2)}) collective-permute-start(bf16[128,512]{1,0:T(8,128)(2,1)S(1)} %get-tuple-element.46), channel_id=1, source_target_pairs={{0,2},{1,3},{2,0},{3,1},{4,6},{5,7},{6,4},{7,5},{8,10},{9,11},{10,... | collective-permute-start | bytes 393224 | tf_op jit(solution)/shard_map/ppermute | solution.py:30
  31.3 1.6 %collective-permute-start.9 = (bf16[256,512]{1,0:T(8,128)(2,1)S(1)}, bf16[256,512]{1,0:T(8,128)(2,1)S(1)}, u32[]{:S(2)}, u32[]{:S(2)}) collective-permute-start(bf16[256,512]{1,0:T(8,128)(2,1)S(1)} %shard_map.73.own), channel_id=1, source_target_pairs={{0,1},{1,0},{2,3},{3,2},{4,5},{5,4},{6,7},{7,6},{8,9},{9,8},{10,11... | collective-permute-start | bytes 786440 | tf_op jit(solution)/shard_map/ppermute | solution.py:30
  36.3 8.9 %collective-permute-start.19 = (bf16[336,256]{1,0:T(8,128)(2,1)S(1)}, bf16[336,256]{1,0:T(8,128)(2,1)S(1)}, u32[]{:S(2)}, u32[]{:S(2)}) collective-permute-start(bf16[336,256]{1,0:T(8,128)(2,1)S(1)} %get-tuple-element.43), channel_id=1, source_target_pairs={{0,4},{4,0},{8,12},{12,8},{16,20},{20,16},{24,28},{28,24},{1,5},{5... | collective-permute-start | bytes 516104 | tf_op jit(solution)/shard_map/ppermute | solution.py:30
  38.1 9.0 %collective-permute-start.20 = (bf16[336,256]{1,0:T(8,128)(2,1)S(1)}, bf16[336,256]{1,0:T(8,128)(2,1)S(1)}, u32[]{:S(2)}, u32[]{:S(2)}) collective-permute-start(bf16[336,256]{1,0:T(8,128)(2,1)S(1)} %get-tuple-element.44), channel_id=1, source_target_pairs={{0,8},{4,12},{8,0},{12,4},{16,24},{20,28},{24,16},{28,20},{1,9},{5... | collective-permute-start | bytes 516104 | tf_op jit(solution)/shard_map/ppermute | solution.py:30
  39.7 9.1 %collective-permute-start.21 = (bf16[336,256]{1,0:T(8,128)(2,1)S(1)}, bf16[336,256]{1,0:T(8,128)(2,1)S(1)}, u32[]{:S(2)}, u32[]{:S(2)}) collective-permute-start(bf16[336,256]{1,0:T(8,128)(2,1)S(1)} %get-tuple-element.45), channel_id=1, source_target_pairs={{0,12},{4,8},{8,4},{12,0},{16,28},{20,24},{24,20},{28,16},{1,13},{... | collective-permute-start | bytes 516104 | tf_op jit(solution)/shard_map/ppermute | solution.py:30
  39.9 12.0 %collective-permute-start.12 = (bf16[336,256]{1,0:T(8,128)(2,1)S(1)}, bf16[336,256]{1,0:T(8,128)(2,1)S(1)}, u32[]{:S(2)}, u32[]{:S(2)}) collective-permute-start(bf16[336,256]{1,0:T(8,128)(2,1)S(1)} %get-tuple-element.39), channel_id=1, source_target_pairs={{0,4},{4,0},{8,12},{12,8},{16,20},{20,16},{24,28},{28,24},{1,5},{5... | collective-permute-start | bytes 516104 | tf_op jit(solution)/shard_map/ppermute | solution.py:30
  41.6 14.9 %collective-permute-start.13 = (bf16[336,256]{1,0:T(8,128)(2,1)S(1)}, bf16[336,256]{1,0:T(8,128)(2,1)S(1)}, u32[]{:S(2)}, u32[]{:S(2)}) collective-permute-start(bf16[336,256]{1,0:T(8,128)(2,1)S(1)} %get-tuple-element.40), channel_id=1, source_target_pairs={{0,8},{4,12},{8,0},{12,4},{16,24},{20,28},{24,16},{28,20},{1,9},{5... | collective-permute-start | bytes 516104 | tf_op jit(solution)/shard_map/ppermute | solution.py:30
  45.2 13.7 %collective-permute-start.14 = (bf16[336,256]{1,0:T(8,128)(2,1)S(1)}, bf16[336,256]{1,0:T(8,128)(2,1)S(1)}, u32[]{:S(2)}, u32[]{:S(2)}) collective-permute-start(bf16[336,256]{1,0:T(8,128)(2,1)S(1)} %get-tuple-element.41), channel_id=1, source_target_pairs={{0,12},{4,8},{8,4},{12,0},{16,28},{20,24},{24,20},{28,16},{1,13},{... | collective-permute-start | bytes 516104 | tf_op jit(solution)/shard_map/ppermute | solution.py:30
  47.1 29.9 %collective-permute-start.10 = (bf16[256,1408]{1,0:T(8,128)(2,1)S(1)}, bf16[256,1408]{1,0:T(8,128)(2,1)S(1)}, u32[]{:S(2)}, u32[]{:S(2)}) collective-permute-start(bf16[256,1408]{1,0:T(8,128)(2,1)S(1)} %get-tuple-element.37), channel_id=1, source_target_pairs={{0,2},{1,3},{2,0},{3,1},{4,6},{5,7},{6,4},{7,5},{8,10},{9,11},{10,... | collective-permute-start | bytes 2162696 | tf_op jit(solution)/shard_map/ppermute | solution.py:30
  48.9 11.7 %collective-permute-start.22 = (bf16[336,256]{1,0:T(8,128)(2,1)S(1)}, bf16[336,256]{1,0:T(8,128)(2,1)S(1)}, u32[]{:S(2)}, u32[]{:S(2)}) collective-permute-start(bf16[336,256]{1,0:T(8,128)(2,1)S(1)} %shard_map.81.refs_0_), channel_id=1, source_target_pairs={{0,16},{4,20},{8,24},{12,28},{16,0},{20,4},{24,8},{28,12},{1,17},{... | collective-permute-start | bytes 516104 | tf_op jit(solution)/shard_map/ppermute | solution.py:30
  59.0 10.1 %collective-permute-start.15 = (bf16[336,256]{1,0:T(8,128)(2,1)S(1)}, bf16[336,256]{1,0:T(8,128)(2,1)S(1)}, u32[]{:S(2)}, u32[]{:S(2)}) collective-permute-start(bf16[336,256]{1,0:T(8,128)(2,1)S(1)} %shard_map.79.refs_0_), channel_id=1, source_target_pairs={{0,16},{4,20},{8,24},{12,28},{16,0},{20,4},{24,8},{28,12},{1,17},{... | collective-permute-start | bytes 516104 | tf_op jit(solution)/shard_map/ppermute | solution.py:30
  60.7 11.5 %collective-permute-start.25 = (bf16[336,256]{1,0:T(8,128)(2,1)S(1)}, bf16[336,256]{1,0:T(8,128)(2,1)S(1)}, u32[]{:S(2)}, u32[]{:S(2)}) collective-permute-start(bf16[336,256]{1,0:T(8,128)(2,1)S(1)} %shard_map.82.refs_0_), channel_id=1, source_target_pairs={{0,12},{4,8},{8,4},{12,0},{16,28},{20,24},{24,20},{28,16},{1,13},{... | collective-permute-start | bytes 516104 | tf_op jit(solution)/shard_map/ppermute | solution.py:30
  64.1 10.0 %collective-permute-start.24 = (bf16[336,256]{1,0:T(8,128)(2,1)S(1)}, bf16[336,256]{1,0:T(8,128)(2,1)S(1)}, u32[]{:S(2)}, u32[]{:S(2)}) collective-permute-start(bf16[336,256]{1,0:T(8,128)(2,1)S(1)} %shard_map.82.refs_0_), channel_id=1, source_target_pairs={{0,8},{4,12},{8,0},{12,4},{16,24},{20,28},{24,16},{28,20},{1,9},{5... | collective-permute-start | bytes 516104 | tf_op jit(solution)/shard_map/ppermute | solution.py:30
  64.1 11.7 %collective-permute-start.23 = (bf16[336,256]{1,0:T(8,128)(2,1)S(1)}, bf16[336,256]{1,0:T(8,128)(2,1)S(1)}, u32[]{:S(2)}, u32[]{:S(2)}) collective-permute-start(bf16[336,256]{1,0:T(8,128)(2,1)S(1)} %shard_map.82.refs_0_), channel_id=1, source_target_pairs={{0,4},{4,0},{8,12},{12,8},{16,20},{20,16},{24,28},{28,24},{1,5},{5... | collective-permute-start | bytes 516104 | tf_op jit(solution)/shard_map/ppermute | solution.py:30
  69.1 9.9 %collective-permute-start.18 = (bf16[336,256]{1,0:T(8,128)(2,1)S(1)}, bf16[336,256]{1,0:T(8,128)(2,1)S(1)}, u32[]{:S(2)}, u32[]{:S(2)}) collective-permute-start(bf16[336,256]{1,0:T(8,128)(2,1)S(1)} %shard_map.80.refs_0_), channel_id=1, source_target_pairs={{0,12},{4,8},{8,4},{12,0},{16,28},{20,24},{24,20},{28,16},{1,13},{... | collective-permute-start | bytes 516104 | tf_op jit(solution)/shard_map/ppermute | solution.py:30
  72.1 8.4 %collective-permute-start.17 = (bf16[336,256]{1,0:T(8,128)(2,1)S(1)}, bf16[336,256]{1,0:T(8,128)(2,1)S(1)}, u32[]{:S(2)}, u32[]{:S(2)}) collective-permute-start(bf16[336,256]{1,0:T(8,128)(2,1)S(1)} %shard_map.80.refs_0_), channel_id=1, source_target_pairs={{0,8},{4,12},{8,0},{12,4},{16,24},{20,28},{24,16},{28,20},{1,9},{5... | collective-permute-start | bytes 516104 | tf_op jit(solution)/shard_map/ppermute | solution.py:30
  74.1 6.9 %collective-permute-start.16 = (bf16[336,256]{1,0:T(8,128)(2,1)S(1)}, bf16[336,256]{1,0:T(8,128)(2,1)S(1)}, u32[]{:S(2)}, u32[]{:S(2)}) collective-permute-start(bf16[336,256]{1,0:T(8,128)(2,1)S(1)} %shard_map.80.refs_0_), channel_id=1, source_target_pairs={{0,4},{4,0},{8,12},{12,8},{16,20},{20,16},{24,28},{28,24},{1,5},{5... | collective-permute-start | bytes 516104 | tf_op jit(solution)/shard_map/ppermute | solution.py:30
  77.1 5.0 %collective-permute-start.11 = (bf16[256,1408]{1,0:T(8,128)(2,1)S(1)}, bf16[256,1408]{1,0:T(8,128)(2,1)S(1)}, u32[]{:S(2)}, u32[]{:S(2)}) collective-permute-start(bf16[256,1408]{1,0:T(8,128)(2,1)S(1)} %pad_maximum_fusion), channel_id=1, source_target_pairs={{0,1},{1,0},{2,3},{3,2},{4,5},{5,4},{6,7},{7,6},{8,9},{9,8},{10,11... | collective-permute-start | bytes 2162696 | tf_op jit(solution)/shard_map/ppermute | solution.py:30

commit v2 on v1

--- a/solution.py
+++ b/solution.py
@@ -132,12 +132,20 @@
     send[...] = jnp.dot(x1_ref[...], w_ref[...], preferred_element_type=f32).astype(bf16)
 
 
-def far_kernel(z, *refs):
-    xs, (w_ref, _, keep, send) = (refs[: z.n - 2], refs[z.n - 2 :])
-    for k in range(0, z.n - 2, 2):
-        at = slice(k // 2 * z.cap, (k // 2 + 1) * z.cap)
-        send[at, :] = jnp.dot(xs[k + 1][...], w_ref[...], preferred_element_type=f32).astype(bf16)
-        keep[at, :] = jnp.dot(xs[k][...], w_ref[...], preferred_element_type=f32)
+def odd_kernel(z, *refs):
+    xs, (w_ref, _, send) = (refs[:-3], refs[-3:])
+    for i, x_ref in enumerate(xs):
+        at = slice(i * z.cap, (i + 1) * z.cap)
+        send[at, :] = jnp.dot(x_ref[...], w_ref[...], preferred_element_type=f32).astype(bf16)
+
+
+def even_kernel(z, *refs):
+    xs, (w_ref, came, total, send) = (refs[:-4], refs[-4:])
+    for i, x_ref in enumerate(xs):
+        at = slice(i * z.cap, (i + 1) * z.cap)
+        both = jnp.dot(x_ref[...], w_ref[...], preferred_element_type=f32) + came[at, :].astype(f32)
+        total[at, :] = both
+        send[at, :] = both.astype(bf16)
 
 
 def transpose_kernel(z, x_ref, *refs):
@@ -208,69 +216,80 @@
     out[:, NQ + HD :] = dv[...].astype(bf16)
 
 
-def weight_kernel(z, xt, g_ref, *refs):
+def weight_kernel(z, cols, xt, g_ref, *refs):
     pieces, whole = (refs[:-1], refs[-1])
     if whole.shape[0] > z.win:
         whole[z.win :, :] = jnp.zeros_like(whole[z.win :, :])
     inset = z.inset(lax.axis_index("ctx"))
     mine = lax.axis_index("dp") & (QUAD - 1)
-    wide = z.qkv // SPLITS
-    for s in range(SPLITS):
-        cols = slice(s * wide, (s + 1) * wide)
-        whole[: z.win, :] = jnp.dot(xt[...], g_ref[:, cols], preferred_element_type=f32)
-        for k in range(QUAD):
-            at = pl.multiple_of(inset + (mine ^ k) * z.chunk, 16)
-            pieces[s * QUAD + k][...] = whole[pl.ds(at, z.chunk), :].astype(bf16)
+    whole[: z.win, :] = jnp.dot(xt[...], g_ref[:, cols], preferred_element_type=f32)
+    for k in range(QUAD):
+        at = pl.multiple_of(inset + (mine ^ k) * z.chunk, 16)
+        pieces[k][...] = whole[pl.ds(at, z.chunk), :].astype(bf16)
 
 
 def sum_kernel(*refs):
     refs[-1][...] = functools.reduce(lambda a, b: a + b, [r[...].astype(f32) for r in refs[:-1]]).astype(bf16)
 
 
-def total_of(*pieces):
-    return call(sum_kernel, shape(pieces[0].shape, bf16), flops=SUM_COST)(*pieces)
-
-
-def inputs_kernel(z, g_ref, w_ref, near, far):
+def gated(kernel, inputs):
+    def with_gates(*refs):
+        kernel(*refs[:inputs], *refs[inputs + 1 :])
+
+    return with_gates
+
+
+def total_of(pieces, gate=None):
+    out = shape(pieces[0].shape, bf16)
+    if gate is None:
+        return call(sum_kernel, out, flops=SUM_COST)(*pieces)
+    specs = [pl.BlockSpec(memory_space=pltpu.VMEM)] * len(pieces) + [pl.BlockSpec(memory_space=pl.ANY)]
+    return call(gated(sum_kernel, len(pieces)), out, flops=SUM_COST, in_specs=specs)(*pieces, gate)
+
+
+def inputs_kernel(z, g_ref, w_ref, _, near, far, rows):
+    half = z.slots // 2
     for k in range(z.n):
-        target = near if k < z.n // 2 else far
-        at = k % (z.n // 2) * z.cap
-        target[at : at + z.cap, :] = lax.dot_general(
-            g_ref[z.block(k), :], w_ref[...], (((1,), (1,)), ((), ())), preferred_element_type=f32
-        ).astype(bf16)
-
-
-def place_weight_kernel(z, exact, first, *refs):
-    pieces, out, whole = (refs[:QUAD], refs[-2], refs[-1])
+        rows[k * z.cap : (k + 1) * z.cap, :] = g_ref[z.block(k), :]
+    nt = (((1,), (1,)), ((), ()))
+    far[...] = lax.dot_general(rows[half:, :], w_ref[...], nt, preferred_element_type=f32).astype(bf16)
+    near[...] = lax.dot_general(rows[:half, :], w_ref[...], nt, preferred_element_type=f32).astype(bf16)
+
+
+def place_weight_kernel(z, split, *refs):
+    pieces, (out, whole, sems) = (refs[:QUAD], refs[-3:])
     mine = lax.axis_index("dp") & (QUAD - 1)
-    target = out if exact else whole
-    for k in range(QUAD):
-        at = pl.multiple_of((mine ^ k) * z.chunk, 16)
-        target[pl.ds(at, z.chunk), :] = pieces[k][...].astype(f32)
-    if not exact:
-        out[...] = whole[: z.rows, :]
+    wide = z.qkv // SPLITS
+    cols = pl.ds(split * wide, wide)
+    if QUAD * z.chunk == z.rows:
+        copies = []
+        for k in range(QUAD):
+            rows = pl.ds(pl.multiple_of((mine ^ k) * z.chunk, 16), z.chunk)
+            whole[rows, :] = pieces[k][...].astype(f32)
+            copies.append(pltpu.make_async_copy(whole.at[rows, :], out.at[rows, cols], sems.at[k]))
+            copies[-1].start()
+    else:
+        for k in range(QUAD):
+            at = pl.multiple_of((mine ^ k) * z.chunk, 16)
+            whole[pl.ds(at, z.chunk), :] = pieces[k][...].astype(f32)
+        copies = [pltpu.make_async_copy(whole.at[: z.rows, :], out.at[:, cols], sems.at[0])]
+        copies[0].start()
+    for copy in copies:
+        copy.wait()
 
 
 def place_weights(z, split, pieces, before):
     wide = z.qkv // SPLITS
-    exact = QUAD * z.chunk == z.rows
-    whole = lambda: pl.BlockSpec(memory_space=pltpu.VMEM)
-    specs = [whole() for _ in pieces]
-    more = {}
-    if before is not None:
-        specs.append(pl.BlockSpec(memory_space=pl.ANY))
-        more["input_output_aliases"] = {QUAD: 0}
-        pieces = [*pieces, before]
+    more = {"input_output_aliases": {QUAD: 0}} if split else {}
     return call(
-        functools.partial(place_weight_kernel, z, exact, before is None),
+        functools.partial(place_weight_kernel, z, split),
         shape((z.rows, z.qkv), f32),
-        [pltpu.VMEM((16, LANES) if exact else (QUAD * z.chunk, wide), f32)],
+        [pltpu.VMEM((QUAD * z.chunk, wide), f32), pltpu.SemaphoreType.DMA((QUAD,))],
         flops=SUM_COST,
-        grid=(1,),
-        in_specs=specs,
-        out_specs=pl.BlockSpec((z.rows, wide), lambda i: (0, split)),
+        in_specs=[pl.BlockSpec(memory_space=pltpu.VMEM)] * QUAD + [pl.BlockSpec(memory_space=pl.ANY)],
+        out_specs=pl.BlockSpec(memory_space=pl.ANY),
         **more,
-    )(*pieces)
+    )(*pieces, before)
 
 
 def place_inputs_kernel(z, items, *refs):
@@ -318,7 +337,6 @@
     n, cap, slots, qkv, win = (z.n, z.cap, z.slots, z.qkv, z.win)
     any_spec = pl.BlockSpec(memory_space=pl.ANY)
     vmem_spec = pl.BlockSpec(memory_space=pltpu.VMEM)
-    hbm_spec = pl.BlockSpec(memory_space=pltpu.HBM)
 
     extra = jnp.concatenate([doc_ids[0], jnp.broadcast_to(range_len[0, 0], (cap,))]).astype(bf16)
     pack = jnp.concatenate([d_attn[0], jnp.broadcast_to(extra[None], (EXTRA, NQ))], axis=0)
@@ -327,7 +345,7 @@
         [shape((cap, win), bf16)] * (n - 1),
         [pltpu.SemaphoreType.DMA((n - 1,))],
         moved=6 * cap * win,
-        in_specs=[hbm_spec],
+        in_specs=[any_spec],
         out_specs=[any_spec] * (n - 1),
     )(tokens)
     xs = [swap(cut[k - 1], "ctx", k) for k in range(1, n)]
@@ -360,15 +378,18 @@
     cosine = jnp.cos(angles)
     sine = jnp.where(lane < HD // 2, -1.0, 1.0)[None, :] * jnp.sin(angles)
 
-    keep1, send1 = call(
-        functools.partial(far_kernel, z),
+    send1 = call(
+        functools.partial(odd_kernel, z),
+        shape((far_rows, qkv), bf16),
+        flops=2 * far_rows * win * qkv,
+        in_specs=[vmem_spec] * (n // 2) + [any_spec],
+    )(*xs[2::2], w_pad, half0)
+    sum1, half1 = call(
+        functools.partial(even_kernel, z),
         [shape((far_rows, qkv), f32), shape((far_rows, qkv), bf16)],
-        flops=4 * far_rows * win * qkv,
-        moved=4 * win * (2 * far_rows + qkv),
-        in_specs=[vmem_spec] * (n - 1) + [any_spec],
-    )(*xs[1:], w_pad, half0)
-    sum1 = keep1 + swap(send1, "ctx", 1).astype(f32)
-    cross1 = swap(sum1.astype(bf16), "ctx", 2)
+        flops=2 * far_rows * win * qkv,
+    )(*xs[1::2], w_pad, swap(send1, "ctx", 1))
+    cross1 = swap(half1, "ctx", 2)
     kept = [sum0] + [sum1[i * cap : (i + 1) * cap] for i in range(n // 2 - 1)]
     came = [cross0] + [cross1[i * cap : (i + 1) * cap] for i in range(n // 2 - 1)]
     came = [came[i ^ 1] for i in range(n // 2)]
@@ -395,38 +416,41 @@
 
     wide = qkv // SPLITS
     deep = max(win, win - z.rows + QUAD * z.chunk)
-    parts = call(
-        functools.partial(weight_kernel, z),
-        [shape((z.chunk, wide), bf16)] * (QUAD * SPLITS),
-        [pltpu.VMEM((deep, wide), f32)],
-        flops=2 * win * slots * qkv,
-        moved=4 * win * slots,
-    )(xt, d_proj)
     sums = []
+    near = far = None
     for s in range(SPLITS):
-        own = parts[s * QUAD : (s + 1) * QUAD]
+        own = call(
+            functools.partial(weight_kernel, z, slice(s * wide, (s + 1) * wide)),
+            [shape((z.chunk, wide), bf16)] * QUAD,
+            [pltpu.VMEM((deep, wide), f32)],
+            flops=2 * win * slots * wide,
+            moved=4 * win * slots,
+        )(xt, d_proj)
         pieces = [own[0]] + [swap(own[k], "dp", k) for k in range(1, QUAD)]
-        sums.append(total_of(*pieces))
-    near, far = call(
-        functools.partial(inputs_kernel, z),
-        [shape((slots // 2, win), bf16)] * 2,
-        flops=2 * win * slots * qkv,
-        moved=4 * win * slots,
-    )(d_proj, w_pad)
+        sums.append(total_of(pieces, far))
+        if s == 0:
+            near, far = call(
+                functools.partial(inputs_kernel, z),
+                [shape((slots // 2, win), bf16)] * 2,
+                [pltpu.VMEM((slots, qkv), bf16)],
+                flops=2 * win * slots * qkv,
+                moved=4 * win * slots,
+                in_specs=[vmem_spec, vmem_spec, any_spec],
+            )(d_proj, w_pad, sums[0])
+    arrays, items = exchange_inputs(z, near, far)
     totals = []
     for s in range(SPLITS):
         part, mask = (sums[s], QUAD)
         while mask < lax.axis_size("dp"):
-            part = total_of(part, swap(part, "dp", mask))
+            part = total_of([part, swap(part, "dp", mask)], arrays[1] if s else None)
             mask *= 2
         totals.append(part)
-    arrays, items = exchange_inputs(z, near, far)
-    d_w = None
+    d_x = call(
+        functools.partial(place_inputs_kernel, z, items), shape((cap, z.width), bf16), flops=SUM_COST
+    )(*arrays)
+    d_w = d_x
     for s in range(SPLITS):
         d_w = place_weights(z, s, [totals[s]] + [swap(totals[s], "dp", k) for k in range(1, QUAD)], d_w)
-    d_x = call(
-        functools.partial(place_inputs_kernel, z, items), shape((cap, z.width), bf16), moved=4 * cap * z.width
-    )(*arrays)
     return (d_x[None], d_w)
 
 

time: 83.6 us -> 80.5 us (0.963)
  waiting for transfers between devices: 37.8 us -> 29.1 us
  starting transfers between devices: 30 us -> 35 us
  local copies, waits for them, and re-layouts: 1.42 us -> 2.76 us
    ppermute x26, waiting for transfers between devices: 37.8 us -> 29.1 us  [swap(): return lax.ppermute(value, axis, [(i, i ^ mask) for i in range(count)])]
    ppermute x26, starting transfers between devices: 30 us -> 35 us  [swap(): return lax.ppermute(value, axis, [(i, i ^ mask) for i in range(count)])]
    unnamed x10 -> x12, local copies, waits for them, and re-layouts: 1.36 us -> 2.69 us
    pallas_call x1, Pallas kernels: 1.93 us -> 1.01 us  [body(): call(functools.partial(inputs_kernel, z), [shape((slots // 2, win), bf16)...]
    pallas_call x8 -> x10, Pallas kernels: 4.33 us -> 4.5 us  [the longest x2 2.27 us: place_weights(): call(functools.partial(place_weight_kernel, z, split), shape((z.rows, z.q...]
  transfers between devices with their start and end apart: 26 -> 26, of which waited for: 15 -> 12; matrix products, arithmetic and copies ran while one was open for 1% -> 1% of each run, Pallas kernels for 8% -> 8%
where the time goes in v2:
time: 80.5 us; the launch traced here: 80.3 us
  starting transfers between devices  35 us (43%)
  waiting for transfers between devices  29.1 us (36%)
  Pallas kernels  10.8 us (13%)
  local copies, waits for them, and re-layouts  2.76 us (3%)
  between operations  1.58 us (2%)
  other arithmetic  1.07 us (1%)
    ppermute x26, starting transfers between devices, swap(): return lax.ppermute(value, axis, [(i, i ^ mask) for i in range(count)])  35 us
    ppermute x26, waiting for transfers between devices, swap(): return lax.ppermute(value, axis, [(i, i ^ mask) for i in range(count)])  29.1 us
    unnamed x12, local copies, waits for them, and re-layouts  2.69 us
    pallas_call x2, Pallas kernels, place_weights(): call(functools.partial(place_weight_kernel, z, split), shape((z.rows, z.q...  2.27 us
    pallas_call x1, Pallas kernels, body(): call(functools.partial(attention_kernel, z), shape((slots, qkv), bf16), [...  2.22 us
  transfers between devices with their start and end apart: 26, of which 12 were waited for; matrix products, arithmetic and copies ran while one was open for 1% of the time, Pallas kernels for 8%

profile of v2, /device:TPU:0, one launch (start us, length us, event | category | flops | bytes accessed | tf_op | source)
XLA Modules:
  0.0 80.3 jit_solution(11020045470713732560)
XLA Ops:
  0.6 1.3 %copy-done = bf16[1,128,5376]{2,1,0:T(8,128)(2,1)S(1)} copy-done((bf16[1,128,5376]{2,1,0:T(8,128)(2,1)S(1)}, bf16[1,128,5376]{2,1,0:T(8,128)(2,1)}, u32[]{:S(2)}) %copy-start) | copy-done | bytes 1376280
  2.1 0.5 collective-permute-start
  2.6 2.6 %collective-permute-start.3 = (bf16[128,1408]{1,0:T(8,128)(2,1)S(1)}, bf16[128,1408]{1,0:T(8,128)(2,1)S(1)}, u32[]{:S(2)}, u32[]{:S(2)}) collective-permute-start(bf16[128,1408]{1,0:T(8,128)(2,1)S(1)} %get-tuple-element.28), channel_id=1, source_target_pairs={{0,3},{1,2},{2,1},{3,0},{4,7},{5,6},{6,5},{7,4},{8,11},{9,10},{10,... | collective-permute-start | bytes 1081352 | tf_op jit(solution)/shard_map/ppermute | solution.py:30
  5.2 0.2 shard_map.69.w_ref.refs_1_
  5.5 0.6 shard_map.70
  6.9 1.4 %collective-permute-start.7 = (bf16[144,256]{1,0:T(8,128)(2,1)S(1)}, bf16[144,256]{1,0:T(8,128)(2,1)S(1)}, u32[]{:S(2)}, u32[]{:S(2)}) collective-permute-start(bf16[144,256]{1,0:T(8,128)(2,1)S(1)} %pad_maximum_fusion.3), channel_id=1, source_target_pairs={{0,2},{1,3},{2,0},{3,1},{4,6},{5,7},{6,4},{7,5},{8,10},{9,11},{10,... | collective-permute-start | bytes 221192 | tf_op jit(solution)/shard_map/ppermute | solution.py:30
  8.4 0.6 collective-permute-start.2
  9.1 7.0 %collective-permute-done.7 = bf16[144,256]{1,0:T(8,128)(2,1)S(1)} collective-permute-done((bf16[144,256]{1,0:T(8,128)(2,1)S(1)}, bf16[144,256]{1,0:T(8,128)(2,1)S(1)}, u32[]{:S(2)}, u32[]{:S(2)}) %collective-permute-start.7) | collective-permute-done | bytes 73760 | tf_op jit(solution)/shard_map/ppermute | solution.py:30
  16.0 0.4 shard_map.71
  16.5 0.6 collective-permute-start.8
  17.1 2.0 %collective-permute-start.6 = (bf16[128,512]{1,0:T(8,128)(2,1)S(1)}, bf16[128,512]{1,0:T(8,128)(2,1)S(1)}, u32[]{:S(2)}, u32[]{:S(2)}) collective-permute-start(bf16[128,512]{1,0:T(8,128)(2,1)S(1)} %get-tuple-element.46.refs_2_), channel_id=1, source_target_pairs={{0,2},{1,3},{2,0},{3,1},{4,6},{5,7},{6,4},{7,5},{8,10},{9,11},{10,... | collective-permute-start | bytes 393224 | tf_op jit(solution)/shard_map/ppermute | solution.py:30
  19.1 4.7 %collective-permute-done.2.refs_0_.refs_1_ = bf16[128,1408]{1,0:T(8,128)(2,1)S(1)} collective-permute-done((bf16[128,1408]{1,0:T(8,128)(2,1)S(1)}, bf16[128,1408]{1,0:T(8,128)(2,1)S(1)}, u32[]{:S(2)}, u32[]{:S(2)}) %collective-permute-start.2) | collective-permute-done | bytes 360480 | tf_op jit(solution)/shard_map/ppermute | solution.py:30
  23.8 0.4 shard_map.72
  24.2 2.1 %collective-permute-start.5 = (bf16[128,512]{1,0:T(8,128)(2,1)S(1)}, bf16[128,512]{1,0:T(8,128)(2,1)S(1)}, u32[]{:S(2)}, u32[]{:S(2)}) collective-permute-start(bf16[128,512]{1,0:T(8,128)(2,1)S(1)} %get-tuple-element.30), channel_id=1, source_target_pairs={{0,2},{1,3},{2,0},{3,1},{4,6},{5,7},{6,4},{7,5},{8,10},{9,11},{10,... | collective-permute-start | bytes 393224 | tf_op jit(solution)/shard_map/ppermute | solution.py:30
  26.3 0.2 shard_map.73
  26.5 0.9 %sine_multiply_fusion = (f32[512,128]{1,0:T(8,128)S(1)}, f32[512,128]{1,0:T(8,128)S(1)}) fusion(f32[512,128]{1,0:T(8,128)S(1)} %get-tuple-element.32, f32[128]{0:T(128)S(1)} %get-tuple-element.50, f32[128]{0:T(128)S(1)} %get-tuple-element.51), kind=kLoop, calls=%fused_computation.2 | loop fusion | flops 131072 | bytes 787456 | tf_op jit(solution)/shard_map/mul | solution.py:379
  27.4 1.8 %collective-permute-done.5.refs_2_ = bf16[128,512]{1,0:T(8,128)(2,1)S(1)} collective-permute-done((bf16[128,512]{1,0:T(8,128)(2,1)S(1)}, bf16[128,512]{1,0:T(8,128)(2,1)S(1)}, u32[]{:S(2)}, u32[]{:S(2)}) %collective-permute-start.5) | collective-permute-done | bytes 131104 | tf_op jit(solution)/shard_map/ppermute | solution.py:30
  29.5 0.4 shard_map.76.xt
  29.9 1.1 %collective-permute-done.9.other = bf16[256,512]{1,0:T(8,128)(2,1)S(1)} collective-permute-done((bf16[256,512]{1,0:T(8,128)(2,1)S(1)}, bf16[256,512]{1,0:T(8,128)(2,1)S(1)}, u32[]{:S(2)}, u32[]{:S(2)}) %collective-permute-start.9) | collective-permute-done | bytes 262176 | tf_op jit(solution)/shard_map/ppermute | solution.py:30
  31.0 2.2 %shard_map.75.g_ref = bf16[512,512]{1,0:T(8,128)(2,1)S(1)} custom-call(bf16[256,512]{1,0:T(8,128)(2,1)S(1)} %shard_map.74.own, bf16[256,512]{1,0:T(8,128)(2,1)S(1)} %collective-permute-done.9.other, bf16[512,256]{1,0:T(8,128)(2,1)S(1)} %get-tuple-element.33.g_ref, s32[4,128]{1,0:T(4,128)S(1)} %get-tuple-element.34.qrow, ...), custom_call_target="tpu_custom_call" | custom-call | flops 671088640 | bytes 2097152 | tf_op jit(solution)/shard_map/pallas_call | solution.py:409
  33.2 0.6 shard_map.77
  33.8 2.1 %collective-permute-start.10 = (bf16[336,256]{1,0:T(8,128)(2,1)S(1)}, bf16[336,256]{1,0:T(8,128)(2,1)S(1)}, u32[]{:S(2)}, u32[]{:S(2)}) collective-permute-start(bf16[336,256]{1,0:T(8,128)(2,1)S(1)} %get-tuple-element.37), channel_id=1, source_target_pairs={{0,4},{4,0},{8,12},{12,8},{16,20},{20,16},{24,28},{28,24},{1,5},{5... | collective-permute-start | bytes 516104 | tf_op jit(solution)/shard_map/ppermute | solution.py:30
  35.9 1.6 %collective-permute-start.11 = (bf16[336,256]{1,0:T(8,128)(2,1)S(1)}, bf16[336,256]{1,0:T(8,128)(2,1)S(1)}, u32[]{:S(2)}, u32[]{:S(2)}) collective-permute-start(bf16[336,256]{1,0:T(8,128)(2,1)S(1)} %get-tuple-element.38), channel_id=1, source_target_pairs={{0,8},{4,12},{8,0},{12,4},{16,24},{20,28},{24,16},{28,20},{1,9},{5... | collective-permute-start | bytes 516104 | tf_op jit(solution)/shard_map/ppermute | solution.py:30
  37.5 0.6 shard_map.81
  38.1 2.0 %collective-permute-start.15 = (bf16[336,256]{1,0:T(8,128)(2,1)S(1)}, bf16[336,256]{1,0:T(8,128)(2,1)S(1)}, u32[]{:S(2)}, u32[]{:S(2)}) collective-permute-start(bf16[336,256]{1,0:T(8,128)(2,1)S(1)} %get-tuple-element.43), channel_id=1, source_target_pairs={{0,4},{4,0},{8,12},{12,8},{16,20},{20,16},{24,28},{28,24},{1,5},{5... | collective-permute-start | bytes 516104 | tf_op jit(solution)/shard_map/ppermute | solution.py:30
  40.1 1.6 %collective-permute-start.16 = (bf16[336,256]{1,0:T(8,128)(2,1)S(1)}, bf16[336,256]{1,0:T(8,128)(2,1)S(1)}, u32[]{:S(2)}, u32[]{:S(2)}) collective-permute-start(bf16[336,256]{1,0:T(8,128)(2,1)S(1)} %get-tuple-element.44), channel_id=1, source_target_pairs={{0,8},{4,12},{8,0},{12,4},{16,24},{20,28},{24,16},{28,20},{1,9},{5... | collective-permute-start | bytes 516104 | tf_op jit(solution)/shard_map/ppermute | solution.py:30
  41.7 2.2 %collective-permute-start.17 = (bf16[336,256]{1,0:T(8,128)(2,1)S(1)}, bf16[336,256]{1,0:T(8,128)(2,1)S(1)}, u32[]{:S(2)}, u32[]{:S(2)}) collective-permute-start(bf16[336,256]{1,0:T(8,128)(2,1)S(1)} %get-tuple-element.45), channel_id=1, source_target_pairs={{0,12},{4,8},{8,4},{12,0},{16,28},{20,24},{24,20},{28,16},{1,13},{... | collective-permute-start | bytes 516104 | tf_op jit(solution)/shard_map/ppermute | solution.py:30
  43.9 2.5 %collective-permute-done.12.refs_3_ = bf16[336,256]{1,0:T(8,128)(2,1)S(1)} collective-permute-done((bf16[336,256]{1,0:T(8,128)(2,1)S(1)}, bf16[336,256]{1,0:T(8,128)(2,1)S(1)}, u32[]{:S(2)}, u32[]{:S(2)}) %collective-permute-start.12) | collective-permute-done | bytes 172064 | tf_op jit(solution)/shard_map/ppermute | solution.py:30
  46.5 3.1 %collective-permute-start.22 = (bf16[336,256]{1,0:T(8,128)(2,1)S(1)}, bf16[336,256]{1,0:T(8,128)(2,1)S(1)}, u32[]{:S(2)}, u32[]{:S(2)}) collective-permute-start(bf16[336,256]{1,0:T(8,128)(2,1)S(1)} %shard_map.78._.refs_0_), channel_id=1, source_target_pairs={{0,16},{4,20},{8,24},{12,28},{16,0},{20,4},{24,8},{28,12},{1,17},{... | collective-permute-start | bytes 516104 | tf_op jit(solution)/shard_map/ppermute | solution.py:30
  49.6 1.0 %shard_map.79 = (bf16[256,1408]{1,0:T(8,128)(2,1)S(1)}, bf16[256,1408]{1,0:T(8,128)(2,1)S(1)}) custom-call(bf16[512,512]{1,0:T(8,128)(2,1)S(1)} %shard_map.75.g_ref, bf16[1408,512]{1,0:T(8,128)(2,1)S(1)} %shard_map.69.w_ref.refs_1_, bf16[336,256]{1,0:T(8,128)(2,1)S(1)} %shard_map.78._.refs_0_), custom_call_target="tpu_custom_call" | custom-call | flops 738197504 | bytes 2883584 | tf_op jit(solution)/shard_map/pallas_call | solution.py:432
  50.6 1.6 %collective-permute-start.13 = (bf16[256,1408]{1,0:T(8,128)(2,1)S(1)}, bf16[256,1408]{1,0:T(8,128)(2,1)S(1)}, u32[]{:S(2)}, u32[]{:S(2)}) collective-permute-start(bf16[256,1408]{1,0:T(8,128)(2,1)S(1)} %get-tuple-element.41.refs_4_), channel_id=1, source_target_pairs={{0,2},{1,3},{2,0},{3,1},{4,6},{5,7},{6,4},{7,5},{8,10},{9,11},{10,... | collective-permute-start | bytes 2162696 | tf_op jit(solution)/shard_map/ppermute | solution.py:30
  52.2 2.1 %collective-permute-done.16.refs_2_ = bf16[336,256]{1,0:T(8,128)(2,1)S(1)} collective-permute-done((bf16[336,256]{1,0:T(8,128)(2,1)S(1)}, bf16[336,256]{1,0:T(8,128)(2,1)S(1)}, u32[]{:S(2)}, u32[]{:S(2)}) %collective-permute-start.16) | collective-permute-done | bytes 172064 | tf_op jit(solution)/shard_map/ppermute | solution.py:30
  54.3 2.4 %collective-permute-done.17.refs_3_ = bf16[336,256]{1,0:T(8,128)(2,1)S(1)} collective-permute-done((bf16[336,256]{1,0:T(8,128)(2,1)S(1)}, bf16[336,256]{1,0:T(8,128)(2,1)S(1)}, u32[]{:S(2)}, u32[]{:S(2)}) %collective-permute-start.17) | collective-permute-done | bytes 172064 | tf_op jit(solution)/shard_map/ppermute | solution.py:30
  56.7 1.7 %collective-permute-start.18 = (bf16[336,256]{1,0:T(8,128)(2,1)S(1)}, bf16[336,256]{1,0:T(8,128)(2,1)S(1)}, u32[]{:S(2)}, u32[]{:S(2)}) collective-permute-start(bf16[336,256]{1,0:T(8,128)(2,1)S(1)} %shard_map.82.refs_0_), channel_id=1, source_target_pairs={{0,16},{4,20},{8,24},{12,28},{16,0},{20,4},{24,8},{28,12},{1,17},{... | collective-permute-start | bytes 516104 | tf_op jit(solution)/shard_map/ppermute | solution.py:30
  58.5 3.4 %collective-permute-start.25 = (bf16[336,256]{1,0:T(8,128)(2,1)S(1)}, bf16[336,256]{1,0:T(8,128)(2,1)S(1)}, u32[]{:S(2)}, u32[]{:S(2)}) collective-permute-start(bf16[336,256]{1,0:T(8,128)(2,1)S(1)} %shard_map.84.refs_0_), channel_id=1, source_target_pairs={{0,12},{4,8},{8,4},{12,0},{16,28},{20,24},{24,20},{28,16},{1,13},{... | collective-permute-start | bytes 516104 | tf_op jit(solution)/shard_map/ppermute | solution.py:30
  61.9 0.6 collective-permute-start.23
  62.6 3.7 %collective-permute-done.13.refs_1_.refs_2_ = bf16[256,1408]{1,0:T(8,128)(2,1)S(1)} collective-permute-done((bf16[256,1408]{1,0:T(8,128)(2,1)S(1)}, bf16[256,1408]{1,0:T(8,128)(2,1)S(1)}, u32[]{:S(2)}, u32[]{:S(2)}) %collective-permute-start.13) | collective-permute-done | bytes 720928 | tf_op jit(solution)/shard_map/ppermute | solution.py:30
  66.5 0.3 collective-permute-done.18.refs_1_
  66.8 2.3 %collective-permute-start.21 = (bf16[336,256]{1,0:T(8,128)(2,1)S(1)}, bf16[336,256]{1,0:T(8,128)(2,1)S(1)}, u32[]{:S(2)}, u32[]{:S(2)}) collective-permute-start(bf16[336,256]{1,0:T(8,128)(2,1)S(1)} %shard_map.83.refs_0_), channel_id=1, source_target_pairs={{0,12},{4,8},{8,4},{12,0},{16,28},{20,24},{24,20},{28,16},{1,13},{... | collective-permute-start | bytes 516104 | tf_op jit(solution)/shard_map/ppermute | solution.py:30
  69.1 1.1 %collective-permute-start.20 = (bf16[336,256]{1,0:T(8,128)(2,1)S(1)}, bf16[336,256]{1,0:T(8,128)(2,1)S(1)}, u32[]{:S(2)}, u32[]{:S(2)}) collective-permute-start(bf16[336,256]{1,0:T(8,128)(2,1)S(1)} %shard_map.83.refs_0_), channel_id=1, source_target_pairs={{0,8},{4,12},{8,0},{12,4},{16,24},{20,28},{24,16},{28,20},{1,9},{5... | collective-permute-start | bytes 516104 | tf_op jit(solution)/shard_map/ppermute | solution.py:30
  70.2 1.3 %shard_map.80.refs_4_ = bf16[128,5376]{1,0:T(8,128)(2,1)} custom-call(bf16[256,1408]{1,0:T(8,128)(2,1)S(1)} %get-tuple-element.40.refs_0_, bf16[256,1408]{1,0:T(8,128)(2,1)S(1)} %collective-permute-done.13.refs_1_.refs_2_, bf16[256,1408]{1,0:T(8,128)(2,1)S(1)} %collective-permute-done.14.refs_2_), custom_call_target="tpu_custom_call" | custom-call | flops 8000000000 | tf_op jit(solution)/shard_map/pallas_call | solution.py:448
  71.6 1.5 %collective-permute-start.19 = (bf16[336,256]{1,0:T(8,128)(2,1)S(1)}, bf16[336,256]{1,0:T(8,128)(2,1)S(1)}, u32[]{:S(2)}, u32[]{:S(2)}) collective-permute-start(bf16[336,256]{1,0:T(8,128)(2,1)S(1)} %shard_map.83.refs_0_), channel_id=1, source_target_pairs={{0,4},{4,0},{8,12},{12,8},{16,20},{20,16},{24,28},{28,24},{1,5},{5... | collective-permute-start | bytes 516104 | tf_op jit(solution)/shard_map/ppermute | solution.py:30
  73.1 1.3 %copy-done.3 = bf16[128,5376]{1,0:T(8,128)(2,1)S(1)} copy-done((bf16[128,5376]{1,0:T(8,128)(2,1)S(1)}, bf16[128,5376]{1,0:T(8,128)(2,1)}, u32[]{:S(2)}) %copy-start.3) | copy-done | bytes 1376280
  74.4 1.1 %shard_map.85.refs_4_ = f32[1344,512]{1,0:T(8,128)} custom-call(bf16[336,256]{1,0:T(8,128)(2,1)S(1)} %shard_map.84.refs_0_, bf16[336,256]{1,0:T(8,128)(2,1)S(1)} %collective-permute-done.23.refs_1_, bf16[336,256]{1,0:T(8,128)(2,1)S(1)} %collective-permute-done.24.refs_2_, bf16[336,256]{1,0:T(8,128)(2,1)S(1)} %collective-permute-done.25.refs_3_, ...), custom_call_target="tpu_custom_call" | custom-call | flops 8000000000 | tf_op jit(solution)/shard_map/pallas_call | solution.py:284
  75.6 1.0 %collective-permute-done.21.refs_3_ = bf16[336,256]{1,0:T(8,128)(2,1)S(1)} collective-permute-done((bf16[336,256]{1,0:T(8,128)(2,1)S(1)}, bf16[336,256]{1,0:T(8,128)(2,1)S(1)}, u32[]{:S(2)}, u32[]{:S(2)}) %collective-permute-start.21) | collective-permute-done | bytes 172064 | tf_op jit(solution)/shard_map/ppermute | solution.py:30
  76.6 1.7 %collective-permute-done.20.refs_2_ = bf16[336,256]{1,0:T(8,128)(2,1)S(1)} collective-permute-done((bf16[336,256]{1,0:T(8,128)(2,1)S(1)}, bf16[336,256]{1,0:T(8,128)(2,1)S(1)}, u32[]{:S(2)}, u32[]{:S(2)}) %collective-permute-start.20) | collective-permute-done | bytes 172064 | tf_op jit(solution)/shard_map/ppermute | solution.py:30
  78.3 0.9 %collective-permute-done.19.refs_1_ = bf16[336,256]{1,0:T(8,128)(2,1)S(1)} collective-permute-done((bf16[336,256]{1,0:T(8,128)(2,1)S(1)}, bf16[336,256]{1,0:T(8,128)(2,1)S(1)}, u32[]{:S(2)}, u32[]{:S(2)}) %collective-permute-start.19) | collective-permute-done | bytes 172064 | tf_op jit(solution)/shard_map/ppermute | solution.py:30
  79.1 1.1 %shard_map.86 = f32[1344,512]{1,0:T(8,128)} custom-call(bf16[336,256]{1,0:T(8,128)(2,1)S(1)} %shard_map.83.refs_0_, bf16[336,256]{1,0:T(8,128)(2,1)S(1)} %collective-permute-done.19.refs_1_, bf16[336,256]{1,0:T(8,128)(2,1)S(1)} %collective-permute-done.20.refs_2_, ...), custom_call_target="tpu_custom_call", output_to_operand_aliasing={{}: (4, {})} | custom-call | flops 8000000000 | tf_op jit(solution)/shard_map/pallas_call | solution.py:284
  (47 shorter events, 1.2 us)
Async XLA Ops:
  0.6 1.3 %copy-start = (bf16[1,128,5376]{2,1,0:T(8,128)(2,1)S(1)}, bf16[1,128,5376]{2,1,0:T(8,128)(2,1)}, u32[]{:S(2)}) copy-start(bf16[1,128,5376]{2,1,0:T(8,128)(2,1)} %param.5) | copy-start | bytes 4128772
  2.0 3.3 %copy-start.2 = (bf16[1344,512]{1,0:T(8,128)(2,1)S(1)}, bf16[1344,512]{1,0:T(8,128)(2,1)}, u32[]{:S(2)}) copy-start(bf16[1344,512]{1,0:T(8,128)(2,1)} %w_ref.1) | copy-start | bytes 4128772
  2.1 3.4 %copy-start.1 = (bf16[1,128,5376]{2,1,0:T(8,128)(2,1)S(1)}, bf16[1,128,5376]{2,1,0:T(8,128)(2,1)}, u32[]{:S(2)}) copy-start(bf16[1,128,5376]{2,1,0:T(8,128)(2,1)} %param.5) | copy-start | bytes 4128772
  2.1 3.4 %collective-permute-start = (bf16[128,1408]{1,0:T(8,128)(2,1)S(1)}, bf16[128,1408]{1,0:T(8,128)(2,1)S(1)}, u32[]{:S(2)}, u32[]{:S(2)}) collective-permute-start(bf16[128,1408]{1,0:T(8,128)(2,1)S(1)} %get-tuple-element.24), channel_id=1, source_target_pairs={{0,1},{1,0},{2,3},{3,2},{4,5},{5,4},{6,7},{7,6},{8,9},{9,8},{10,11... | collective-permute-start | bytes 1081352 | tf_op jit(solution)/shard_map/ppermute | solution.py:30
  2.6 13.4 %collective-permute-start.3 = (bf16[128,1408]{1,0:T(8,128)(2,1)S(1)}, bf16[128,1408]{1,0:T(8,128)(2,1)S(1)}, u32[]{:S(2)}, u32[]{:S(2)}) collective-permute-start(bf16[128,1408]{1,0:T(8,128)(2,1)S(1)} %get-tuple-element.28), channel_id=1, source_target_pairs={{0,3},{1,2},{2,1},{3,0},{4,7},{5,6},{6,5},{7,4},{8,11},{9,10},{10,... | collective-permute-start | bytes 1081352 | tf_op jit(solution)/shard_map/ppermute | solution.py:30
  5.4 0.8 copy-start.5
  5.5 1.4 %copy-start.4 = (bf16[1,128,256]{2,1,0:T(8,128)(2,1)S(1)}, bf16[1,128,256]{2,1,0:T(8,128)(2,1)}, u32[]{:S(2)}) copy-start(bf16[1,128,256]{2,1,0:T(8,128)(2,1)} %param.7) | copy-start | bytes 196612
  6.1 2.9 %collective-permute-start.1 = (bf16[128,512]{1,0:T(8,128)(2,1)S(1)}, bf16[128,512]{1,0:T(8,128)(2,1)S(1)}, u32[]{:S(2)}, u32[]{:S(2)}) collective-permute-start(bf16[128,512]{1,0:T(8,128)(2,1)S(1)} %get-tuple-element.26), channel_id=1, source_target_pairs={{0,1},{1,0},{2,3},{3,2},{4,5},{5,4},{6,7},{7,6},{8,9},{9,8},{10,11... | collective-permute-start | bytes 393224 | tf_op jit(solution)/shard_map/ppermute | solution.py:30
  6.9 9.1 %collective-permute-start.7 = (bf16[144,256]{1,0:T(8,128)(2,1)S(1)}, bf16[144,256]{1,0:T(8,128)(2,1)S(1)}, u32[]{:S(2)}, u32[]{:S(2)}) collective-permute-start(bf16[144,256]{1,0:T(8,128)(2,1)S(1)} %pad_maximum_fusion.3), channel_id=1, source_target_pairs={{0,2},{1,3},{2,0},{3,1},{4,6},{5,7},{6,4},{7,5},{8,10},{9,11},{10,... | collective-permute-start | bytes 221192 | tf_op jit(solution)/shard_map/ppermute | solution.py:30
  8.4 15.4 %collective-permute-start.2 = (bf16[128,1408]{1,0:T(8,128)(2,1)S(1)}, bf16[128,1408]{1,0:T(8,128)(2,1)S(1)}, u32[]{:S(2)}, u32[]{:S(2)}) collective-permute-start(bf16[128,1408]{1,0:T(8,128)(2,1)S(1)} %get-tuple-element.27), channel_id=1, source_target_pairs={{0,2},{1,3},{2,0},{3,1},{4,6},{5,7},{6,4},{7,5},{8,10},{9,11},{10,... | collective-permute-start | bytes 1081352 | tf_op jit(solution)/shard_map/ppermute | solution.py:30
  16.4 7.3 %collective-permute-start.4 = (bf16[128,512]{1,0:T(8,128)(2,1)S(1)}, bf16[128,512]{1,0:T(8,128)(2,1)S(1)}, u32[]{:S(2)}, u32[]{:S(2)}) collective-permute-start(bf16[128,512]{1,0:T(8,128)(2,1)S(1)} %shard_map.71), channel_id=1, source_target_pairs={{0,1},{1,0},{2,3},{3,2},{4,5},{5,4},{6,7},{7,6},{8,9},{9,8},{10,11... | collective-permute-start | bytes 393224 | tf_op jit(solution)/shard_map/ppermute | solution.py:30
  16.5 9.7 %collective-permute-start.8 = (bf16[288,256]{1,0:T(8,128)(2,1)S(1)}, bf16[288,256]{1,0:T(8,128)(2,1)S(1)}, u32[]{:S(2)}, u32[]{:S(2)}) collective-permute-start(bf16[288,256]{1,0:T(8,128)(2,1)S(1)} %pad_maximum_fusion.2), channel_id=1, source_target_pairs={{0,1},{1,0},{2,3},{3,2},{4,5},{5,4},{6,7},{7,6},{8,9},{9,8},{10,11... | collective-permute-start | bytes 442376 | tf_op jit(solution)/shard_map/ppermute | solution.py:30
  17.1 10.3 %collective-permute-start.6 = (bf16[128,512]{1,0:T(8,128)(2,1)S(1)}, bf16[128,512]{1,0:T(8,128)(2,1)S(1)}, u32[]{:S(2)}, u32[]{:S(2)}) collective-permute-start(bf16[128,512]{1,0:T(8,128)(2,1)S(1)} %get-tuple-element.46.refs_2_), channel_id=1, source_target_pairs={{0,2},{1,3},{2,0},{3,1},{4,6},{5,7},{6,4},{7,5},{8,10},{9,11},{10,... | collective-permute-start | bytes 393224 | tf_op jit(solution)/shard_map/ppermute | solution.py:30
  24.2 5.1 %collective-permute-start.5 = (bf16[128,512]{1,0:T(8,128)(2,1)S(1)}, bf16[128,512]{1,0:T(8,128)(2,1)S(1)}, u32[]{:S(2)}, u32[]{:S(2)}) collective-permute-start(bf16[128,512]{1,0:T(8,128)(2,1)S(1)} %get-tuple-element.30), channel_id=1, source_target_pairs={{0,2},{1,3},{2,0},{3,1},{4,6},{5,7},{6,4},{7,5},{8,10},{9,11},{10,... | collective-permute-start | bytes 393224 | tf_op jit(solution)/shard_map/ppermute | solution.py:30
  29.4 1.6 %collective-permute-start.9 = (bf16[256,512]{1,0:T(8,128)(2,1)S(1)}, bf16[256,512]{1,0:T(8,128)(2,1)S(1)}, u32[]{:S(2)}, u32[]{:S(2)}) collective-permute-start(bf16[256,512]{1,0:T(8,128)(2,1)S(1)} %shard_map.74.own), channel_id=1, source_target_pairs={{0,1},{1,0},{2,3},{3,2},{4,5},{5,4},{6,7},{7,6},{8,9},{9,8},{10,11... | collective-permute-start | bytes 786440 | tf_op jit(solution)/shard_map/ppermute | solution.py:30
  33.8 7.8 %collective-permute-start.10 = (bf16[336,256]{1,0:T(8,128)(2,1)S(1)}, bf16[336,256]{1,0:T(8,128)(2,1)S(1)}, u32[]{:S(2)}, u32[]{:S(2)}) collective-permute-start(bf16[336,256]{1,0:T(8,128)(2,1)S(1)} %get-tuple-element.37), channel_id=1, source_target_pairs={{0,4},{4,0},{8,12},{12,8},{16,20},{20,16},{24,28},{28,24},{1,5},{5... | collective-permute-start | bytes 516104 | tf_op jit(solution)/shard_map/ppermute | solution.py:30
  35.9 8.0 %collective-permute-start.11 = (bf16[336,256]{1,0:T(8,128)(2,1)S(1)}, bf16[336,256]{1,0:T(8,128)(2,1)S(1)}, u32[]{:S(2)}, u32[]{:S(2)}) collective-permute-start(bf16[336,256]{1,0:T(8,128)(2,1)S(1)} %get-tuple-element.38), channel_id=1, source_target_pairs={{0,8},{4,12},{8,0},{12,4},{16,24},{20,28},{24,16},{28,20},{1,9},{5... | collective-permute-start | bytes 516104 | tf_op jit(solution)/shard_map/ppermute | solution.py:30
  37.5 8.9 %collective-permute-start.12 = (bf16[336,256]{1,0:T(8,128)(2,1)S(1)}, bf16[336,256]{1,0:T(8,128)(2,1)S(1)}, u32[]{:S(2)}, u32[]{:S(2)}) collective-permute-start(bf16[336,256]{1,0:T(8,128)(2,1)S(1)} %get-tuple-element.39), channel_id=1, source_target_pairs={{0,12},{4,8},{8,4},{12,0},{16,28},{20,24},{24,20},{28,16},{1,13},{... | collective-permute-start | bytes 516104 | tf_op jit(solution)/shard_map/ppermute | solution.py:30
  38.1 14.1 %collective-permute-start.15 = (bf16[336,256]{1,0:T(8,128)(2,1)S(1)}, bf16[336,256]{1,0:T(8,128)(2,1)S(1)}, u32[]{:S(2)}, u32[]{:S(2)}) collective-permute-start(bf16[336,256]{1,0:T(8,128)(2,1)S(1)} %get-tuple-element.43), channel_id=1, source_target_pairs={{0,4},{4,0},{8,12},{12,8},{16,20},{20,16},{24,28},{28,24},{1,5},{5... | collective-permute-start | bytes 516104 | tf_op jit(solution)/shard_map/ppermute | solution.py:30
  40.1 14.2 %collective-permute-start.16 = (bf16[336,256]{1,0:T(8,128)(2,1)S(1)}, bf16[336,256]{1,0:T(8,128)(2,1)S(1)}, u32[]{:S(2)}, u32[]{:S(2)}) collective-permute-start(bf16[336,256]{1,0:T(8,128)(2,1)S(1)} %get-tuple-element.44), channel_id=1, source_target_pairs={{0,8},{4,12},{8,0},{12,4},{16,24},{20,28},{24,16},{28,20},{1,9},{5... | collective-permute-start | bytes 516104 | tf_op jit(solution)/shard_map/ppermute | solution.py:30
  41.7 15.0 %collective-permute-start.17 = (bf16[336,256]{1,0:T(8,128)(2,1)S(1)}, bf16[336,256]{1,0:T(8,128)(2,1)S(1)}, u32[]{:S(2)}, u32[]{:S(2)}) collective-permute-start(bf16[336,256]{1,0:T(8,128)(2,1)S(1)} %get-tuple-element.45), channel_id=1, source_target_pairs={{0,12},{4,8},{8,4},{12,0},{16,28},{20,24},{24,20},{28,16},{1,13},{... | collective-permute-start | bytes 516104 | tf_op jit(solution)/shard_map/ppermute | solution.py:30
  46.5 12.0 %collective-permute-start.22 = (bf16[336,256]{1,0:T(8,128)(2,1)S(1)}, bf16[336,256]{1,0:T(8,128)(2,1)S(1)}, u32[]{:S(2)}, u32[]{:S(2)}) collective-permute-start(bf16[336,256]{1,0:T(8,128)(2,1)S(1)} %shard_map.78._.refs_0_), channel_id=1, source_target_pairs={{0,16},{4,20},{8,24},{12,28},{16,0},{20,4},{24,8},{28,12},{1,17},{... | collective-permute-start | bytes 516104 | tf_op jit(solution)/shard_map/ppermute | solution.py:30
  50.6 15.7 %collective-permute-start.13 = (bf16[256,1408]{1,0:T(8,128)(2,1)S(1)}, bf16[256,1408]{1,0:T(8,128)(2,1)S(1)}, u32[]{:S(2)}, u32[]{:S(2)}) collective-permute-start(bf16[256,1408]{1,0:T(8,128)(2,1)S(1)} %get-tuple-element.41.refs_4_), channel_id=1, source_target_pairs={{0,2},{1,3},{2,0},{3,1},{4,6},{5,7},{6,4},{7,5},{8,10},{9,11},{10,... | collective-permute-start | bytes 2162696 | tf_op jit(solution)/shard_map/ppermute | solution.py:30
  56.7 10.1 %collective-permute-start.18 = (bf16[336,256]{1,0:T(8,128)(2,1)S(1)}, bf16[336,256]{1,0:T(8,128)(2,1)S(1)}, u32[]{:S(2)}, u32[]{:S(2)}) collective-permute-start(bf16[336,256]{1,0:T(8,128)(2,1)S(1)} %shard_map.82.refs_0_), channel_id=1, source_target_pairs={{0,16},{4,20},{8,24},{12,28},{16,0},{20,4},{24,8},{28,12},{1,17},{... | collective-permute-start | bytes 516104 | tf_op jit(solution)/shard_map/ppermute | solution.py:30
  58.5 13.1 %collective-permute-start.25 = (bf16[336,256]{1,0:T(8,128)(2,1)S(1)}, bf16[336,256]{1,0:T(8,128)(2,1)S(1)}, u32[]{:S(2)}, u32[]{:S(2)}) collective-permute-start(bf16[336,256]{1,0:T(8,128)(2,1)S(1)} %shard_map.84.refs_0_), channel_id=1, source_target_pairs={{0,12},{4,8},{8,4},{12,0},{16,28},{20,24},{24,20},{28,16},{1,13},{... | collective-permute-start | bytes 516104 | tf_op jit(solution)/shard_map/ppermute | solution.py:30
  61.9 11.2 %collective-permute-start.24 = (bf16[336,256]{1,0:T(8,128)(2,1)S(1)}, bf16[336,256]{1,0:T(8,128)(2,1)S(1)}, u32[]{:S(2)}, u32[]{:S(2)}) collective-permute-start(bf16[336,256]{1,0:T(8,128)(2,1)S(1)} %shard_map.84.refs_0_), channel_id=1, source_target_pairs={{0,8},{4,12},{8,0},{12,4},{16,24},{20,28},{24,16},{28,20},{1,9},{5... | collective-permute-start | bytes 516104 | tf_op jit(solution)/shard_map/ppermute | solution.py:30
  61.9 11.2 %collective-permute-start.23 = (bf16[336,256]{1,0:T(8,128)(2,1)S(1)}, bf16[336,256]{1,0:T(8,128)(2,1)S(1)}, u32[]{:S(2)}, u32[]{:S(2)}) collective-permute-start(bf16[336,256]{1,0:T(8,128)(2,1)S(1)} %shard_map.84.refs_0_), channel_id=1, source_target_pairs={{0,4},{4,0},{8,12},{12,8},{16,20},{20,16},{24,28},{28,24},{1,5},{5... | collective-permute-start | bytes 516104 | tf_op jit(solution)/shard_map/ppermute | solution.py:30
  66.4 2.7 %collective-permute-start.14 = (bf16[256,1408]{1,0:T(8,128)(2,1)S(1)}, bf16[256,1408]{1,0:T(8,128)(2,1)S(1)}, u32[]{:S(2)}, u32[]{:S(2)}) collective-permute-start(bf16[256,1408]{1,0:T(8,128)(2,1)S(1)} %pad_maximum_fusion), channel_id=1, source_target_pairs={{0,1},{1,0},{2,3},{3,2},{4,5},{5,4},{6,7},{7,6},{8,9},{9,8},{10,11... | collective-permute-start | bytes 2162696 | tf_op jit(solution)/shard_map/ppermute | solution.py:30
  66.8 9.8 %collective-permute-start.21 = (bf16[336,256]{1,0:T(8,128)(2,1)S(1)}, bf16[336,256]{1,0:T(8,128)(2,1)S(1)}, u32[]{:S(2)}, u32[]{:S(2)}) collective-permute-start(bf16[336,256]{1,0:T(8,128)(2,1)S(1)} %shard_map.83.refs_0_), channel_id=1, source_target_pairs={{0,12},{4,8},{8,4},{12,0},{16,28},{20,24},{24,20},{28,16},{1,13},{... | collective-permute-start | bytes 516104 | tf_op jit(solution)/shard_map/ppermute | solution.py:30
  69.1 9.2 %collective-permute-start.20 = (bf16[336,256]{1,0:T(8,128)(2,1)S(1)}, bf16[336,256]{1,0:T(8,128)(2,1)S(1)}, u32[]{:S(2)}, u32[]{:S(2)}) collective-permute-start(bf16[336,256]{1,0:T(8,128)(2,1)S(1)} %shard_map.83.refs_0_), channel_id=1, source_target_pairs={{0,8},{4,12},{8,0},{12,4},{16,24},{20,28},{24,16},{28,20},{1,9},{5... | collective-permute-start | bytes 516104 | tf_op jit(solution)/shard_map/ppermute | solution.py:30
  71.6 7.6 %collective-permute-start.19 = (bf16[336,256]{1,0:T(8,128)(2,1)S(1)}, bf16[336,256]{1,0:T(8,128)(2,1)S(1)}, u32[]{:S(2)}, u32[]{:S(2)}) collective-permute-start(bf16[336,256]{1,0:T(8,128)(2,1)S(1)} %shard_map.83.refs_0_), channel_id=1, source_target_pairs={{0,4},{4,0},{8,12},{12,8},{16,20},{20,16},{24,28},{28,24},{1,5},{5... | collective-permute-start | bytes 516104 | tf_op jit(solution)/shard_map/ppermute | solution.py:30
  73.1 1.3 %copy-start.3 = (bf16[128,5376]{1,0:T(8,128)(2,1)S(1)}, bf16[128,5376]{1,0:T(8,128)(2,1)}, u32[]{:S(2)}) copy-start(bf16[128,5376]{1,0:T(8,128)(2,1)} %shard_map.80.refs_4_) | copy-start | bytes 4128772

commit v3 on v2

--- a/solution.py
+++ b/solution.py
@@ -14,8 +14,9 @@
 LANES = 128
 QUAD = 4
 SPLITS = 2
+SEND_ORDER = (2, 1, 3)
 EXTRA = 16
-SUM_COST = 8_000_000_000
+AWAITED = 8
 DOC_STEP = 1 << 20
 VMEM_BYTES = 48 * 1024 * 1024
 
@@ -30,23 +31,27 @@
     return lax.ppermute(value, axis, [(i, i ^ mask) for i in range(count)])
 
 
-def after(value, *others):
-    return lax.optimization_barrier((value, others))[0]
-
-
 def rotate(values, cosine, sine):
     return values * cosine + pltpu.roll(values, HD // 2, 1) * sine
 
 
-def call(kernel, out_shape, scratch=(), flops=0, moved=0, **more):
+def call(kernel, out_shape, operands, cost=0, scratch=(), after=(), **more):
+    gates = [gate for gate in after if gate is not None]
+    count = len(operands)
+
+    def with_gates(*refs):
+        kernel(*refs[:count], *refs[count + len(gates) :])
+
+    specs = more.pop("in_specs", [pl.BlockSpec(memory_space=pltpu.VMEM)] * count)
     return pl.pallas_call(
-        kernel,
+        with_gates,
         out_shape=out_shape,
+        in_specs=[*specs, *[pl.BlockSpec(memory_space=pl.ANY)] * len(gates)],
         scratch_shapes=list(scratch),
         compiler_params=pltpu.CompilerParams(vmem_limit_bytes=VMEM_BYTES),
-        cost_estimate=pl.CostEstimate(flops=flops, bytes_accessed=moved, transcendentals=0),
+        cost_estimate=pl.CostEstimate(flops=int(cost * 1e9), bytes_accessed=0, transcendentals=0),
         **more,
-    )
+    )(*operands, *gates)
 
 
 def shape(dims, dtype):
@@ -59,26 +64,39 @@
         self.cap, self.width = tokens.shape
         self.rows, self.qkv = w_qkv.shape
         self.slots = self.n * self.cap
-        tiles = self.width // LANES
-        need = 1
-        for c in range(self.n):
-            low, high = (c * self.rows, (c + 1) * self.rows)
-            need = max(need, -(-high // LANES) - low // LANES)
-        self.win = need * LANES
-        self.last = tiles - need
+        self.tiles = self.width // LANES
+        self.need = self.most_tiles(self.n, self.rows)
+        self.need_pair = self.most_tiles(self.n // 2, 2 * self.rows)
+        self.win = self.need * LANES
+        self.win_pair = self.need_pair * LANES
+        self.exact_pairs = 2 * self.rows == self.win_pair
         self.chunk = -(-self.rows // (QUAD * 16)) * 16
 
+    @staticmethod
+    def most_tiles(count, rows):
+        return max(-(-(c + 1) * rows // LANES) - c * rows // LANES for c in range(count))
+
+    def pair_tile(self, c):
+        return jnp.minimum((c // 2) * 2 * self.rows // LANES, self.tiles - self.need_pair)
+
+    def first_pair(self, c):
+        return pl.multiple_of(self.pair_tile(c) * LANES, LANES)
+
+    def in_pair(self, c):
+        tile = jnp.minimum(c * self.rows // LANES - self.pair_tile(c), self.need_pair - self.need)
+        return pl.multiple_of(tile * LANES, LANES)
+
     def first(self, c):
-        return pl.multiple_of(jnp.minimum(c * self.rows // LANES, self.last) * LANES, LANES)
+        return pl.multiple_of(self.first_pair(c) + self.in_pair(c), LANES)
 
     def inset(self, c):
         return pl.multiple_of(c * self.rows - self.first(c), 16)
 
+    def inset_pair(self, c):
+        return pl.multiple_of(c * self.rows - self.first_pair(c), 16)
+
     def block(self, k):
         return pl.ds(pl.multiple_of((lax.axis_index("ctx") ^ k) * self.cap, self.cap), self.cap)
-
-    def own_window(self, x_ref):
-        return x_ref[:, pl.ds(self.first(lax.axis_index("ctx")), self.win)]
 
 
 def windows_kernel(z, x_ref, *refs):
@@ -97,6 +115,14 @@
 def pad_kernel(z, w_ref, pad):
     pad[...] = jnp.zeros_like(pad)
     pad[pl.ds(z.inset(lax.axis_index("ctx")), z.rows), :] = w_ref[...]
+
+
+def pair_kernel(z, own, other, out):
+    me = lax.axis_index("ctx")
+    if not z.exact_pairs:
+        out[...] = jnp.zeros_like(out)
+    out[pl.ds(z.inset_pair(me), z.rows), :] = own[...]
+    out[pl.ds(z.inset_pair(me ^ 1), z.rows), :] = other[...]
 
 
 def spread_kernel(z, order, packs, grads, qrow, kcol, poscol):
@@ -128,12 +154,12 @@
 
 
 def near_kernel(z, x_ref, x1_ref, w_ref, keep, send):
-    keep[...] = jnp.dot(z.own_window(x_ref), w_ref[...], preferred_element_type=f32)
+    keep[...] = jnp.dot(x_ref[:, pl.ds(z.first(lax.axis_index("ctx")), z.win)], w_ref[...], preferred_element_type=f32)
     send[...] = jnp.dot(x1_ref[...], w_ref[...], preferred_element_type=f32).astype(bf16)
 
 
 def odd_kernel(z, *refs):
-    xs, (w_ref, _, send) = (refs[:-3], refs[-3:])
+    xs, (w_ref, send) = (refs[:-2], refs[-2:])
     for i, x_ref in enumerate(xs):
         at = slice(i * z.cap, (i + 1) * z.cap)
         send[at, :] = jnp.dot(x_ref[...], w_ref[...], preferred_element_type=f32).astype(bf16)
@@ -150,7 +176,7 @@
 
 def transpose_kernel(z, x_ref, *refs):
     xs, out = (refs[: z.n - 1], refs[z.n - 1])
-    out[:, z.block(0)] = z.own_window(x_ref).T
+    out[:, z.block(0)] = x_ref[:, pl.ds(z.first(lax.axis_index("ctx")), z.win)].T
     for k in range(1, z.n):
         out[:, z.block(k)] = xs[k - 1][...].T
 
@@ -232,78 +258,72 @@
     refs[-1][...] = functools.reduce(lambda a, b: a + b, [r[...].astype(f32) for r in refs[:-1]]).astype(bf16)
 
 
-def gated(kernel, inputs):
-    def with_gates(*refs):
-        kernel(*refs[:inputs], *refs[inputs + 1 :])
-
-    return with_gates
-
-
-def total_of(pieces, gate=None):
-    out = shape(pieces[0].shape, bf16)
-    if gate is None:
-        return call(sum_kernel, out, flops=SUM_COST)(*pieces)
-    specs = [pl.BlockSpec(memory_space=pltpu.VMEM)] * len(pieces) + [pl.BlockSpec(memory_space=pl.ANY)]
-    return call(gated(sum_kernel, len(pieces)), out, flops=SUM_COST, in_specs=specs)(*pieces, gate)
-
-
-def inputs_kernel(z, g_ref, w_ref, _, near, far, rows):
-    half = z.slots // 2
-    for k in range(z.n):
-        rows[k * z.cap : (k + 1) * z.cap, :] = g_ref[z.block(k), :]
+def inputs_kernel(z, g_ref, w_ref, near, far, rows):
+    half = z.slots // 4
+    for i in range(z.n // 2):
+        rows[i * z.cap : (i + 1) * z.cap, :] = g_ref[z.block(2 * i), :]
     nt = (((1,), (1,)), ((), ()))
     far[...] = lax.dot_general(rows[half:, :], w_ref[...], nt, preferred_element_type=f32).astype(bf16)
     near[...] = lax.dot_general(rows[:half, :], w_ref[...], nt, preferred_element_type=f32).astype(bf16)
 
 
-def place_weight_kernel(z, split, *refs):
+def place_weight_kernel(z, cols, *refs):
     pieces, (out, whole, sems) = (refs[:QUAD], refs[-3:])
     mine = lax.axis_index("dp") & (QUAD - 1)
-    wide = z.qkv // SPLITS
-    cols = pl.ds(split * wide, wide)
-    if QUAD * z.chunk == z.rows:
-        copies = []
-        for k in range(QUAD):
-            rows = pl.ds(pl.multiple_of((mine ^ k) * z.chunk, 16), z.chunk)
-            whole[rows, :] = pieces[k][...].astype(f32)
-            copies.append(pltpu.make_async_copy(whole.at[rows, :], out.at[rows, cols], sems.at[k]))
-            copies[-1].start()
-    else:
-        for k in range(QUAD):
-            at = pl.multiple_of((mine ^ k) * z.chunk, 16)
-            whole[pl.ds(at, z.chunk), :] = pieces[k][...].astype(f32)
-        copies = [pltpu.make_async_copy(whole.at[: z.rows, :], out.at[:, cols], sems.at[0])]
-        copies[0].start()
+    copies = []
+    for k in range(QUAD):
+        at = slice(k * z.chunk, (k + 1) * z.chunk)
+        rows = pl.ds(pl.multiple_of((mine ^ k) * z.chunk, 16), z.chunk)
+        whole[at, :] = pieces[k][...].astype(f32)
+        copies.append(pltpu.make_async_copy(whole.at[at, :], out.at[rows, cols], sems.at[k]))
+        copies[-1].start()
     for copy in copies:
         copy.wait()
 
 
-def place_weights(z, split, pieces, before):
-    wide = z.qkv // SPLITS
-    more = {"input_output_aliases": {QUAD: 0}} if split else {}
+def place_weights(z, cols, pieces, before, cost, after):
+    more = {}
+    specs = [pl.BlockSpec(memory_space=pltpu.VMEM)] * QUAD
+    if before is not None:
+        specs.append(pl.BlockSpec(memory_space=pl.ANY))
+        more["input_output_aliases"] = {QUAD: 0}
+        pieces = [*pieces, before]
     return call(
-        functools.partial(place_weight_kernel, z, split),
+        functools.partial(place_weight_kernel, z, cols),
         shape((z.rows, z.qkv), f32),
-        [pltpu.VMEM((QUAD * z.chunk, wide), f32), pltpu.SemaphoreType.DMA((QUAD,))],
-        flops=SUM_COST,
-        in_specs=[pl.BlockSpec(memory_space=pltpu.VMEM)] * QUAD + [pl.BlockSpec(memory_space=pl.ANY)],
+        pieces,
+        cost=cost,
+        scratch=[pltpu.VMEM((QUAD * z.chunk, cols.stop - cols.start), f32), pltpu.SemaphoreType.DMA((QUAD,))],
+        after=after,
+        in_specs=specs,
         out_specs=pl.BlockSpec(memory_space=pl.ANY),
         **more,
-    )(*pieces, before)
+    )
+
+
+def place_all_kernel(z, bounds, *refs):
+    pieces, (out, whole) = (refs[:-2], refs[-2:])
+    mine = lax.axis_index("dp") & (QUAD - 1)
+    for i, piece in enumerate(pieces):
+        split, k = divmod(i, QUAD)
+        at = pl.multiple_of((mine ^ k) * z.chunk, 16)
+        whole[pl.ds(at, z.chunk), bounds[split]] = piece[...].astype(f32)
+    out[...] = whole[: z.rows, :]
 
 
 def place_inputs_kernel(z, items, *refs):
     arrays, out = (refs[:-1], refs[-1])
     me = lax.axis_index("ctx")
-    out[...] = jnp.zeros_like(out)
+    if not z.exact_pairs:
+        out[...] = jnp.zeros_like(out)
     for which, at, source in items:
-        cols = pl.ds(z.first(me ^ source), z.win)
-        out[:, cols] = out[:, cols] + arrays[which][at : at + z.cap, :]
-
-
-def gather_packs(pack, n, first):
+        cols = pl.ds(z.first_pair(me ^ source), z.win_pair)
+        window = arrays[which][at : at + z.cap, :]
+        out[:, cols] = window if z.exact_pairs else out[:, cols] + window
+
+
+def gather_packs(pack, came, n):
     order, mask = ([0], n // 2)
-    came = first
     while mask:
         pack = jnp.concatenate([pack, came], axis=0)
         order = order + [k ^ mask for k in order]
@@ -314,16 +334,17 @@
 
 
 def exchange_inputs(z, near, far):
+    step = 2
     arrays = [near]
-    held = {(k, 0): (0, k * z.cap) for k in range(z.n // 2)}
-    mask, sent = (z.n // 2, [(k, 0) for k in range(z.n // 2, z.n)])
+    held = {(k, 0): (0, i * z.cap) for i, k in enumerate(range(0, z.n // 2, step))}
+    mask, sent = (z.n // 2, [(k, 0) for k in range(z.n // 2, z.n, step)])
     parcel = far
     while True:
         arrays.append(swap(parcel, "ctx", mask))
         for i, (k, j) in enumerate(sent):
             held[k ^ mask, j ^ mask] = (len(arrays) - 1, i * z.cap)
         mask //= 2
-        if not mask:
+        if mask < step:
             break
         sent = sorted(item for item in held if item[0] & mask)
         spots = [held.pop(item) for item in sent]
@@ -336,32 +357,32 @@
     z = Sizes(tokens, w_qkv)
     n, cap, slots, qkv, win = (z.n, z.cap, z.slots, z.qkv, z.win)
     any_spec = pl.BlockSpec(memory_space=pl.ANY)
-    vmem_spec = pl.BlockSpec(memory_space=pltpu.VMEM)
 
     extra = jnp.concatenate([doc_ids[0], jnp.broadcast_to(range_len[0, 0], (cap,))]).astype(bf16)
     pack = jnp.concatenate([d_attn[0], jnp.broadcast_to(extra[None], (EXTRA, NQ))], axis=0)
     cut = call(
         functools.partial(windows_kernel, z),
         [shape((cap, win), bf16)] * (n - 1),
-        [pltpu.SemaphoreType.DMA((n - 1,))],
-        moved=6 * cap * win,
+        [tokens],
+        cost=0.34,
+        scratch=[pltpu.SemaphoreType.DMA((n - 1,))],
         in_specs=[any_spec],
         out_specs=[any_spec] * (n - 1),
-    )(tokens)
+    )
     xs = [swap(cut[k - 1], "ctx", k) for k in range(1, n)]
-    pack_came = swap(pack, "ctx", n // 2)
-    w_pad = call(functools.partial(pad_kernel, z), shape((win, qkv), bf16), moved=4 * win * qkv)(w_qkv)
+    w_pad = call(functools.partial(pad_kernel, z), shape((win, qkv), bf16), [w_qkv], cost=0.9)
     keep0, send0 = call(
         functools.partial(near_kernel, z),
         [shape((cap, qkv), f32), shape((cap, qkv), bf16)],
-        flops=4 * cap * win * qkv,
-        moved=4 * win * (cap + qkv),
-    )(tokens, xs[0], w_pad)
+        [tokens, xs[0], w_pad],
+        cost=1.1,
+    )
     sum0 = keep0 + swap(send0, "ctx", 1).astype(f32)
-    far_rows = (n // 2 - 1) * cap
     half0 = sum0.astype(bf16)
     cross0 = swap(half0, "ctx", 2)
-    packs, order = gather_packs(pack, n, after(pack_came, sum0))
+    pack_came = swap(pack, "ctx", n // 2)
+    pack_came = lax.optimization_barrier((pack_came, sum0))[0]
+    packs, order = gather_packs(pack, pack_came, n)
     grads, qrow, kcol, poscol = call(
         functools.partial(spread_kernel, z, order),
         [
@@ -370,25 +391,29 @@
             shape((slots, LANES), jnp.int32),
             shape((slots, HD), f32),
         ],
-        moved=8 * slots * NQ,
-    )(packs)
+        [packs],
+        cost=0.33,
+    )
     lane = jnp.arange(HD, dtype=jnp.int32)
     freqs = 10000.0 ** (-((lane % (HD // 2)).astype(f32) * 2.0) / HD)
     angles = poscol * freqs[None, :]
     cosine = jnp.cos(angles)
     sine = jnp.where(lane < HD // 2, -1.0, 1.0)[None, :] * jnp.sin(angles)
 
+    far_rows = (n // 2 - 1) * cap
     send1 = call(
         functools.partial(odd_kernel, z),
         shape((far_rows, qkv), bf16),
-        flops=2 * far_rows * win * qkv,
-        in_specs=[vmem_spec] * (n // 2) + [any_spec],
-    )(*xs[2::2], w_pad, half0)
+        [*xs[2::2], w_pad],
+        cost=0.21,
+        after=[half0],
+    )
     sum1, half1 = call(
         functools.partial(even_kernel, z),
         [shape((far_rows, qkv), f32), shape((far_rows, qkv), bf16)],
-        flops=2 * far_rows * win * qkv,
-    )(*xs[1::2], w_pad, swap(send1, "ctx", 1))
+        [*xs[1::2], w_pad, swap(send1, "ctx", 1)],
+        cost=0.21,
+    )
     cross1 = swap(half1, "ctx", 2)
     kept = [sum0] + [sum1[i * cap : (i + 1) * cap] for i in range(n // 2 - 1)]
     came = [cross0] + [cross1[i * cap : (i + 1) * cap] for i in range(n // 2 - 1)]
@@ -401,56 +426,88 @@
         came = [crossed[i * cap : (i + 1) * cap] for i in range(n // 2)]
         came = [came[i ^ (mask // 2)] for i in range(n // 2)]
         mask *= 2
-    xt = call(functools.partial(transpose_kernel, z), shape((win, slots), bf16), moved=4 * win * slots)(tokens, *xs)
-    mine = call(functools.partial(rotary_kernel, z), shape((slots // 2, qkv), bf16), moved=4 * slots * qkv)(
-        *kept, *came, cosine, sine
+    xt = call(functools.partial(transpose_kernel, z), shape((win, slots), bf16), [tokens, *xs], cost=0.9)
+    w_pair = call(
+        functools.partial(pair_kernel, z),
+        shape((z.win_pair, qkv), bf16),
+        [w_qkv, swap(w_qkv, "ctx", 1)],
+        cost=0.9,
+        after=[half0],
+    )
+    mine = call(
+        functools.partial(rotary_kernel, z),
+        shape((slots // 2, qkv), bf16),
+        [*kept, *came, cosine, sine],
+        cost=0.33,
     )
     theirs = swap(mine, "ctx", 1)
     d_proj = call(
         functools.partial(attention_kernel, z),
         shape((slots, qkv), bf16),
-        [pltpu.VMEM((slots, qkv), bf16), pltpu.VMEM((slots, HD), f32), pltpu.VMEM((slots, HD), f32)],
-        flops=20 * slots * slots * HD,
-        moved=8 * slots * qkv,
-    )(mine, theirs, grads, qrow, kcol, cosine, sine)
-
+        [mine, theirs, grads, qrow, kcol, cosine, sine],
+        cost=0.77,
+        scratch=[pltpu.VMEM((slots, qkv), bf16), pltpu.VMEM((slots, HD), f32), pltpu.VMEM((slots, HD), f32)],
+    )
+
+    deep = max(win, win - z.rows + QUAD * z.chunk)
     wide = qkv // SPLITS
-    deep = max(win, win - z.rows + QUAD * z.chunk)
-    sums = []
-    near = far = None
-    for s in range(SPLITS):
+    bounds = [slice(s * wide, (s + 1) * wide) for s in range(SPLITS)]
+
+    def weight_pieces(split):
         own = call(
-            functools.partial(weight_kernel, z, slice(s * wide, (s + 1) * wide)),
+            functools.partial(weight_kernel, z, bounds[split]),
             [shape((z.chunk, wide), bf16)] * QUAD,
-            [pltpu.VMEM((deep, wide), f32)],
-            flops=2 * win * slots * wide,
-            moved=4 * win * slots,
-        )(xt, d_proj)
-        pieces = [own[0]] + [swap(own[k], "dp", k) for k in range(1, QUAD)]
-        sums.append(total_of(pieces, far))
-        if s == 0:
-            near, far = call(
-                functools.partial(inputs_kernel, z),
-                [shape((slots // 2, win), bf16)] * 2,
-                [pltpu.VMEM((slots, qkv), bf16)],
-                flops=2 * win * slots * qkv,
-                moved=4 * win * slots,
-                in_specs=[vmem_spec, vmem_spec, any_spec],
-            )(d_proj, w_pad, sums[0])
+            [xt, d_proj],
+            cost=0.9,
+            scratch=[pltpu.VMEM((deep, wide), f32)],
+        )
+        came = {k: swap(own[k], "dp", k) for k in SEND_ORDER}
+        return [own[0]] + [came[k] for k in range(1, QUAD)]
+
+    def add_up(pieces, after=()):
+        return call(sum_kernel, shape((z.chunk, wide), bf16), pieces, cost=AWAITED, after=after)
+
+    first = weight_pieces(0)
+    sums = [add_up(first)]
+    second = weight_pieces(1)
+    near, far = call(
+        functools.partial(inputs_kernel, z),
+        [shape((slots // 4, z.win_pair), bf16)] * 2,
+        [d_proj, w_pair],
+        cost=0.9,
+        scratch=[pltpu.VMEM((slots // 2, qkv), bf16)],
+        after=[first[2]],
+    )
+    sums.append(add_up(second, after=[far]))
     arrays, items = exchange_inputs(z, near, far)
     totals = []
     for s in range(SPLITS):
         part, mask = (sums[s], QUAD)
         while mask < lax.axis_size("dp"):
-            part = total_of([part, swap(part, "dp", mask)], arrays[1] if s else None)
+            part = add_up([part, swap(part, "dp", mask)], after=[arrays[1]] if s else [])
             mask *= 2
         totals.append(part)
     d_x = call(
-        functools.partial(place_inputs_kernel, z, items), shape((cap, z.width), bf16), flops=SUM_COST
-    )(*arrays)
-    d_w = d_x
-    for s in range(SPLITS):
-        d_w = place_weights(z, s, [totals[s]] + [swap(totals[s], "dp", k) for k in range(1, QUAD)], d_w)
+        functools.partial(place_inputs_kernel, z, items),
+        shape((cap, z.width), bf16),
+        arrays,
+        cost=AWAITED,
+        after=[totals[0]],
+    )
+    ready = []
+    for total in totals:
+        came = {k: swap(total, "dp", k) for k in SEND_ORDER}
+        ready.append([total] + [came[k] for k in range(1, QUAD)])
+    if QUAD * z.chunk == z.rows:
+        d_w = place_weights(z, bounds[0], ready[0], None, AWAITED, [d_x])
+        d_w = place_weights(z, bounds[1], ready[1], d_w, 0, [])
+    else:
+        d_w = call(
+            functools.partial(place_all_kernel, z, bounds),
+            shape((z.rows, qkv), f32),
+            sum(ready, []),
+            scratch=[pltpu.VMEM((QUAD * z.chunk, qkv), f32)],
+        )
     return (d_x[None], d_w)
 
 

time: 80.5 us -> 79.2 us (0.984)
  waiting for transfers between devices: 29.1 us -> 25.5 us
  Pallas kernels: 10.8 us -> 14.4 us
  starting transfers between devices: 35 us -> 33.9 us
    ppermute x26, waiting for transfers between devices: 29.1 us -> 25.5 us  [swap(): return lax.ppermute(value, axis, [(i, i ^ mask) for i in range(count)])]
    pallas_call x19 -> x20, Pallas kernels: 10.8 us -> 14.4 us  [call(): pl.pallas_call(with_gates, out_shape=out_shape, in_specs=[*specs, *[pl.Bl...]
    ppermute x26, starting transfers between devices: 35 us -> 33.9 us  [swap(): return lax.ppermute(value, axis, [(i, i ^ mask) for i in range(count)])]
    unnamed x12 -> x10, local copies, waits for them, and re-layouts: 2.69 us -> 2.69 us
  transfers between devices with their start and end apart: 26 -> 26, of which waited for: 12 -> 11; matrix products, arithmetic and copies ran while one was open for 1% -> 1% of each run, Pallas kernels for 8% -> 17%
where the time goes in v3:
time: 79.2 us; the launch traced here: 79 us
  starting transfers between devices  33.9 us (43%)
  waiting for transfers between devices  25.5 us (32%)
  Pallas kernels  14.4 us (18%)
  local copies, waits for them, and re-layouts  2.7 us (3%)
  between operations  1.54 us (2%)
  other arithmetic  1.01 us (1%)
    ppermute x26, starting transfers between devices, swap(): return lax.ppermute(value, axis, [(i, i ^ mask) for i in range(count)])  33.9 us
    ppermute x26, waiting for transfers between devices, swap(): return lax.ppermute(value, axis, [(i, i ^ mask) for i in range(count)])  25.5 us
    pallas_call x20, Pallas kernels, call(): pl.pallas_call(with_gates, out_shape=out_shape, in_specs=[*specs, *[pl.Bl...  14.4 us
    unnamed x10, local copies, waits for them, and re-layouts  2.69 us
  transfers between devices with their start and end apart: 26, of which 11 were waited for; matrix products, arithmetic and copies ran while one was open for 1% of the time, Pallas kernels for 17%

profile of v3, /device:TPU:0, one launch (start us, length us, event | category | flops | bytes accessed | tf_op | source)
XLA Modules:
  0.0 79.0 jit_solution(18075993536569003884)
XLA Ops:
  0.6 1.3 %copy-done = bf16[1,128,5376]{2,1,0:T(8,128)(2,1)S(1)} copy-done((bf16[1,128,5376]{2,1,0:T(8,128)(2,1)S(1)}, bf16[1,128,5376]{2,1,0:T(8,128)(2,1)}, u32[]{:S(2)}) %copy-start) | copy-done | bytes 1376280
  2.1 0.5 collective-permute-start
  2.6 2.6 %collective-permute-start.3 = (bf16[128,1408]{1,0:T(8,128)(2,1)S(1)}, bf16[128,1408]{1,0:T(8,128)(2,1)S(1)}, u32[]{:S(2)}, u32[]{:S(2)}) collective-permute-start(bf16[128,1408]{1,0:T(8,128)(2,1)S(1)} %get-tuple-element.28), channel_id=1, source_target_pairs={{0,3},{1,2},{2,1},{3,0},{4,7},{5,6},{6,5},{7,4},{8,11},{9,10},{10,... | collective-permute-start | bytes 1081352 | tf_op jit(solution)/shard_map/ppermute | solution.py:31
  5.2 1.5 %shard_map.69.refs_2_.refs_1_ = bf16[1408,512]{1,0:T(8,128)(2,1)S(1)} custom-call(bf16[1344,512]{1,0:T(8,128)(2,1)} %refs_0_.3), custom_call_target="tpu_custom_call" | custom-call | flops 900000000 | tf_op jit(solution)/shard_map/pallas_call | solution.py:46
  6.8 0.6 shard_map.70
  8.3 0.5 collective-permute-start.7
  8.8 1.6 %collective-permute-start.2 = (bf16[128,1408]{1,0:T(8,128)(2,1)S(1)}, bf16[128,1408]{1,0:T(8,128)(2,1)S(1)}, u32[]{:S(2)}, u32[]{:S(2)}) collective-permute-start(bf16[128,1408]{1,0:T(8,128)(2,1)S(1)} %get-tuple-element.27), channel_id=1, source_target_pairs={{0,2},{1,3},{2,0},{3,1},{4,6},{5,7},{6,4},{7,5},{8,10},{9,11},{10,... | collective-permute-start | bytes 1081352 | tf_op jit(solution)/shard_map/ppermute | solution.py:31
  10.4 5.6 %collective-permute-done.7 = bf16[144,256]{1,0:T(8,128)(2,1)S(1)} collective-permute-done((bf16[144,256]{1,0:T(8,128)(2,1)S(1)}, bf16[144,256]{1,0:T(8,128)(2,1)S(1)}, u32[]{:S(2)}, u32[]{:S(2)}) %collective-permute-start.7) | collective-permute-done | bytes 73760 | tf_op jit(solution)/shard_map/ppermute | solution.py:31
  16.0 0.4 shard_map.71
  16.5 0.6 collective-permute-start.8
  17.2 2.0 %collective-permute-start.6 = (bf16[128,512]{1,0:T(8,128)(2,1)S(1)}, bf16[128,512]{1,0:T(8,128)(2,1)S(1)}, u32[]{:S(2)}, u32[]{:S(2)}) collective-permute-start(bf16[128,512]{1,0:T(8,128)(2,1)S(1)} %get-tuple-element.46.refs_2_), channel_id=1, source_target_pairs={{0,2},{1,3},{2,0},{3,1},{4,6},{5,7},{6,4},{7,5},{8,10},{9,11},{10,... | collective-permute-start | bytes 393224 | tf_op jit(solution)/shard_map/ppermute | solution.py:31
  19.2 4.6 %collective-permute-done.2.refs_0_.refs_2_ = bf16[128,1408]{1,0:T(8,128)(2,1)S(1)} collective-permute-done((bf16[128,1408]{1,0:T(8,128)(2,1)S(1)}, bf16[128,1408]{1,0:T(8,128)(2,1)S(1)}, u32[]{:S(2)}, u32[]{:S(2)}) %collective-permute-start.2) | collective-permute-done | bytes 360480 | tf_op jit(solution)/shard_map/ppermute | solution.py:31
  23.8 0.4 shard_map.72
  24.1 2.1 %collective-permute-start.5 = (bf16[128,512]{1,0:T(8,128)(2,1)S(1)}, bf16[128,512]{1,0:T(8,128)(2,1)S(1)}, u32[]{:S(2)}, u32[]{:S(2)}) collective-permute-start(bf16[128,512]{1,0:T(8,128)(2,1)S(1)} %get-tuple-element.30), channel_id=1, source_target_pairs={{0,2},{1,3},{2,0},{3,1},{4,6},{5,7},{6,4},{7,5},{8,10},{9,11},{10,... | collective-permute-start | bytes 393224 | tf_op jit(solution)/shard_map/ppermute | solution.py:31
  26.2 0.2 shard_map.73
  26.5 0.9 %sine_multiply_fusion = (f32[512,128]{1,0:T(8,128)S(1)}, f32[512,128]{1,0:T(8,128)S(1)}) fusion(f32[512,128]{1,0:T(8,128)S(1)} %get-tuple-element.32, f32[128]{0:T(128)S(1)} %get-tuple-element.50, f32[128]{0:T(128)S(1)} %get-tuple-element.51), kind=kLoop, calls=%fused_computation.1 | loop fusion | flops 131072 | bytes 787456 | tf_op jit(solution)/shard_map/mul | solution.py:401
  27.4 1.8 %collective-permute-done.5.refs_2_ = bf16[128,512]{1,0:T(8,128)(2,1)S(1)} collective-permute-done((bf16[128,512]{1,0:T(8,128)(2,1)S(1)}, bf16[128,512]{1,0:T(8,128)(2,1)S(1)}, u32[]{:S(2)}, u32[]{:S(2)}) %collective-permute-start.5) | collective-permute-done | bytes 131104 | tf_op jit(solution)/shard_map/ppermute | solution.py:31
  29.4 0.5 shard_map.77.refs_0_
  29.9 1.1 %collective-permute-done.9.refs_1_ = bf16[256,512]{1,0:T(8,128)(2,1)S(1)} collective-permute-done((bf16[256,512]{1,0:T(8,128)(2,1)S(1)}, bf16[256,512]{1,0:T(8,128)(2,1)S(1)}, u32[]{:S(2)}, u32[]{:S(2)}) %collective-permute-start.9) | collective-permute-done | bytes 262176 | tf_op jit(solution)/shard_map/ppermute | solution.py:31
  31.0 2.2 %shard_map.75.refs_1_.refs_0_ = bf16[512,512]{1,0:T(8,128)(2,1)S(1)} custom-call(bf16[256,512]{1,0:T(8,128)(2,1)S(1)} %shard_map.74.refs_0_, bf16[256,512]{1,0:T(8,128)(2,1)S(1)} %collective-permute-done.9.refs_1_, bf16[512,256]{1,0:T(8,128)(2,1)S(1)} %get-tuple-element.33.refs_2_, s32[4,128]{1,0:T(4,128)S(1)} %get-tuple-element.34.refs_3_, ...), custom_call_target="tpu_custom_call" | custom-call | flops 770000000 | tf_op jit(solution)/shard_map/pallas_call | solution.py:46
  33.2 0.6 shard_map.78
  33.8 2.2 %collective-permute-start.11 = (bf16[336,256]{1,0:T(8,128)(2,1)S(1)}, bf16[336,256]{1,0:T(8,128)(2,1)S(1)}, u32[]{:S(2)}, u32[]{:S(2)}) collective-permute-start(bf16[336,256]{1,0:T(8,128)(2,1)S(1)} %get-tuple-element.36), channel_id=1, source_target_pairs={{0,8},{4,12},{8,0},{12,4},{16,24},{20,28},{24,16},{28,20},{1,9},{5... | collective-permute-start | bytes 516104 | tf_op jit(solution)/shard_map/ppermute | solution.py:31
  36.0 1.5 %collective-permute-start.13 = (bf16[336,256]{1,0:T(8,128)(2,1)S(1)}, bf16[336,256]{1,0:T(8,128)(2,1)S(1)}, u32[]{:S(2)}, u32[]{:S(2)}) collective-permute-start(bf16[336,256]{1,0:T(8,128)(2,1)S(1)} %get-tuple-element.40), channel_id=1, source_target_pairs={{0,4},{4,0},{8,12},{12,8},{16,20},{20,16},{24,28},{28,24},{1,5},{5... | collective-permute-start | bytes 516104 | tf_op jit(solution)/shard_map/ppermute | solution.py:31
  37.5 0.6 shard_map.83
  38.1 2.0 %collective-permute-start.16 = (bf16[336,256]{1,0:T(8,128)(2,1)S(1)}, bf16[336,256]{1,0:T(8,128)(2,1)S(1)}, u32[]{:S(2)}, u32[]{:S(2)}) collective-permute-start(bf16[336,256]{1,0:T(8,128)(2,1)S(1)} %get-tuple-element.43), channel_id=1, source_target_pairs={{0,4},{4,0},{8,12},{12,8},{16,20},{20,16},{24,28},{28,24},{1,5},{5... | collective-permute-start | bytes 516104 | tf_op jit(solution)/shard_map/ppermute | solution.py:31
  40.1 1.1 %collective-permute-done.11.refs_2_ = bf16[336,256]{1,0:T(8,128)(2,1)S(1)} collective-permute-done((bf16[336,256]{1,0:T(8,128)(2,1)S(1)}, bf16[336,256]{1,0:T(8,128)(2,1)S(1)}, u32[]{:S(2)}, u32[]{:S(2)}) %collective-permute-start.11) | collective-permute-done | bytes 172064 | tf_op jit(solution)/shard_map/ppermute | solution.py:31
  41.1 2.1 %collective-permute-start.17 = (bf16[336,256]{1,0:T(8,128)(2,1)S(1)}, bf16[336,256]{1,0:T(8,128)(2,1)S(1)}, u32[]{:S(2)}, u32[]{:S(2)}) collective-permute-start(bf16[336,256]{1,0:T(8,128)(2,1)S(1)} %get-tuple-element.44), channel_id=1, source_target_pairs={{0,8},{4,12},{8,0},{12,4},{16,24},{20,28},{24,16},{28,20},{1,9},{5... | collective-permute-start | bytes 516104 | tf_op jit(solution)/shard_map/ppermute | solution.py:31
  43.2 3.7 %collective-permute-done.13.refs_1_ = bf16[336,256]{1,0:T(8,128)(2,1)S(1)} collective-permute-done((bf16[336,256]{1,0:T(8,128)(2,1)S(1)}, bf16[336,256]{1,0:T(8,128)(2,1)S(1)}, u32[]{:S(2)}, u32[]{:S(2)}) %collective-permute-start.13) | collective-permute-done | bytes 172064 | tf_op jit(solution)/shard_map/ppermute | solution.py:31
  46.9 1.0 %collective-permute-start.18 = (bf16[336,256]{1,0:T(8,128)(2,1)S(1)}, bf16[336,256]{1,0:T(8,128)(2,1)S(1)}, u32[]{:S(2)}, u32[]{:S(2)}) collective-permute-start(bf16[336,256]{1,0:T(8,128)(2,1)S(1)} %get-tuple-element.45), channel_id=1, source_target_pairs={{0,12},{4,8},{8,4},{12,0},{16,28},{20,24},{24,20},{28,16},{1,13},{... | collective-permute-start | bytes 516104 | tf_op jit(solution)/shard_map/ppermute | solution.py:31
  48.0 2.7 %collective-permute-start.15 = (bf16[336,256]{1,0:T(8,128)(2,1)S(1)}, bf16[336,256]{1,0:T(8,128)(2,1)S(1)}, u32[]{:S(2)}, u32[]{:S(2)}) collective-permute-start(bf16[336,256]{1,0:T(8,128)(2,1)S(1)} %shard_map.80.refs_0_), channel_id=1, source_target_pairs={{0,16},{4,20},{8,24},{12,28},{16,0},{20,4},{24,8},{28,12},{1,17},{... | collective-permute-start | bytes 516104 | tf_op jit(solution)/shard_map/ppermute | solution.py:31
  50.7 1.5 %shard_map.76.refs_1_ = bf16[2688,512]{1,0:T(8,128)(2,1)S(1)} custom-call(bf16[1344,512]{1,0:T(8,128)(2,1)} %refs_0_.3, bf16[1344,512]{1,0:T(8,128)(2,1)S(1)} %collective-permute-done.10.refs_1_, bf16[128,512]{1,0:T(8,128)(2,1)S(1)} %get-tuple-element.46.refs_2_), custom_call_target="tpu_custom_call" | custom-call | flops 900000000 | tf_op jit(solution)/shard_map/pallas_call | solution.py:46
  52.2 1.9 %shard_map.79 = (bf16[128,2688]{1,0:T(8,128)(2,1)S(1)}, bf16[128,2688]{1,0:T(8,128)(2,1)S(1)}) custom-call(bf16[512,512]{1,0:T(8,128)(2,1)S(1)} %shard_map.75.refs_1_.refs_0_, bf16[2688,512]{1,0:T(8,128)(2,1)S(1)} %shard_map.76.refs_1_, bf16[336,256]{1,0:T(8,128)(2,1)S(1)} %collective-permute-done.11.refs_2_), custom_call_target="tpu_custom_call" | custom-call | flops 900000000 | tf_op jit(solution)/shard_map/pallas_call | solution.py:46
  54.1 1.5 %collective-permute-start.12 = (bf16[128,2688]{1,0:T(8,128)(2,1)S(1)}, bf16[128,2688]{1,0:T(8,128)(2,1)S(1)}, u32[]{:S(2)}, u32[]{:S(2)}) collective-permute-start(bf16[128,2688]{1,0:T(8,128)(2,1)S(1)} %get-tuple-element.38.refs_4_), channel_id=1, source_target_pairs={{0,2},{1,3},{2,0},{3,1},{4,6},{5,7},{6,4},{7,5},{8,10},{9,11},{10,... | collective-permute-start | bytes 2064392 | tf_op jit(solution)/shard_map/ppermute | solution.py:31
  55.6 0.9 %collective-permute-done.18.refs_3_ = bf16[336,256]{1,0:T(8,128)(2,1)S(1)} collective-permute-done((bf16[336,256]{1,0:T(8,128)(2,1)S(1)}, bf16[336,256]{1,0:T(8,128)(2,1)S(1)}, u32[]{:S(2)}, u32[]{:S(2)}) %collective-permute-start.18) | collective-permute-done | bytes 172064 | tf_op jit(solution)/shard_map/ppermute | solution.py:31
  56.6 0.9 %collective-permute-start.19 = (bf16[336,256]{1,0:T(8,128)(2,1)S(1)}, bf16[336,256]{1,0:T(8,128)(2,1)S(1)}, u32[]{:S(2)}, u32[]{:S(2)}) collective-permute-start(bf16[336,256]{1,0:T(8,128)(2,1)S(1)} %shard_map.84.refs_0_), channel_id=1, source_target_pairs={{0,16},{4,20},{8,24},{12,28},{16,0},{20,4},{24,8},{28,12},{1,17},{... | collective-permute-start | bytes 516104 | tf_op jit(solution)/shard_map/ppermute | solution.py:31
  57.5 5.6 %collective-permute-start.25 = (bf16[336,256]{1,0:T(8,128)(2,1)S(1)}, bf16[336,256]{1,0:T(8,128)(2,1)S(1)}, u32[]{:S(2)}, u32[]{:S(2)}) collective-permute-start(bf16[336,256]{1,0:T(8,128)(2,1)S(1)} %shard_map.81.refs_2_.refs_0_), channel_id=1, source_target_pairs={{0,12},{4,8},{8,4},{12,0},{16,28},{20,24},{24,20},{28,16},{1,13},{... | collective-permute-start | bytes 516104 | tf_op jit(solution)/shard_map/ppermute | solution.py:31
  63.2 0.6 collective-permute-start.23
  63.8 2.6 %collective-permute-done.19.refs_1_ = bf16[336,256]{1,0:T(8,128)(2,1)S(1)} collective-permute-done((bf16[336,256]{1,0:T(8,128)(2,1)S(1)}, bf16[336,256]{1,0:T(8,128)(2,1)S(1)}, u32[]{:S(2)}, u32[]{:S(2)}) %collective-permute-start.19) | collective-permute-done | bytes 172064 | tf_op jit(solution)/shard_map/ppermute | solution.py:31
  66.4 1.7 %collective-permute-done.12.refs_1_.refs_2_ = bf16[128,2688]{1,0:T(8,128)(2,1)S(1)} collective-permute-done((bf16[128,2688]{1,0:T(8,128)(2,1)S(1)}, bf16[128,2688]{1,0:T(8,128)(2,1)S(1)}, u32[]{:S(2)}, u32[]{:S(2)}) %collective-permute-start.12) | collective-permute-done | bytes 688160 | tf_op jit(solution)/shard_map/ppermute | solution.py:31
  68.1 1.6 %collective-permute-start.22 = (bf16[336,256]{1,0:T(8,128)(2,1)S(1)}, bf16[336,256]{1,0:T(8,128)(2,1)S(1)}, u32[]{:S(2)}, u32[]{:S(2)}) collective-permute-start(bf16[336,256]{1,0:T(8,128)(2,1)S(1)} %shard_map.85.refs_0_), channel_id=1, source_target_pairs={{0,12},{4,8},{8,4},{12,0},{16,28},{20,24},{24,20},{28,16},{1,13},{... | collective-permute-start | bytes 516104 | tf_op jit(solution)/shard_map/ppermute | solution.py:31
  69.7 0.8 %collective-permute-start.21 = (bf16[336,256]{1,0:T(8,128)(2,1)S(1)}, bf16[336,256]{1,0:T(8,128)(2,1)S(1)}, u32[]{:S(2)}, u32[]{:S(2)}) collective-permute-start(bf16[336,256]{1,0:T(8,128)(2,1)S(1)} %shard_map.85.refs_0_), channel_id=1, source_target_pairs={{0,8},{4,12},{8,0},{12,4},{16,24},{20,28},{24,16},{28,20},{1,9},{5... | collective-permute-start | bytes 516104 | tf_op jit(solution)/shard_map/ppermute | solution.py:31
  70.5 1.2 %shard_map.82.refs_4_ = bf16[128,5376]{1,0:T(8,128)(2,1)} custom-call(bf16[128,2688]{1,0:T(8,128)(2,1)S(1)} %get-tuple-element.37.refs_0_, bf16[128,2688]{1,0:T(8,128)(2,1)S(1)} %collective-permute-done.12.refs_1_.refs_2_, bf16[336,256]{1,0:T(8,128)(2,1)S(1)} %shard_map.81.refs_2_.refs_0_), custom_call_target="tpu_custom_call" | custom-call | flops 8000000000 | tf_op jit(solution)/shard_map/pallas_call | solution.py:46
  71.7 1.2 %collective-permute-start.20 = (bf16[336,256]{1,0:T(8,128)(2,1)S(1)}, bf16[336,256]{1,0:T(8,128)(2,1)S(1)}, u32[]{:S(2)}, u32[]{:S(2)}) collective-permute-start(bf16[336,256]{1,0:T(8,128)(2,1)S(1)} %shard_map.85.refs_0_), channel_id=1, source_target_pairs={{0,4},{4,0},{8,12},{12,8},{16,20},{20,16},{24,28},{28,24},{1,5},{5... | collective-permute-start | bytes 516104 | tf_op jit(solution)/shard_map/ppermute | solution.py:31
  72.9 1.3 %copy-done.2 = bf16[128,5376]{1,0:T(8,128)(2,1)S(1)} copy-done((bf16[128,5376]{1,0:T(8,128)(2,1)S(1)}, bf16[128,5376]{1,0:T(8,128)(2,1)}, u32[]{:S(2)}) %copy-start.2) | copy-done | bytes 1376280
  74.3 1.1 %shard_map.86.refs_4_ = f32[1344,512]{1,0:T(8,128)} custom-call(bf16[336,256]{1,0:T(8,128)(2,1)S(1)} %shard_map.81.refs_2_.refs_0_, bf16[336,256]{1,0:T(8,128)(2,1)S(1)} %collective-permute-done.23.refs_1_, bf16[336,256]{1,0:T(8,128)(2,1)S(1)} %collective-permute-done.24.refs_2_, bf16[336,256]{1,0:T(8,128)(2,1)S(1)} %collective-permute-done.25.refs_3_, ...), custom_call_target="tpu_custom_call" | custom-call | flops 8000000000 | tf_op jit(solution)/shard_map/pallas_call | solution.py:46
  75.4 0.6 collective-permute-done.22.refs_3_
  76.0 1.8 %collective-permute-done.21.refs_2_ = bf16[336,256]{1,0:T(8,128)(2,1)S(1)} collective-permute-done((bf16[336,256]{1,0:T(8,128)(2,1)S(1)}, bf16[336,256]{1,0:T(8,128)(2,1)S(1)}, u32[]{:S(2)}, u32[]{:S(2)}) %collective-permute-start.21) | collective-permute-done | bytes 172064 | tf_op jit(solution)/shard_map/ppermute | solution.py:31
  77.8 1.1 %shard_map.87 = f32[1344,512]{1,0:T(8,128)} custom-call(bf16[336,256]{1,0:T(8,128)(2,1)S(1)} %shard_map.85.refs_0_, bf16[336,256]{1,0:T(8,128)(2,1)S(1)} %collective-permute-done.20.refs_1_, bf16[336,256]{1,0:T(8,128)(2,1)S(1)} %collective-permute-done.21.refs_2_, ...), custom_call_target="tpu_custom_call", output_to_operand_aliasing={{}: (4, {})} | custom-call | tf_op jit(solution)/shard_map/pallas_call | solution.py:46
  (43 shorter events, 1.1 us)
Async XLA Ops:
  0.6 1.3 %copy-start = (bf16[1,128,5376]{2,1,0:T(8,128)(2,1)S(1)}, bf16[1,128,5376]{2,1,0:T(8,128)(2,1)}, u32[]{:S(2)}) copy-start(bf16[1,128,5376]{2,1,0:T(8,128)(2,1)} %param.5) | copy-start | bytes 4128772
  2.1 4.7 %collective-permute-start = (bf16[128,1408]{1,0:T(8,128)(2,1)S(1)}, bf16[128,1408]{1,0:T(8,128)(2,1)S(1)}, u32[]{:S(2)}, u32[]{:S(2)}) collective-permute-start(bf16[128,1408]{1,0:T(8,128)(2,1)S(1)} %get-tuple-element.24), channel_id=1, source_target_pairs={{0,1},{1,0},{2,3},{3,2},{4,5},{5,4},{6,7},{7,6},{8,9},{9,8},{10,11... | collective-permute-start | bytes 1081352 | tf_op jit(solution)/shard_map/ppermute | solution.py:31
  2.6 4.2 %copy-start.1 = (bf16[1,128,5376]{2,1,0:T(8,128)(2,1)S(1)}, bf16[1,128,5376]{2,1,0:T(8,128)(2,1)}, u32[]{:S(2)}) copy-start(bf16[1,128,5376]{2,1,0:T(8,128)(2,1)} %param.5) | copy-start | bytes 4128772
  2.6 13.4 %collective-permute-start.3 = (bf16[128,1408]{1,0:T(8,128)(2,1)S(1)}, bf16[128,1408]{1,0:T(8,128)(2,1)S(1)}, u32[]{:S(2)}, u32[]{:S(2)}) collective-permute-start(bf16[128,1408]{1,0:T(8,128)(2,1)S(1)} %get-tuple-element.28), channel_id=1, source_target_pairs={{0,3},{1,2},{2,1},{3,0},{4,7},{5,6},{6,5},{7,4},{8,11},{9,10},{10,... | collective-permute-start | bytes 1081352 | tf_op jit(solution)/shard_map/ppermute | solution.py:31
  6.8 0.8 copy-start.4
  6.8 1.4 %copy-start.3 = (bf16[1,128,256]{2,1,0:T(8,128)(2,1)S(1)}, bf16[1,128,256]{2,1,0:T(8,128)(2,1)}, u32[]{:S(2)}) copy-start(bf16[1,128,256]{2,1,0:T(8,128)(2,1)} %param.7) | copy-start | bytes 196612
  7.4 2.9 %collective-permute-start.1 = (bf16[128,512]{1,0:T(8,128)(2,1)S(1)}, bf16[128,512]{1,0:T(8,128)(2,1)S(1)}, u32[]{:S(2)}, u32[]{:S(2)}) collective-permute-start(bf16[128,512]{1,0:T(8,128)(2,1)S(1)} %get-tuple-element.26), channel_id=1, source_target_pairs={{0,1},{1,0},{2,3},{3,2},{4,5},{5,4},{6,7},{7,6},{8,9},{9,8},{10,11... | collective-permute-start | bytes 393224 | tf_op jit(solution)/shard_map/ppermute | solution.py:31
  8.3 7.8 %collective-permute-start.7 = (bf16[144,256]{1,0:T(8,128)(2,1)S(1)}, bf16[144,256]{1,0:T(8,128)(2,1)S(1)}, u32[]{:S(2)}, u32[]{:S(2)}) collective-permute-start(bf16[144,256]{1,0:T(8,128)(2,1)S(1)} %pad_maximum_fusion.2), channel_id=1, source_target_pairs={{0,2},{1,3},{2,0},{3,1},{4,6},{5,7},{6,4},{7,5},{8,10},{9,11},{10,... | collective-permute-start | bytes 221192 | tf_op jit(solution)/shard_map/ppermute | solution.py:31
  8.8 15.0 %collective-permute-start.2 = (bf16[128,1408]{1,0:T(8,128)(2,1)S(1)}, bf16[128,1408]{1,0:T(8,128)(2,1)S(1)}, u32[]{:S(2)}, u32[]{:S(2)}) collective-permute-start(bf16[128,1408]{1,0:T(8,128)(2,1)S(1)} %get-tuple-element.27), channel_id=1, source_target_pairs={{0,2},{1,3},{2,0},{3,1},{4,6},{5,7},{6,4},{7,5},{8,10},{9,11},{10,... | collective-permute-start | bytes 1081352 | tf_op jit(solution)/shard_map/ppermute | solution.py:31
  16.4 7.3 %collective-permute-start.4 = (bf16[128,512]{1,0:T(8,128)(2,1)S(1)}, bf16[128,512]{1,0:T(8,128)(2,1)S(1)}, u32[]{:S(2)}, u32[]{:S(2)}) collective-permute-start(bf16[128,512]{1,0:T(8,128)(2,1)S(1)} %shard_map.71), channel_id=1, source_target_pairs={{0,1},{1,0},{2,3},{3,2},{4,5},{5,4},{6,7},{7,6},{8,9},{9,8},{10,11... | collective-permute-start | bytes 393224 | tf_op jit(solution)/shard_map/ppermute | solution.py:31
  16.5 9.7 %collective-permute-start.8 = (bf16[288,256]{1,0:T(8,128)(2,1)S(1)}, bf16[288,256]{1,0:T(8,128)(2,1)S(1)}, u32[]{:S(2)}, u32[]{:S(2)}) collective-permute-start(bf16[288,256]{1,0:T(8,128)(2,1)S(1)} %pad_maximum_fusion.1), channel_id=1, source_target_pairs={{0,1},{1,0},{2,3},{3,2},{4,5},{5,4},{6,7},{7,6},{8,9},{9,8},{10,11... | collective-permute-start | bytes 442376 | tf_op jit(solution)/shard_map/ppermute | solution.py:31
  17.1 33.6 %collective-permute-start.10 = (bf16[1344,512]{1,0:T(8,128)(2,1)}, bf16[1344,512]{1,0:T(8,128)(2,1)S(1)}, u32[]{:S(2)}, u32[]{:S(2)}) collective-permute-start(bf16[1344,512]{1,0:T(8,128)(2,1)} %refs_0_.3), channel_id=1, source_target_pairs={{0,1},{1,0},{2,3},{3,2},{4,5},{5,4},{6,7},{7,6},{8,9},{9,8},{10,11... | collective-permute-start | bytes 4128776 | tf_op jit(solution)/shard_map/ppermute | solution.py:31
  17.2 10.2 %collective-permute-start.6 = (bf16[128,512]{1,0:T(8,128)(2,1)S(1)}, bf16[128,512]{1,0:T(8,128)(2,1)S(1)}, u32[]{:S(2)}, u32[]{:S(2)}) collective-permute-start(bf16[128,512]{1,0:T(8,128)(2,1)S(1)} %get-tuple-element.46.refs_2_), channel_id=1, source_target_pairs={{0,2},{1,3},{2,0},{3,1},{4,6},{5,7},{6,4},{7,5},{8,10},{9,11},{10,... | collective-permute-start | bytes 393224 | tf_op jit(solution)/shard_map/ppermute | solution.py:31
  24.1 5.0 %collective-permute-start.5 = (bf16[128,512]{1,0:T(8,128)(2,1)S(1)}, bf16[128,512]{1,0:T(8,128)(2,1)S(1)}, u32[]{:S(2)}, u32[]{:S(2)}) collective-permute-start(bf16[128,512]{1,0:T(8,128)(2,1)S(1)} %get-tuple-element.30), channel_id=1, source_target_pairs={{0,2},{1,3},{2,0},{3,1},{4,6},{5,7},{6,4},{7,5},{8,10},{9,11},{10,... | collective-permute-start | bytes 393224 | tf_op jit(solution)/shard_map/ppermute | solution.py:31
  29.4 1.6 %collective-permute-start.9 = (bf16[256,512]{1,0:T(8,128)(2,1)S(1)}, bf16[256,512]{1,0:T(8,128)(2,1)S(1)}, u32[]{:S(2)}, u32[]{:S(2)}) collective-permute-start(bf16[256,512]{1,0:T(8,128)(2,1)S(1)} %shard_map.74.refs_0_), channel_id=1, source_target_pairs={{0,1},{1,0},{2,3},{3,2},{4,5},{5,4},{6,7},{7,6},{8,9},{9,8},{10,11... | collective-permute-start | bytes 786440 | tf_op jit(solution)/shard_map/ppermute | solution.py:31
  33.8 7.3 %collective-permute-start.11 = (bf16[336,256]{1,0:T(8,128)(2,1)S(1)}, bf16[336,256]{1,0:T(8,128)(2,1)S(1)}, u32[]{:S(2)}, u32[]{:S(2)}) collective-permute-start(bf16[336,256]{1,0:T(8,128)(2,1)S(1)} %get-tuple-element.36), channel_id=1, source_target_pairs={{0,8},{4,12},{8,0},{12,4},{16,24},{20,28},{24,16},{28,20},{1,9},{5... | collective-permute-start | bytes 516104 | tf_op jit(solution)/shard_map/ppermute | solution.py:31
  36.0 10.9 %collective-permute-start.13 = (bf16[336,256]{1,0:T(8,128)(2,1)S(1)}, bf16[336,256]{1,0:T(8,128)(2,1)S(1)}, u32[]{:S(2)}, u32[]{:S(2)}) collective-permute-start(bf16[336,256]{1,0:T(8,128)(2,1)S(1)} %get-tuple-element.40), channel_id=1, source_target_pairs={{0,4},{4,0},{8,12},{12,8},{16,20},{20,16},{24,28},{28,24},{1,5},{5... | collective-permute-start | bytes 516104 | tf_op jit(solution)/shard_map/ppermute | solution.py:31
  37.5 10.4 %collective-permute-start.14 = (bf16[336,256]{1,0:T(8,128)(2,1)S(1)}, bf16[336,256]{1,0:T(8,128)(2,1)S(1)}, u32[]{:S(2)}, u32[]{:S(2)}) collective-permute-start(bf16[336,256]{1,0:T(8,128)(2,1)S(1)} %get-tuple-element.41), channel_id=1, source_target_pairs={{0,12},{4,8},{8,4},{12,0},{16,28},{20,24},{24,20},{28,16},{1,13},{... | collective-permute-start | bytes 516104 | tf_op jit(solution)/shard_map/ppermute | solution.py:31
  38.1 17.5 %collective-permute-start.16 = (bf16[336,256]{1,0:T(8,128)(2,1)S(1)}, bf16[336,256]{1,0:T(8,128)(2,1)S(1)}, u32[]{:S(2)}, u32[]{:S(2)}) collective-permute-start(bf16[336,256]{1,0:T(8,128)(2,1)S(1)} %get-tuple-element.43), channel_id=1, source_target_pairs={{0,4},{4,0},{8,12},{12,8},{16,20},{20,16},{24,28},{28,24},{1,5},{5... | collective-permute-start | bytes 516104 | tf_op jit(solution)/shard_map/ppermute | solution.py:31
  41.1 14.5 %collective-permute-start.17 = (bf16[336,256]{1,0:T(8,128)(2,1)S(1)}, bf16[336,256]{1,0:T(8,128)(2,1)S(1)}, u32[]{:S(2)}, u32[]{:S(2)}) collective-permute-start(bf16[336,256]{1,0:T(8,128)(2,1)S(1)} %get-tuple-element.44), channel_id=1, source_target_pairs={{0,8},{4,12},{8,0},{12,4},{16,24},{20,28},{24,16},{28,20},{1,9},{5... | collective-permute-start | bytes 516104 | tf_op jit(solution)/shard_map/ppermute | solution.py:31
  46.9 9.6 %collective-permute-start.18 = (bf16[336,256]{1,0:T(8,128)(2,1)S(1)}, bf16[336,256]{1,0:T(8,128)(2,1)S(1)}, u32[]{:S(2)}, u32[]{:S(2)}) collective-permute-start(bf16[336,256]{1,0:T(8,128)(2,1)S(1)} %get-tuple-element.45), channel_id=1, source_target_pairs={{0,12},{4,8},{8,4},{12,0},{16,28},{20,24},{24,20},{28,16},{1,13},{... | collective-permute-start | bytes 516104 | tf_op jit(solution)/shard_map/ppermute | solution.py:31
  48.0 9.5 %collective-permute-start.15 = (bf16[336,256]{1,0:T(8,128)(2,1)S(1)}, bf16[336,256]{1,0:T(8,128)(2,1)S(1)}, u32[]{:S(2)}, u32[]{:S(2)}) collective-permute-start(bf16[336,256]{1,0:T(8,128)(2,1)S(1)} %shard_map.80.refs_0_), channel_id=1, source_target_pairs={{0,16},{4,20},{8,24},{12,28},{16,0},{20,4},{24,8},{28,12},{1,17},{... | collective-permute-start | bytes 516104 | tf_op jit(solution)/shard_map/ppermute | solution.py:31
  54.1 14.0 %collective-permute-start.12 = (bf16[128,2688]{1,0:T(8,128)(2,1)S(1)}, bf16[128,2688]{1,0:T(8,128)(2,1)S(1)}, u32[]{:S(2)}, u32[]{:S(2)}) collective-permute-start(bf16[128,2688]{1,0:T(8,128)(2,1)S(1)} %get-tuple-element.38.refs_4_), channel_id=1, source_target_pairs={{0,2},{1,3},{2,0},{3,1},{4,6},{5,7},{6,4},{7,5},{8,10},{9,11},{10,... | collective-permute-start | bytes 2064392 | tf_op jit(solution)/shard_map/ppermute | solution.py:31
  56.6 9.7 %collective-permute-start.19 = (bf16[336,256]{1,0:T(8,128)(2,1)S(1)}, bf16[336,256]{1,0:T(8,128)(2,1)S(1)}, u32[]{:S(2)}, u32[]{:S(2)}) collective-permute-start(bf16[336,256]{1,0:T(8,128)(2,1)S(1)} %shard_map.84.refs_0_), channel_id=1, source_target_pairs={{0,16},{4,20},{8,24},{12,28},{16,0},{20,4},{24,8},{28,12},{1,17},{... | collective-permute-start | bytes 516104 | tf_op jit(solution)/shard_map/ppermute | solution.py:31
  57.5 14.2 %collective-permute-start.25 = (bf16[336,256]{1,0:T(8,128)(2,1)S(1)}, bf16[336,256]{1,0:T(8,128)(2,1)S(1)}, u32[]{:S(2)}, u32[]{:S(2)}) collective-permute-start(bf16[336,256]{1,0:T(8,128)(2,1)S(1)} %shard_map.81.refs_2_.refs_0_), channel_id=1, source_target_pairs={{0,12},{4,8},{8,4},{12,0},{16,28},{20,24},{24,20},{28,16},{1,13},{... | collective-permute-start | bytes 516104 | tf_op jit(solution)/shard_map/ppermute | solution.py:31
  63.2 9.8 %collective-permute-start.24 = (bf16[336,256]{1,0:T(8,128)(2,1)S(1)}, bf16[336,256]{1,0:T(8,128)(2,1)S(1)}, u32[]{:S(2)}, u32[]{:S(2)}) collective-permute-start(bf16[336,256]{1,0:T(8,128)(2,1)S(1)} %shard_map.81.refs_2_.refs_0_), channel_id=1, source_target_pairs={{0,8},{4,12},{8,0},{12,4},{16,24},{20,28},{24,16},{28,20},{1,9},{5... | collective-permute-start | bytes 516104 | tf_op jit(solution)/shard_map/ppermute | solution.py:31
  63.2 9.8 %collective-permute-start.23 = (bf16[336,256]{1,0:T(8,128)(2,1)S(1)}, bf16[336,256]{1,0:T(8,128)(2,1)S(1)}, u32[]{:S(2)}, u32[]{:S(2)}) collective-permute-start(bf16[336,256]{1,0:T(8,128)(2,1)S(1)} %shard_map.81.refs_2_.refs_0_), channel_id=1, source_target_pairs={{0,4},{4,0},{8,12},{12,8},{16,20},{20,16},{24,28},{28,24},{1,5},{5... | collective-permute-start | bytes 516104 | tf_op jit(solution)/shard_map/ppermute | solution.py:31
  68.1 7.9 %collective-permute-start.22 = (bf16[336,256]{1,0:T(8,128)(2,1)S(1)}, bf16[336,256]{1,0:T(8,128)(2,1)S(1)}, u32[]{:S(2)}, u32[]{:S(2)}) collective-permute-start(bf16[336,256]{1,0:T(8,128)(2,1)S(1)} %shard_map.85.refs_0_), channel_id=1, source_target_pairs={{0,12},{4,8},{8,4},{12,0},{16,28},{20,24},{24,20},{28,16},{1,13},{... | collective-permute-start | bytes 516104 | tf_op jit(solution)/shard_map/ppermute | solution.py:31
  69.7 8.1 %collective-permute-start.21 = (bf16[336,256]{1,0:T(8,128)(2,1)S(1)}, bf16[336,256]{1,0:T(8,128)(2,1)S(1)}, u32[]{:S(2)}, u32[]{:S(2)}) collective-permute-start(bf16[336,256]{1,0:T(8,128)(2,1)S(1)} %shard_map.85.refs_0_), channel_id=1, source_target_pairs={{0,8},{4,12},{8,0},{12,4},{16,24},{20,28},{24,16},{28,20},{1,9},{5... | collective-permute-start | bytes 516104 | tf_op jit(solution)/shard_map/ppermute | solution.py:31
  71.7 6.1 %collective-permute-start.20 = (bf16[336,256]{1,0:T(8,128)(2,1)S(1)}, bf16[336,256]{1,0:T(8,128)(2,1)S(1)}, u32[]{:S(2)}, u32[]{:S(2)}) collective-permute-start(bf16[336,256]{1,0:T(8,128)(2,1)S(1)} %shard_map.85.refs_0_), channel_id=1, source_target_pairs={{0,4},{4,0},{8,12},{12,8},{16,20},{20,16},{24,28},{28,24},{1,5},{5... | collective-permute-start | bytes 516104 | tf_op jit(solution)/shard_map/ppermute | solution.py:31
  72.9 1.3 %copy-start.2 = (bf16[128,5376]{1,0:T(8,128)(2,1)S(1)}, bf16[128,5376]{1,0:T(8,128)(2,1)}, u32[]{:S(2)}) copy-start(bf16[128,5376]{1,0:T(8,128)(2,1)} %shard_map.82.refs_4_) | copy-start | bytes 4128772
